TPU v7x, 128 devices: a whole 4x4x4 slice. The times are simulated.
128 devices in a mesh: inl: 8 (over x_hi, z), xl: 16 (over x_lo, y, core).
Axes of the slice: x: 4 (x_hi: 2, x_lo: 2; x = x_hi * 2 + x_lo), y: 4, z: 4, core: 2. Of those that a mesh axis runs over, the one named last changes fastest.
Arguments:
- receiver: bfloat16 [2, 2, 4096, 4096], P(None, None, 'inl', 'xl'), may hold values from -6 to 6
- source: bfloat16 [2, 2, 4096, 4096], P(None, None, 'inl', 'xl'), may hold values from -6 to 6
- weight: int32 [4096, 4096], P('inl', 'xl'), may hold values from 0 to 4096
- omega: float32 [2], replicated, may hold values from 0.6 to 1.4
- slowness: float32 [2], replicated, may hold values from 1 to 2
- wedge_map: int32 [128, 128], replicated, may hold values from 0 to 7
Outputs:
- next_field: bfloat16 [2, 2, 4096, 4096], P(None, None, 'inl', 'xl')
- angle_gather: float32 [8, 4096], replicated
Inputs may be any that keep to these rules, and one draw needn't show every extreme that they name: The weight of the first reference velocity is this value divided by 4096. `wedge_map`: tile rows follow the inline wavenumber index, tile columns the crossline one, in unshifted order.
All inputs are finite; a program needn't handle non-finite values.
Results may differ from a plain program's by a relative error of at most 0.0056.
Values may be sent and summed in bfloat16 or wider, within the bound.
No kernel may reach another device: no remote copies, remote signals or barrier semaphores. Data moves between devices by JAX's collectives and lax.ppermute only.
A program may use at most 128 MiB of HBM per device.

v0:
```python
import math

import jax
import jax.numpy as jnp
from jax import lax
from jax.sharding import PartitionSpec as P

WEDGES = 8
TILE = 32


def factor_pair(length):
    first = 1
    trial = 1
    while trial * trial <= length:
        if length % trial == 0:
            first = trial
        trial = trial + 1
    return (first, length // first)


def table(count, length, inverse):
    sign = 1.0 if inverse else -1.0
    rows = jnp.arange(count[0], dtype=jnp.int32)
    cols = jnp.arange(count[1], dtype=jnp.int32)
    angle = 2.0 * math.pi / length * (rows[:, None] * cols[None, :] % length).astype(jnp.float32)
    return (jnp.cos(angle), sign * jnp.sin(angle))


def contract(form, values, matrix):
    return jnp.einsum(form, values, matrix, precision=lax.Precision.HIGHEST)


def dft_lines(real_in, imag_in, last, inverse):
    length = real_in.shape[-1] if last else real_in.shape[-2]
    first, second = factor_pair(length)
    cos_one, sin_one = table((first, first), first, inverse)
    cos_two, sin_two = table((second, second), second, inverse)
    cos_tw, sin_tw = table((first, second), length, inverse)
    if last:
        shape = real_in.shape[:-1] + (first, second)
        form_one, form_two = ("...an,ak->...kn", "...kn,nl->...lk")
        twist = (first, second)
    else:
        shape = real_in.shape[:-2] + (first, second, real_in.shape[-1])
        form_one, form_two = ("...anm,ak->...knm", "...knm,nl->...lkm")
        twist = (first, second, 1)
    xr = real_in.reshape(shape)
    xi = imag_in.reshape(shape)
    yr = contract(form_one, xr, cos_one) - contract(form_one, xi, sin_one)
    yi = contract(form_one, xr, sin_one) + contract(form_one, xi, cos_one)
    tr = cos_tw.reshape(twist)
    ti = sin_tw.reshape(twist)
    zr = yr * tr - yi * ti
    zi = yr * ti + yi * tr
    out_r = contract(form_two, zr, cos_two) - contract(form_two, zi, sin_two)
    out_i = contract(form_two, zr, sin_two) + contract(form_two, zi, cos_two)
    out_r = out_r.reshape(real_in.shape)
    out_i = out_i.reshape(real_in.shape)
    if inverse:
        out_r = out_r * (1.0 / length)
        out_i = out_i * (1.0 / length)
    return (out_r, out_i)


def to_spectrum(packed):
    return lax.all_to_all(packed, ("inl", "xl"), split_axis=4, concat_axis=3, tiled=True)


def to_lines(packed):
    return lax.all_to_all(packed, ("inl", "xl"), split_axis=3, concat_axis=4, tiled=True)


def signed_numbers(start, count, length):
    index = start + jnp.arange(count, dtype=jnp.int32)
    index = jnp.where(index >= length // 2, index - length, index)
    return 2.0 * math.pi / length * index.astype(jnp.float32)


def one_step(block, omega_part, slowness, wedge_map, weight):
    wide = lax.all_to_all(block, "xl", split_axis=3, concat_axis=4, tiled=True)
    yr, yi = dft_lines(wide[:, 0].astype(jnp.float32), wide[:, 1].astype(jnp.float32), True, False)
    spec = to_spectrum(jnp.stack([yr, yi], axis=1).astype(jnp.bfloat16))
    sr, si = dft_lines(spec[:, 0].astype(jnp.float32), spec[:, 1].astype(jnp.float32), False, False)
    rows = spec.shape[3]
    cols = spec.shape[4]
    width = cols * lax.axis_size("inl") * lax.axis_size("xl")
    start = (lax.axis_index("inl") * lax.axis_size("xl") + lax.axis_index("xl")) * cols
    kx = signed_numbers(0, rows, rows)
    ky = signed_numbers(start, cols, width)
    number = omega_part[:, None] * slowness[None, :]
    quad = (number * number)[:, :, None, None] - (kx * kx)[:, None] - (ky * ky)[None, :]
    root = jnp.sqrt(jnp.abs(quad))
    real_phase = jnp.where(quad >= 0, jnp.cos(root), jnp.exp(-root))
    imag_phase = jnp.where(quad >= 0, jnp.sin(root), 0.0)
    term = jnp.sum(sr[1] * sr[0] + si[1] * si[0], axis=0)
    rec_r = sr[0][:, None]
    rec_i = si[0][:, None]
    tiles = cols // TILE
    tile_sums = term.reshape(rows, tiles, TILE).sum(axis=-1)
    wedge_cols = lax.dynamic_slice_in_dim(wedge_map, start // TILE, tiles, 1)
    tile_rows = jnp.repeat(wedge_cols, TILE, axis=0, total_repeat_length=rows)
    hits = tile_rows[None] == jnp.arange(WEDGES, dtype=jnp.int32)[:, None, None]
    contrib = jnp.sum(jnp.where(hits, tile_sums[None], 0.0), axis=2)
    shifted_r = rec_r * real_phase - rec_i * imag_phase
    shifted_i = rec_r * imag_phase + rec_i * real_phase
    ur, ui = dft_lines(shifted_r, shifted_i, False, True)
    lines = to_lines(jnp.stack([ur, ui], axis=0).astype(jnp.bfloat16))
    vr, vi = dft_lines(lines[0].astype(jnp.float32), lines[1].astype(jnp.float32), True, True)
    home = lax.all_to_all(
        jnp.stack([vr, vi], axis=0).astype(jnp.bfloat16),
        "xl",
        split_axis=4,
        concat_axis=3,
        tiled=True,
    )
    share = weight.astype(jnp.float32) / 4096.0
    mixed = home[:, :, 0].astype(jnp.float32) * share + home[:, :, 1].astype(jnp.float32) * (
        1.0 - share
    )
    return (mixed.astype(jnp.bfloat16), contrib)


def per_device(receiver, source, weight, omega, slowness, wedge_map):
    fields = jnp.stack([receiver, source])
    mixed, contrib = one_step(fields, omega, slowness, wedge_map, weight)
    summed = lax.psum(contrib, ("inl", "xl"))
    rows = receiver.shape[2] * lax.axis_size("inl")
    width = receiver.shape[3] * lax.axis_size("xl")
    angle_gather = summed * (1.0 / (rows * width * math.sqrt(width)))
    return (mixed, angle_gather)


def solution(mesh):
    return jax.shard_map(
        per_device,
        mesh=mesh,
        in_specs=(
            P(None, None, "inl", "xl"),
            P(None, None, "inl", "xl"),
            P("inl", "xl"),
            P(),
            P(),
            P(),
        ),
        out_specs=(P(None, None, "inl", "xl"), P()),
        check_vma=False,
    )
```

profile of v0, /device:TPU:1, one launch (start us, length us, event | category | flops | bytes accessed | tf_op | source)
XLA Modules:
  0.0 901.8 jit_solution(3703537754444967372)
XLA Ops:
  15.7 7.2 all-to-all-start
  23.4 27.4 %all-to-all-done = bf16[2,2,2,512,256]{4,2,1,0,3:T(2,128)(2,1)S(1)} async-done(((bf16[2,2,2,512,256]{4,2,1,0,3:T(2,128)(2,1)}), bf16[2,2,2,512,256]{4,2,1,0,3:T(2,128)(2,1)S(1)}, u32[]{:S(2)}, u32[]{:S(2)}) %all-to-all-start) | async-done | bytes 2097184 | tf_op jit(solution)/shard_map/all_to_all | solution.py:81
  77.9 12.3 %fusion.37 = f32[64,2,2,32,64]{4,0,3,2,1:T(8,128)S(1)} fusion(f32[64,2,2,32,64]{4,0,3,2,1:T(8,128)S(1)} %convolution_add_fusion.3, f32[64,2,2,32,64]{4,0,3,2,1:T(8,128)S(1)} %convolution_subtract_fusion.3, f32[64,64]{1,0:T(8,128)S(1)} %copy.80, f32[64,64]{1,0:T(8,128)S(1)} %copy.79), kind=kOutput, calls=%fused_computation.42 | convolution fusion | flops 404287488 | bytes 6324224 | tf_op jit(solution)/shard_map/...kn,nl->...lk/dot_general | solution.py:31
  90.2 14.2 %fusion.35 = f32[64,2,2,32,64]{4,0,3,2,1:T(8,128)} fusion(f32[64,2,2,32,64]{4,0,3,2,1:T(8,128)S(1)} %convolution_add_fusion.3, f32[64,2,2,32,64]{4,0,3,2,1:T(8,128)S(1)} %convolution_subtract_fusion.3, f32[64,64]{1,0:T(8,128)S(1)} %copy.80, f32[64,64]{1,0:T(8,128)S(1)} %copy.79), kind=kOutput, calls=%fused_computation.40 | convolution fusion | flops 404283392 | bytes 6324224 | tf_op jit(solution)/shard_map/...kn,nl->...lk/dot_general | solution.py:31
  104.5 12.5 %fusion.69 = bf16[2,2,32,64,64]{4,3,2,1,0:T(8,128)(2,1)S(1)} fusion(f32[64,2,2,32,64]{4,0,3,2,1:T(8,128)S(1)} %fusion.37, f32[64,2,2,32,64]{4,0,3,2,1:T(8,128)S(1)} %convolution_add_fusion.3, f32[64,2,2,32,64]{4,0,3,2,1:T(8,128)S(1)} %convolution_subtract_fusion.3, f32[64,64]{1,0:T(8,128)S(1)} %copy.80, f32[64,64]{1,0:T(8,128)S(1)} %copy.79), kind=kOutput, calls=%fused_computation.87 | convolution fusion | flops 405331968 | bytes 7372800 | tf_op jit(solution)/shard_map/...kn,nl->...lk/dot_general | solution.py:31
  117.0 8.2 copy.99
  125.2 16.9 %fusion.72 = bf16[2,2,32,64,64]{4,3,2,1,0:T(8,128)(2,1)S(1)} fusion(f32[64,2,2,32,64]{4,0,3,2,1:T(8,128)} %fusion.35, f32[64,2,2,32,64]{4,0,3,2,1:T(8,128)} %copy-done.4, f32[64,2,2,32,64]{4,0,3,2,1:T(8,128)} %copy-done.3, f32[64,64]{1,0:T(8,128)S(1)} %copy.80, f32[64,64]{1,0:T(8,128)S(1)} %copy.79), kind=kOutput, calls=%fused_computation.88 | convolution fusion | flops 405336064 | bytes 7372800 | tf_op jit(solution)/shard_map/...kn,nl->...lk/dot_general | solution.py:31
  142.2 8.0 copy.100
  150.1 16.3 %fusion.338 = bf16[4096,2,2,2,32]{4,3,2,1,0:T(2,128)(2,1)} fusion(bf16[2,1,2,32,4096]{3,2,1,0,4:T(2,128)(2,1)} %bitcast.269, bf16[2,1,2,32,4096]{3,2,1,0,4:T(2,128)(2,1)} %bitcast.268), kind=kLoop, calls=%fused_computation.339 | loop fusion | flops 1048576 | bytes 4194304
  166.5 18.3 %reshape.436 = bf16[128,2,4096]{2,1,0:T(2,128)(2,1)} reshape(bf16[4096,2,2,2,32]{4,3,2,1,0:T(2,128)(2,1)} %fusion.338) | data formatting | bytes 4194304
  184.7 11.2 %all-to-all-start.1 = ((bf16[128,2,4096]{2,1,0:T(2,128)(2,1)}), bf16[128,2,4096]{2,1,0:T(2,128)(2,1)S(1)}, u32[]{:S(2)}, u32[]{:S(2)}) async-start(bf16[128,2,4096]{2,1,0:T(2,128)(2,1)} %reshape.436), calls=%async_computation.1 | async-start | bytes 4194304 | tf_op jit(solution)/shard_map/all_to_all | solution.py:67
  196.5 29.9 %all-to-all-done.1 = bf16[128,2,4096]{2,1,0:T(2,128)(2,1)S(1)} async-done(((bf16[128,2,4096]{2,1,0:T(2,128)(2,1)}), bf16[128,2,4096]{2,1,0:T(2,128)(2,1)S(1)}, u32[]{:S(2)}, u32[]{:S(2)}) %all-to-all-start.1) | async-done | bytes 2097184 | tf_op jit(solution)/shard_map/all_to_all | solution.py:67
  226.4 6.6 reshape.437
  232.9 12.0 %copy.107 = bf16[2,2,2,32,128,32]{3,4,5,2,1,0:T(8,128)(2,1)} copy(bf16[2,2,2,32,128,32]{3,2,1,0,5,4:T(2,128)(2,1)} %bitcast.264) | data formatting | bytes 4194304 | tf_op jit(solution)/shard_map/all_to_all | solution.py:67
  244.9 10.6 %all_to_all.57 = bf16[2,2,2,4096,32]{3,4,2,1,0:T(8,128)(2,1)S(1)} reshape(bf16[2,2,2,128,32,32]{4,3,5,2,1,0:T(8,128)(2,1)} %bitcast.265) | data formatting | bytes 4194304 | tf_op jit(solution)/shard_map/all_to_all | solution.py:67
  276.9 12.3 %fusion.29 = f32[64,2,2,64,32]{3,0,4,2,1:T(8,128)S(1)} fusion(f32[64,2,2,64,32]{3,0,4,2,1:T(8,128)S(1)} %convolution_add_fusion.2, f32[64,2,2,64,32]{3,0,4,2,1:T(8,128)S(1)} %convolution_subtract_fusion.2, f32[64,64]{1,0:T(8,128)S(1)} %copy.80, f32[64,64]{1,0:T(8,128)S(1)} %copy.79), kind=kOutput, calls=%fused_computation.34 | convolution fusion | flops 404287488 | bytes 6324224 | tf_op jit(solution)/shard_map/...knm,nl->...lkm/dot_general | solution.py:31
  289.1 12.7 %fusion.27 = f32[64,2,2,64,32]{3,0,4,2,1:T(8,128)S(1)} fusion(f32[64,2,2,64,32]{3,0,4,2,1:T(8,128)S(1)} %convolution_add_fusion.2, f32[64,2,2,64,32]{3,0,4,2,1:T(8,128)S(1)} %convolution_subtract_fusion.2, f32[64,64]{1,0:T(8,128)S(1)} %copy.80, f32[64,64]{1,0:T(8,128)S(1)} %copy.79), kind=kOutput, calls=%fused_computation.32 | convolution fusion | flops 404283392 | bytes 6324224 | tf_op jit(solution)/shard_map/...knm,nl->...lkm/dot_general | solution.py:31
  301.8 12.5 %subtract_bitcast_fusion = f32[2,2,64,64,32]{3,2,4,1,0:T(8,128)S(1)} fusion(f32[64,2,2,64,32]{3,0,4,2,1:T(8,128)S(1)} %fusion.29, f32[64,2,2,64,32]{3,0,4,2,1:T(8,128)S(1)} %convolution_add_fusion.2, f32[64,2,2,64,32]{3,0,4,2,1:T(8,128)S(1)} %convolution_subtract_fusion.2, f32[64,64]{1,0:T(8,128)S(1)} %copy.80, f32[64,64]{1,0:T(8,128)S(1)} %copy.79), kind=kOutput, calls=%fused_computation.57 | convolution fusion | flops 404807680 | bytes 8421376 | tf_op jit(solution)/shard_map/...knm,nl->...lkm/dot_general | solution.py:31
  314.3 12.3 %add_bitcast_fusion = f32[2,2,64,64,32]{3,2,4,1,0:T(8,128)S(1)} fusion(f32[64,2,2,64,32]{3,0,4,2,1:T(8,128)S(1)} %fusion.27, f32[64,2,2,64,32]{3,0,4,2,1:T(8,128)S(1)} %convolution_add_fusion.2, f32[64,2,2,64,32]{3,0,4,2,1:T(8,128)S(1)} %convolution_subtract_fusion.2, f32[64,64]{1,0:T(8,128)S(1)} %copy.80, f32[64,64]{1,0:T(8,128)S(1)} %copy.79), kind=kOutput, calls=%fused_computation.56 | convolution fusion | flops 404811776 | bytes 8421376 | tf_op jit(solution)/shard_map/...knm,nl->...lkm/dot_general | solution.py:31
  327.8 21.1 %fusion.67 = f32[64,2,2,64,32]{3,0,4,2,1:T(8,128)S(1)} fusion(f32[2,64,64,32]{2,1,3,0:T(8,128)S(1)} %get-tuple-element.18, f32[32]{0:T(128)S(1)} %fusion.194, f32[2,2,64,64]{3,2,1,0:T(8,128)S(1)} %broadcast_subtract_fusion.1, f32[2,64,64,32]{2,1,3,0:T(8,128)S(1)} %get-tuple-element.17), kind=kOutput, calls=%fused_computation.84 | convolution fusion | flops 407429120 | bytes 4259968 | tf_op jit(solution)/shard_map/...anm,ak->...knm/dot_general | solution.py:31
  348.9 21.3 %fusion.65 = f32[64,2,2,64,32]{3,0,4,2,1:T(8,128)S(1)} fusion(f32[2,64,64,32]{2,1,3,0:T(8,128)S(1)} %get-tuple-element.18, f32[32]{0:T(128)S(1)} %fusion.194, f32[2,2,64,64]{3,2,1,0:T(8,128)S(1)} %broadcast_subtract_fusion.1, f32[2,64,64,32]{2,1,3,0:T(8,128)S(1)} %get-tuple-element.17), kind=kOutput, calls=%fused_computation.83 | convolution fusion | flops 407429120 | bytes 4259968 | tf_op jit(solution)/shard_map/...anm,ak->...knm/dot_general | solution.py:31
  370.2 21.0 %convolution_subtract_fusion.1 = f32[64,2,2,64,32]{3,0,4,2,1:T(8,128)S(1)} fusion(f32[64,2,2,64,32]{3,0,4,2,1:T(8,128)S(1)} %fusion.67, f32[2,64,64,32]{2,1,3,0:T(8,128)S(1)} %get-tuple-element.18, f32[32]{0:T(128)S(1)} %fusion.194, f32[2,2,64,64]{3,2,1,0:T(8,128)S(1)} %broadcast_subtract_fusion.1, f32[2,64,64,32]{2,1,3,0:T(8,128)S(1)} %get-tuple-element.17), kind=kOutput, calls=%fused_computation.67 | convolution fusion | flops 407953408 | bytes 6357120 | tf_op jit(solution)/shard_map/...anm,ak->...knm/dot_general | solution.py:31
  391.2 21.5 %convolution_add_fusion.1 = f32[64,2,2,64,32]{3,0,4,2,1:T(8,128)S(1)} fusion(f32[64,2,2,64,32]{3,0,4,2,1:T(8,128)S(1)} %fusion.65, f32[2,64,64,32]{2,1,3,0:T(8,128)S(1)} %get-tuple-element.18, f32[32]{0:T(128)S(1)} %fusion.194, f32[2,2,64,64]{3,2,1,0:T(8,128)S(1)} %broadcast_subtract_fusion.1, f32[2,64,64,32]{2,1,3,0:T(8,128)S(1)} %get-tuple-element.17), kind=kOutput, calls=%fused_computation.66 | convolution fusion | flops 407953408 | bytes 6357120 | tf_op jit(solution)/shard_map/...anm,ak->...knm/dot_general | solution.py:31
  412.8 12.3 %fusion.21 = f32[64,2,2,64,32]{3,0,4,2,1:T(8,128)S(1)} fusion(f32[64,2,2,64,32]{3,0,4,2,1:T(8,128)S(1)} %convolution_add_fusion.1, f32[64,2,2,64,32]{3,0,4,2,1:T(8,128)S(1)} %convolution_subtract_fusion.1, f32[64,64]{1,0:T(8,128)S(1)} %copy.88, f32[64,64]{1,0:T(8,128)S(1)} %copy.79), kind=kOutput, calls=%fused_computation.26 | convolution fusion | flops 404283392 | bytes 6324224 | tf_op jit(solution)/shard_map/...knm,nl->...lkm/dot_general | solution.py:31
  425.1 13.8 %fusion.19 = f32[64,2,2,64,32]{3,0,4,2,1:T(8,128)} fusion(f32[64,2,2,64,32]{3,0,4,2,1:T(8,128)S(1)} %convolution_add_fusion.1, f32[64,2,2,64,32]{3,0,4,2,1:T(8,128)S(1)} %convolution_subtract_fusion.1, f32[64,64]{1,0:T(8,128)S(1)} %copy.88, f32[64,64]{1,0:T(8,128)S(1)} %copy.79), kind=kOutput, calls=%fused_computation.24 | convolution fusion | flops 404283392 | bytes 6324224 | tf_op jit(solution)/shard_map/...knm,nl->...lkm/dot_general | solution.py:31
  438.8 12.7 %fusion.75 = bf16[2,2,64,64,32]{3,2,4,1,0:T(8,128)(2,1)S(1)} fusion(f32[64,2,2,64,32]{3,0,4,2,1:T(8,128)S(1)} %fusion.21, f32[64,2,2,64,32]{3,0,4,2,1:T(8,128)S(1)} %convolution_add_fusion.1, f32[64,2,2,64,32]{3,0,4,2,1:T(8,128)S(1)} %convolution_subtract_fusion.1, f32[64,64]{1,0:T(8,128)S(1)} %copy.88, f32[64,64]{1,0:T(8,128)S(1)} %copy.79), kind=kOutput, calls=%fused_computation.89 | convolution fusion | flops 405856256 | bytes 7372800 | tf_op jit(solution)/shard_map/...knm,nl->...lkm/dot_general | solution.py:31
  453.2 16.9 %fusion.78 = bf16[2,2,64,64,32]{3,2,4,1,0:T(8,128)(2,1)S(1)} fusion(f32[64,2,2,64,32]{3,0,4,2,1:T(8,128)} %fusion.19, f32[64,2,2,64,32]{3,0,4,2,1:T(8,128)} %copy-done.6, f32[64,2,2,64,32]{3,0,4,2,1:T(8,128)} %copy-done.5, f32[64,64]{1,0:T(8,128)S(1)} %copy.88, f32[64,64]{1,0:T(8,128)S(1)} %copy.79), kind=kOutput, calls=%fused_computation.90 | convolution fusion | flops 405856256 | bytes 7372800 | tf_op jit(solution)/shard_map/...knm,nl->...lkm/dot_general | solution.py:31
  474.1 14.2 %copy.89 = bf16[2,2,2,4096,32]{4,2,1,0,3:T(2,128)(2,1)} copy(bf16[2,2,2,4096,32]{3,4,2,1,0:T(8,128)(2,1)S(1)} %pad_maximum_fusion.2) | data formatting | bytes 4194304 | tf_op jit(solution)/shard_map/stack | solution.py:108
  488.3 18.3 %reshape.438 = bf16[128,2,4096]{2,1,0:T(2,128)(2,1)} reshape(bf16[4096,2,2,2,32]{4,3,2,1,0:T(2,128)(2,1)} %bitcast.261) | data formatting | bytes 4194304
  506.5 4.7 all-to-all-start.2
  511.6 24.7 %gather_fusion = s32[4096]{0:T(1024)S(1)} fusion(s32[128]{0:T(128)S(1)} %dynamic-slice_reduce_fusion, s32[4096]{0:T(1024)S(1)} %broadcast_clamp_fusion), kind=kCustom, calls=%fused_computation | custom fusion | bytes 49152 | tf_op jit(solution)/shard_map/jit(_take)/gather | solution.py:102
  536.4 5.4 all-to-all-done.2
  541.8 6.6 reshape.439
  548.4 23.0 %copy.103 = bf16[2,2,2,128,32,32]{4,3,5,2,1,0:T(8,128)(2,1)} copy(bf16[2,2,2,128,32,32]{5,2,1,0,4,3:T(2,128)(2,1)} %bitcast.266) | data formatting | bytes 4194304 | tf_op jit(solution)/shard_map/all_to_all | solution.py:71
  571.4 6.0 fusion.335
  577.4 8.9 copy.91
  586.3 5.0 reshape.417
  599.3 8.9 copy.92
  608.2 5.2 reshape.418
  620.3 12.3 %fusion.13 = f32[64,2,2,32,64]{4,0,3,2,1:T(8,128)S(1)} fusion(f32[64,2,2,32,64]{4,0,3,2,1:T(8,128)S(1)} %convolution_add_fusion, f32[64,2,2,32,64]{4,0,3,2,1:T(8,128)S(1)} %convolution_subtract_fusion, f32[64,64]{1,0:T(8,128)S(1)} %copy.88, f32[64,64]{1,0:T(8,128)S(1)} %copy.79), kind=kOutput, calls=%fused_computation.18 | convolution fusion | flops 404283392 | bytes 6324224 | tf_op jit(solution)/shard_map/...kn,nl->...lk/dot_general | solution.py:31
  632.6 14.0 %fusion.11 = f32[64,2,2,32,64]{4,0,3,2,1:T(8,128)} fusion(f32[64,2,2,32,64]{4,0,3,2,1:T(8,128)S(1)} %convolution_add_fusion, f32[64,2,2,32,64]{4,0,3,2,1:T(8,128)S(1)} %convolution_subtract_fusion, f32[64,64]{1,0:T(8,128)S(1)} %copy.88, f32[64,64]{1,0:T(8,128)S(1)} %copy.79), kind=kOutput, calls=%fused_computation.16 | convolution fusion | flops 404283392 | bytes 6324224 | tf_op jit(solution)/shard_map/...kn,nl->...lk/dot_general | solution.py:31
  646.6 12.5 %fusion.81 = bf16[2,2,32,64,64]{4,3,2,1,0:T(8,128)(2,1)S(1)} fusion(f32[64,2,2,32,64]{4,0,3,2,1:T(8,128)S(1)} %fusion.13, f32[64,2,2,32,64]{4,0,3,2,1:T(8,128)S(1)} %convolution_add_fusion, f32[64,2,2,32,64]{4,0,3,2,1:T(8,128)S(1)} %convolution_subtract_fusion, f32[64,64]{1,0:T(8,128)S(1)} %copy.88, f32[64,64]{1,0:T(8,128)S(1)} %copy.79), kind=kOutput, calls=%fused_computation.91 | convolution fusion | flops 405856256 | bytes 7372800 | tf_op jit(solution)/shard_map/...kn,nl->...lk/dot_general | solution.py:31
  661.1 16.9 %fusion.84 = bf16[2,2,32,64,64]{4,3,2,1,0:T(8,128)(2,1)S(1)} fusion(f32[64,2,2,32,64]{4,0,3,2,1:T(8,128)} %fusion.11, f32[64,2,2,32,64]{4,0,3,2,1:T(8,128)} %copy-done.2, f32[64,2,2,32,64]{4,0,3,2,1:T(8,128)} %copy-done.1, f32[64,64]{1,0:T(8,128)S(1)} %copy.88, f32[64,64]{1,0:T(8,128)S(1)} %copy.79), kind=kOutput, calls=%fused_computation.92 | convolution fusion | flops 405856256 | bytes 7372800 | tf_op jit(solution)/shard_map/...kn,nl->...lk/dot_general | solution.py:31
  681.9 14.2 %copy.94 = bf16[2,2,2,32,4096]{3,2,1,0,4:T(2,128)(2,1)} copy(bf16[2,2,2,32,4096]{4,3,2,1,0:T(8,128)(2,1)S(1)} %pad_maximum_fusion.3) | data formatting | bytes 4194304 | tf_op jit(solution)/shard_map/stack | solution.py:111
  696.1 14.5 %reshape.440 = bf16[16,2,32768]{2,1,0:T(2,128)(2,1)} reshape(bf16[4096,2,2,2,32]{4,3,2,1,0:T(2,128)(2,1)} %bitcast.262) | data formatting | bytes 4194304
  717.1 147.9 %all-reduce.2.cloned.1.call-done = f32[8,4096]{1,0:T(8,128)} async-done(((f32[8,4096]{1,0:T(8,128)}), f32[8,4096]{1,0:T(8,128)}) %all-reduce.2.cloned.1.call-update) | async-done | bytes 131088 | tf_op jit(solution)/shard_map/psum | solution.py:127
  866.6 8.7 reshape.441
  875.3 17.8 %copy.95 = bf16[2,2,2,16,32,256]{5,4,3,1,0,2:T(8,128)(2,1)S(1)} copy(bf16[2,2,2,16,32,256]{4,2,1,0,5,3:T(2,128)(2,1)} %bitcast.263) | data formatting | bytes 4194304 | tf_op jit(solution)/shard_map/all_to_all | solution.py:110
  (81 shorter events, 95.1 us)
Async XLA Ops:
  7.2 504.1 %copy-start = (s32[128,128]{1,0:T(8,128)S(1)}, s32[128,128]{1,0:T(8,128)}, u32[]{:S(2)}) copy-start(s32[128,128]{1,0:T(8,128)} %param.13) | copy-start | bytes 196612
  15.7 35.1 %all-to-all-start = ((bf16[2,2,2,512,256]{4,2,1,0,3:T(2,128)(2,1)}), bf16[2,2,2,512,256]{4,2,1,0,3:T(2,128)(2,1)S(1)}, u32[]{:S(2)}, u32[]{:S(2)}) async-start(bf16[2,2,2,512,256]{4,2,1,0,3:T(2,128)(2,1)} %pad_maximum_fusion.1), calls=%async_computation | async-start | bytes 4194304 | tf_op jit(solution)/shard_map/all_to_all | solution.py:81
  71.1 4.7 copy-start.8
  75.8 28.7 %copy-start.3 = (f32[64,2,2,32,64]{4,0,3,2,1:T(8,128)}, f32[64,2,2,32,64]{4,0,3,2,1:T(8,128)S(1)}, u32[]{:S(2)}) copy-start(f32[64,2,2,32,64]{4,0,3,2,1:T(8,128)S(1)} %convolution_subtract_fusion.3) | copy-start | bytes 6291460
  77.9 26.5 %copy-start.4 = (f32[64,2,2,32,64]{4,0,3,2,1:T(8,128)}, f32[64,2,2,32,64]{4,0,3,2,1:T(8,128)S(1)}, u32[]{:S(2)}) copy-start(f32[64,2,2,32,64]{4,0,3,2,1:T(8,128)S(1)} %convolution_add_fusion.3) | copy-start | bytes 6291460
  184.7 11.5 %copy-start.11 = (f32[2]{0:T(128)S(1)}, f32[2]{0:T(128)}, u32[]{:S(2)}) copy-start(f32[2]{0:T(128)} %param.12) | copy-start | bytes 28
  184.7 11.5 %copy-start.12 = (f32[2]{0:T(128)S(1)}, f32[2]{0:T(128)}, u32[]{:S(2)}) copy-start(f32[2]{0:T(128)} %param.11) | copy-start | bytes 28
  184.7 41.6 %all-to-all-start.1 = ((bf16[128,2,4096]{2,1,0:T(2,128)(2,1)}), bf16[128,2,4096]{2,1,0:T(2,128)(2,1)S(1)}, u32[]{:S(2)}, u32[]{:S(2)}) async-start(bf16[128,2,4096]{2,1,0:T(2,128)(2,1)} %reshape.436), calls=%async_computation.1 | async-start | bytes 4194304 | tf_op jit(solution)/shard_map/all_to_all | solution.py:67
  270.3 4.4 copy-start.9
  391.2 47.6 %copy-start.5 = (f32[64,2,2,64,32]{3,0,4,2,1:T(8,128)}, f32[64,2,2,64,32]{3,0,4,2,1:T(8,128)S(1)}, u32[]{:S(2)}) copy-start(f32[64,2,2,64,32]{3,0,4,2,1:T(8,128)S(1)} %convolution_subtract_fusion.1) | copy-start | bytes 6291460
  412.8 26.1 %copy-start.6 = (f32[64,2,2,64,32]{3,0,4,2,1:T(8,128)}, f32[64,2,2,64,32]{3,0,4,2,1:T(8,128)S(1)}, u32[]{:S(2)}) copy-start(f32[64,2,2,64,32]{3,0,4,2,1:T(8,128)S(1)} %convolution_add_fusion.1) | copy-start | bytes 6291460
  506.5 4.9 copy-start.10
  506.5 35.3 %all-to-all-start.2 = ((bf16[128,2,4096]{2,1,0:T(2,128)(2,1)}), bf16[128,2,4096]{2,1,0:T(2,128)(2,1)S(1)}, u32[]{:S(2)}, u32[]{:S(2)}) async-start(bf16[128,2,4096]{2,1,0:T(2,128)(2,1)} %reshape.438), calls=%async_computation.2 | async-start | bytes 4194304 | tf_op jit(solution)/shard_map/all_to_all | solution.py:71
  613.5 4.7 copy-start.7
  618.2 28.4 %copy-start.1 = (f32[64,2,2,32,64]{4,0,3,2,1:T(8,128)}, f32[64,2,2,32,64]{4,0,3,2,1:T(8,128)S(1)}, u32[]{:S(2)}) copy-start(f32[64,2,2,32,64]{4,0,3,2,1:T(8,128)S(1)} %convolution_subtract_fusion) | copy-start | bytes 6291460
  620.3 26.3 %copy-start.2 = (f32[64,2,2,32,64]{4,0,3,2,1:T(8,128)}, f32[64,2,2,32,64]{4,0,3,2,1:T(8,128)S(1)}, u32[]{:S(2)}) copy-start(f32[64,2,2,32,64]{4,0,3,2,1:T(8,128)S(1)} %convolution_add_fusion) | copy-start | bytes 6291460
  710.6 156.0 %all-to-all-start.3 = ((bf16[16,2,32768]{2,1,0:T(2,128)(2,1)}), bf16[16,2,32768]{2,1,0:T(2,128)(2,1)S(1)}, u32[]{:S(2)}, u32[]{:S(2)}) async-start(bf16[16,2,32768]{2,1,0:T(2,128)(2,1)} %reshape.440), calls=%async_computation.3 | async-start | bytes 4194304 | tf_op jit(solution)/shard_map/all_to_all | solution.py:110
  715.2 149.8 %all-reduce.2.cloned.1.call-start = ((), (), s32[]{:S(2)}) async-start(), calls=%async_computation.4 | async-start | bytes 262144 | tf_op jit(solution)/shard_map/psum | solution.py:127
Sparse Core Ops, SparseCore 0:
  721.4 143.6 all-reduce.1
where the time goes:
time: 908 us; the launch traced here: 902 us
  matrix products  346 us (38%)
  local copies, waits for them, and re-layouts  273 us (30%)
  waiting for transfers between devices  211 us (23%)
  other arithmetic  29.9 us (3%)
  starting transfers between devices  27.8 us (3%)
  between operations  15 us (2%)
    dot_general x32, matrix products, contract(): return jnp.einsum(form, values, matrix, precision=lax.Precision.HIGHEST)  346 us
    psum x1, waiting for transfers between devices, per_device(): summed = lax.psum(contrib, ('inl', 'xl'))  148 us
    unnamed x32, local copies, waits for them, and re-layouts  72.9 us
    all_to_all x1, waiting for transfers between devices, to_spectrum(): lax.all_to_all(packed, ('inl', 'xl'), split_axis=4, concat_axis=3, tiled=...  29.9 us
    all_to_all x1, waiting for transfers between devices, one_step(): wide = lax.all_to_all(block, 'xl', split_axis=3, concat_axis=4, tiled=True)  27.4 us
    gather x1, local copies, waits for them, and re-layouts, one_step(): tile_rows = jnp.repeat(wedge_cols, TILE, axis=0, total_repeat_length=rows)  24.7 us
    all_to_all x1, local copies, waits for them, and re-layouts, to_lines(): lax.all_to_all(packed, ('inl', 'xl'), split_axis=3, concat_axis=4, tiled=...  23 us
    all_to_all x2, local copies, waits for them, and re-layouts, to_spectrum(): lax.all_to_all(packed, ('inl', 'xl'), split_axis=4, concat_axis=3, tiled=...  22.6 us
  transfers between devices with their start and end apart: 5, of which 4 were waited for; matrix products, arithmetic and copies ran while one was open for 3% of the time, Pallas kernels for 0%

commit v1 on v0

v1 whole, which is shorter than its diff:
```python
import functools
import math

import jax
import jax.numpy as jnp
import ml_dtypes
import numpy as np
from jax import lax
from jax.experimental import pallas as pl
from jax.experimental.pallas import tpu as pltpu
from jax.sharding import PartitionSpec as P

SIZE = 4096
DEVICES = 128
GROUP = 16
BF16 = jnp.bfloat16
F32 = jnp.float32
EVERY = ("inl", "xl")
HALF = math.sqrt(0.5)


def roots(rows, cols, length, sign):
    turn = np.outer(np.arange(rows), np.arange(cols)) % length
    return np.exp(sign * 2j * np.pi * turn / length)


def as_block(matrix):
    return np.block([[matrix.real, matrix.imag], [-matrix.imag, matrix.real]])


def two_parts(matrix):
    high = matrix.astype(np.float32).astype(ml_dtypes.bfloat16)
    low = (matrix - high.astype(np.float64)).astype(np.float32).astype(ml_dtypes.bfloat16)
    return high, low


def pair_table(values):
    return np.stack([values.real, values.imag]).astype(np.float32)


@functools.lru_cache(None)
def tables():
    out = {}
    high, low = two_parts(as_block(roots(128, 128, 128, -1)).T)
    out["cross_fwd"] = np.concatenate([high, high, low], axis=1)
    high, low = two_parts(as_block(roots(128, 128, 128, 1)) / SIZE)
    out["cross_inv"] = np.concatenate([high, low], axis=0)
    out["cross_tw_fwd"] = pair_table(roots(32, 128, SIZE, -1))
    out["cross_tw_inv"] = pair_table(roots(32, 128, SIZE, 1))
    for name, sign, scale in (("fwd", -1, 1.0), ("inv", 1, 1.0 / SIZE)):
        lanes = np.kron(np.eye(4), roots(32, 32, 32, sign))
        high, low = two_parts(as_block(lanes) * scale)
        out["inline_" + name] = np.concatenate([high, high, low], axis=0)
        out["inline_tw_" + name] = pair_table(np.tile(roots(128, 32, SIZE, sign), (1, 4)))
    return out


def add(x, y):
    return (x[0] + y[0], x[1] + y[1])


def sub(x, y):
    return (x[0] - y[0], x[1] - y[1])


def times(x, y):
    return (x[0] * y[0] - x[1] * y[1], x[0] * y[1] + x[1] * y[0])


def turn(x, numerator, length, sign):
    eighth = 8 * (numerator % length) * sign % (8 * length)
    if eighth % length:
        angle = sign * 2.0 * math.pi * (numerator % length) / length
        c, s = math.cos(angle), math.sin(angle)
        return (x[0] * c - x[1] * s, x[0] * s + x[1] * c)
    eighth = eighth // length
    r, i = x
    if eighth == 0:
        return x
    if eighth == 1:
        return ((r - i) * HALF, (r + i) * HALF)
    if eighth == 2:
        return (-i, r)
    if eighth == 3:
        return ((r + i) * -HALF, (r - i) * HALF)
    if eighth == 4:
        return (-r, -i)
    if eighth == 5:
        return ((i - r) * HALF, (r + i) * -HALF)
    if eighth == 6:
        return (i, -r)
    return ((r + i) * HALF, (i - r) * HALF)


def dft(x, sign):
    length = len(x)
    if length == 2:
        return [add(x[0], x[1]), sub(x[0], x[1])]
    if length == 4:
        t0, t1 = add(x[0], x[2]), sub(x[0], x[2])
        t2, t3 = add(x[1], x[3]), sub(x[1], x[3])
        r, i = t3
        if sign < 0:
            return [add(t0, t2), (t1[0] + i, t1[1] - r), sub(t0, t2), (t1[0] - i, t1[1] + r)]
        return [add(t0, t2), (t1[0] - i, t1[1] + r), sub(t0, t2), (t1[0] + i, t1[1] - r)]
    first = {8: 2, 16: 4, 32: 8}[length]
    second = length // first
    inner = [dft(x[low::second], sign) for low in range(second)]
    out = [None] * length
    for q in range(first):
        row = [turn(inner[low][q], low * q, length, sign) for low in range(second)]
        for p, value in enumerate(dft(row, sign)):
            out[q + first * p] = value
    return out


def dft128(load, store, work, sign):
    for low in range(8):
        values = dft([load(8 * high + low) for high in range(16)], sign)
        for q in range(16):
            r, i = turn(values[q], low * q, 128, sign)
            work[q * 8 + low, 0] = r
            work[q * 8 + low, 1] = i
    for q in range(16):
        values = dft([(work[q * 8 + low, 0], work[q * 8 + low, 1]) for low in range(8)], sign)
        for p in range(8):
            store(q + 16 * p, values[p])


def split(value):
    high = value.astype(BF16)
    low = (value - high.astype(F32)).astype(BF16)
    return jnp.concatenate([high, low, high], axis=1)


def dot(x, y, dims=((1,), (0,))):
    return lax.dot_general(x, y, (dims, ((), ())), preferred_element_type=F32)


def pack_kernel(receiver, source, weight, out):
    for which, field in enumerate((receiver, source)):
        for part in range(2):
            row = which * 64 + part * 32
            out[:, row : row + 32, :] = field[part, 0]
    value = weight[:, 0]
    high = value >> 7
    code = 1.0 + (value & 127).astype(F32) * (1.0 / 128.0)
    for power in (1, 2, 4, 8, 16, 32):
        code = code * jnp.where((high & power) != 0, 2.0**power, 1.0)
    out[:, 128:144, :] = code.astype(BF16)


def phase_kernel(place, omega, slowness, wedge_map, phase, wedges):
    freq = pl.program_id(0)
    device = place[0]
    step = 2.0 * math.pi / SIZE

    def signed(index):
        index = jnp.where(index >= SIZE // 2, index - SIZE, index)
        return step * index.astype(F32)

    def body(part, carry):
        row = part * 64 + lax.broadcasted_iota(jnp.int32, (64, 128), 0)
        lane = lax.broadcasted_iota(jnp.int32, (64, 128), 1)
        kx = signed((row >> 3) + 128 * (lane & 31))
        ky = signed(device * 32 + 4 * (row & 7) + (lane >> 5))
        kx_sq = kx * kx
        ky_sq = ky * ky
        rows = pl.ds(pl.multiple_of(part * 64, 64), 64)
        for ref in range(2):
            number = omega[freq] * slowness[ref]
            quad = number * number - kx_sq - ky_sq
            root = jnp.sqrt(jnp.abs(quad))
            decay = jnp.exp(-root)
            inside = jnp.maximum(quad, 0.0)
            even = jnp.full_like(quad, 1.0 / math.factorial(22))
            odd = jnp.full_like(quad, 1.0 / math.factorial(23))
            for n in range(10, -1, -1):
                even = 1.0 / math.factorial(2 * n) - inside * even
                odd = 1.0 / math.factorial(2 * n + 1) - inside * odd
            phase[0, ref, 0, rows, :] = jnp.where(quad >= 0, even, decay)
            phase[0, ref, 1, rows, :] = jnp.where(quad >= 0, odd * root, 0.0)
        return carry

    lax.fori_loop(0, 16, body, 0)

    @pl.when(freq == 0)
    def _():
        rows = wedge_map[pl.ds(place[1] // 4, 32, stride=4), :].astype(F32)
        wedges[...] = jnp.concatenate([rows] * 4, axis=0).T


def cross_forward_kernel(lines, twist, matrix, out, mid, turned):
    def field(which, carry):
        for part in range(2):
            values = []
            for a in range(32):
                lanes = pl.ds((a % 2) * 128, 128)
                pair = []
                for side in range(2):
                    row = pl.multiple_of(which * 64 + side * 32 + part * 16, 16)
                    pair.append(lines[a // 2, pl.ds(row, 16), lanes].astype(F32))
                values.append(tuple(pair))
            for k, value in enumerate(dft(values, -1)):
                r, i = times(value, (twist[0, k : k + 1, :], twist[1, k : k + 1, :]))
                row = k * 32 + part * 16
                mid[row : row + 16, 0:128] = r
                mid[row : row + 16, 128:256] = i
        for part in range(4):
            parts = split(mid[part * 256 : part * 256 + 256, :])
            value = dot(matrix[...], parts, ((1,), (1,)))
            for side in range(2):
                for half in range(2):
                    turned[pl.ds(side * 8 + part * 2 + half, 128, stride=16), :] = value[
                        side * 128 : side * 128 + 128, half * 128 : half * 128 + 128
                    ]
        rows = pl.ds(pl.multiple_of(which * 16, 16), 16)
        out[:, rows, :] = turned[...].reshape(128, 16, 128).astype(BF16)
        return carry

    lax.fori_loop(0, 2, field, 0)


def inline_kernel(
    lines, phase, twist, twist_inv, matrix, matrix_inv, out, work, mid, spec, term
):
    freq = pl.program_id(0)

    def forward(which, carry):
        rows = pl.ds(pl.multiple_of(which * 16, 16), 16)

        def load(s):
            value = lines[s, rows, :].astype(F32)
            return (value[0:8], value[8:16])

        def store(k, value):
            r, i = times(value, (twist[0, k : k + 1, :], twist[1, k : k + 1, :]))
            mid[8 * k : 8 * k + 8, 0:128] = r
            mid[8 * k : 8 * k + 8, 128:256] = i

        dft128(load, store, work, -1)
        for part in range(4):
            block = slice(part * 256, part * 256 + 256)
            spec[which, block, :] = dot(split(mid[block, :]), matrix[...])
        return carry

    lax.fori_loop(0, 2, forward, 0)

    @pl.when(freq == 0)
    def _():
        term[...] = jnp.zeros_like(term)

    for part in range(4):
        block = slice(part * 256, part * 256 + 256)
        both = spec[0, block, :] * spec[1, block, :]
        term[block, :] += both[:, 0:128] + both[:, 128:256]

    def inverse(ref, carry):
        for part in range(4):
            block = slice(part * 256, part * 256 + 256)
            value = (spec[0, block, 0:128], spec[0, block, 128:256])
            turned = times(value, (phase[0, ref, 0, block, :], phase[0, ref, 1, block, :]))
            mid[block, :] = dot(split(jnp.concatenate(turned, axis=1)), matrix_inv[...])

        def load(k):
            value = (mid[8 * k : 8 * k + 8, 0:128], mid[8 * k : 8 * k + 8, 128:256])
            return times(value, (twist_inv[0, k : k + 1, :], twist_inv[1, k : k + 1, :]))

        rows = pl.ds(pl.multiple_of(freq * 32 + ref * 16, 16), 16)

        def store(s, value):
            out[s, rows, :] = jnp.concatenate(value, axis=0).astype(BF16)

        dft128(load, store, work, 1)
        return carry

    lax.fori_loop(0, 2, inverse, 0)

    @pl.when(freq == 1)
    def _():
        total = term[...].reshape(128, 8, 128).sum(axis=1)
        total = total + pltpu.roll(total, 64, 1)
        total = total + pltpu.roll(total, 32, 1)
        high = total.astype(BF16).astype(F32)
        rest = total - high
        middle = rest.astype(BF16).astype(F32)
        low = rest - middle
        place = lax.broadcasted_iota(jnp.int32, (128, 128), 1) >> 5
        value = jnp.where(place == 0, high, jnp.where(place == 1, middle, low))
        value = jnp.where(place == 3, 0.0, value).reshape(16, 8, 128).astype(BF16)
        for group in range(8):
            out[group * 16 : group * 16 + 16, 64:72, :] = value


def cross_inverse_kernel(
    lines, sums, wedges, weight_one, weight_two, twist, matrix, out, flat, mid, kept, share
):
    freq = pl.program_id(0)

    @pl.when(freq == 0)
    def _():
        for half, coded in enumerate((weight_one, weight_two)):
            value = coded[...].astype(F32)
            high = jnp.zeros_like(value)
            for power in (32, 16, 8, 4, 2, 1):
                over = value >= 2.0**power
                value = jnp.where(over, value * 2.0**-power, value)
                high = jnp.where(over, high + float(power), high)
            share[:, half * 16 : half * 16 + 16, :] = (high + (value - 1.0)) * (1.0 / 32.0)

        def gather(d, totals):
            value = sums[d].astype(F32)
            where = wedges[pl.ds(d, 1), :]
            return tuple(
                total + jnp.where(where == float(w), value, 0.0) for w, total in enumerate(totals)
            )

        zero = jnp.zeros((8, 128), F32)
        totals = lax.fori_loop(0, 128, gather, (zero,) * 8, unroll=8)
        highs, lows = [], []
        for total in totals:
            total = total + pltpu.roll(total, 64, 1)
            total = total + pltpu.roll(total, 32, 1)
            total = total * (1.0 / (SIZE * SIZE * math.sqrt(SIZE)))
            highs.append(total.astype(BF16).astype(F32))
            lows.append(total - highs[-1])
        place = lax.broadcasted_iota(jnp.int32, (8, 128), 1) >> 5
        for half in range(2):
            rows = []
            for first in (half * 2, half * 2 + 4):
                even = jnp.where(place == 0, highs[first], lows[first])
                odd = jnp.where(place == 2, highs[first + 1], lows[first + 1])
                rows.append(jnp.where(place < 2, even, odd))
            value = jnp.concatenate(rows, axis=0).astype(BF16)
            for group in range(16):
                out[group, 128:144, half * 128 : half * 128 + 128] = value

    for ref in range(2):
        flat[...] = lines[:, ref * 16 : ref * 16 + 16, :].astype(F32).reshape(2048, 128)
        for g in range(8):
            pair = [flat[pl.ds(side * 8 + g, 128, stride=16), :] for side in range(2)]
            value = jnp.concatenate([x.T for x in pair], axis=1).astype(BF16)
            mid[g * 128 : g * 128 + 128, :] = dot(
                jnp.concatenate([value, value], axis=1), matrix[...]
            )

        def rows16(part, carry):
            start = pl.multiple_of(part * 16, 16)
            values = []
            for k in range(32):
                rows = pl.ds(pl.multiple_of(k * 32 + part * 16, 16), 16)
                values.append(
                    times(
                        (mid[rows, 0:128], mid[rows, 128:256]),
                        (twist[0, k : k + 1, :], twist[1, k : k + 1, :]),
                    )
                )
            for a, value in enumerate(dft(values, 1)):
                lanes = slice((a % 2) * 128, (a % 2) * 128 + 128)
                for side in range(2):
                    rounded = value[side].astype(BF16)
                    if ref == 0:
                        kept[a, side, pl.ds(start, 16), :] = rounded
                    else:
                        s = share[a // 2, pl.ds(start, 16), lanes]
                        first = kept[a, side, pl.ds(start, 16), :].astype(F32)
                        mixed = first * s + rounded.astype(F32) * (1.0 - s)
                        row = pl.multiple_of(freq * 64 + side * 32 + part * 16, 16)
                        out[a // 2, pl.ds(row, 16), lanes] = mixed.astype(BF16)
            return carry

        lax.fori_loop(0, 2, rows16, 0)


def unpack_kernel(block, coded, out, angles):
    out[0, 0] = block[...]

    @pl.when(pl.program_id(0) == 0)
    def _():
        value = coded[...].astype(F32)
        for half in range(2):
            for top in range(2):
                part = value[:, top * 8 : top * 8 + 8, half * 128 : half * 128 + 128]
                flipped = part.reshape(128, 128).T
                w = top * 4 + half * 2
                angles[w] = flipped[0:32] + flipped[32:64]
                angles[w + 1] = flipped[64:96] + flipped[96:128]


def whole(shape):
    return pl.BlockSpec(shape, lambda *_: (0,) * len(shape))


def fixed(shape, index):
    return pl.BlockSpec(shape, lambda *_: index)


def params():
    return pltpu.CompilerParams(vmem_limit_bytes=56 * 2**20)


def pack(receiver, source, weight):
    field = pl.BlockSpec((2, 1, GROUP, 32, 256), lambda f: (0, f, 0, 0, 0))
    return pl.pallas_call(
        pack_kernel,
        grid=(2,),
        in_specs=[field, field, pl.BlockSpec((GROUP, 1, 16, 256), lambda f: (0, f, 0, 0))],
        out_specs=pl.BlockSpec((GROUP, 144, 256), lambda f: (0, f, 0)),
        out_shape=jax.ShapeDtypeStruct((GROUP, 288, 256), BF16),
        compiler_params=params(),
        name="pack_fields",
    )(
        receiver.reshape(2, 2, GROUP, 32, 256),
        source.reshape(2, 2, GROUP, 32, 256),
        weight.reshape(GROUP, 2, 16, 256),
    )


def phases(place, omega, slowness, wedge_map):
    scalar = pl.BlockSpec(memory_space=pltpu.SMEM)
    return pl.pallas_call(
        phase_kernel,
        grid=(2,),
        in_specs=[scalar, scalar, scalar, whole((128, 128))],
        out_specs=[
            pl.BlockSpec((1, 2, 2, 1024, 128), lambda f: (f, 0, 0, 0, 0)),
            whole((128, 128)),
        ],
        out_shape=[
            jax.ShapeDtypeStruct((2, 2, 2, 1024, 128), F32),
            jax.ShapeDtypeStruct((128, 128), F32),
        ],
        compiler_params=params(),
        name="phase_table",
    )(place, omega, slowness, wedge_map)


def cross_forward(packed):
    t = tables()
    return pl.pallas_call(
        cross_forward_kernel,
        grid=(2,),
        in_specs=[
            pl.BlockSpec((GROUP, 144, 256), lambda f: (0, f, 0)),
            whole((2, 32, 128)),
            whole((256, 768)),
        ],
        out_specs=pl.BlockSpec((DEVICES, 32, 128), lambda f: (0, f, 0)),
        out_shape=jax.ShapeDtypeStruct((DEVICES, 64, 128), BF16),
        scratch_shapes=[pltpu.VMEM((1024, 256), F32), pltpu.VMEM((2048, 128), F32)],
        compiler_params=params(),
        name="crossline_forward",
    )(packed, jnp.asarray(t["cross_tw_fwd"]), jnp.asarray(t["cross_fwd"]))


def inline_step(lines, phase):
    t = tables()
    return pl.pallas_call(
        inline_kernel,
        grid=(2,),
        in_specs=[
            pl.BlockSpec((DEVICES, 32, 128), lambda f: (0, f, 0)),
            pl.BlockSpec((1, 2, 2, 1024, 128), lambda f: (f, 0, 0, 0, 0)),
            whole((2, 128, 128)),
            whole((2, 128, 128)),
            whole((768, 256)),
            whole((768, 256)),
        ],
        out_specs=whole((DEVICES, 72, 128)),
        out_shape=jax.ShapeDtypeStruct((DEVICES, 72, 128), BF16),
        scratch_shapes=[
            pltpu.VMEM((128, 2, 8, 128), F32),
            pltpu.VMEM((1024, 256), F32),
            pltpu.VMEM((2, 1024, 256), F32),
            pltpu.VMEM((1024, 128), F32),
        ],
        compiler_params=params(),
        name="inline_step",
    )(
        lines,
        phase,
        jnp.asarray(t["inline_tw_fwd"]),
        jnp.asarray(t["inline_tw_inv"]),
        jnp.asarray(t["inline_fwd"]),
        jnp.asarray(t["inline_inv"]),
    )


def cross_inverse(partial, wedges, packed):
    t = tables()
    return pl.pallas_call(
        cross_inverse_kernel,
        grid=(2,),
        in_specs=[
            pl.BlockSpec((DEVICES, 32, 128), lambda f: (0, f, 0)),
            fixed((DEVICES, 8, 128), (0, 8, 0)),
            whole((128, 128)),
            fixed((GROUP, 16, 256), (0, 8, 0)),
            fixed((GROUP, 16, 256), (0, 17, 0)),
            whole((2, 32, 128)),
            whole((512, 256)),
        ],
        out_specs=whole((GROUP, 144, 256)),
        out_shape=jax.ShapeDtypeStruct((GROUP, 144, 256), BF16),
        scratch_shapes=[
            pltpu.VMEM((2048, 128), F32),
            pltpu.VMEM((1024, 256), F32),
            pltpu.VMEM((32, 2, 32, 128), BF16),
            pltpu.VMEM((GROUP, 32, 256), F32),
        ],
        compiler_params=params(),
        name="crossline_inverse",
    )(
        partial,
        partial,
        wedges,
        packed,
        packed,
        jnp.asarray(t["cross_tw_inv"]),
        jnp.asarray(t["cross_inv"]),
    )


def unpack(home):
    return pl.pallas_call(
        unpack_kernel,
        grid=(4,),
        in_specs=[
            pl.BlockSpec((GROUP, 32, 256), lambda c: (0, c, 0)),
            fixed((GROUP, 16, 256), (0, 8, 0)),
        ],
        out_specs=[
            pl.BlockSpec((1, 1, GROUP, 32, 256), lambda c: (c % 2, c // 2, 0, 0, 0)),
            whole((8, 32, 128)),
        ],
        out_shape=[
            jax.ShapeDtypeStruct((2, 2, GROUP, 32, 256), BF16),
            jax.ShapeDtypeStruct((8, 32, 128), F32),
        ],
        compiler_params=params(),
        name="unpack_fields",
    )(home, home)


def exchange(value, axes):
    return lax.all_to_all(value, axes, 0, 0, tiled=True)


def per_device(receiver, source, weight, omega, slowness, wedge_map):
    line = lax.axis_index("xl")
    place = jnp.stack([lax.axis_index("inl") * GROUP + line, line]).astype(jnp.int32)
    packed = exchange(pack(receiver, source, weight), "xl")
    phase, wedges = phases(place, omega, slowness, wedge_map)
    lines = exchange(cross_forward(packed), EVERY)
    partial = exchange(inline_step(lines, phase), EVERY)
    home = exchange(cross_inverse(partial, wedges, packed), "xl")
    mixed, angles = unpack(home)
    return (mixed.reshape(2, 2, 512, 256), angles.reshape(8, SIZE))


def solution(mesh):
    return jax.shard_map(
        per_device,
        mesh=mesh,
        in_specs=(
            P(None, None, "inl", "xl"),
            P(None, None, "inl", "xl"),
            P("inl", "xl"),
            P(),
            P(),
            P(),
        ),
        out_specs=(P(None, None, "inl", "xl"), P()),
        check_vma=False,
    )
```

time: 908 us -> 177 us (0.19)
  matrix products: 346 us -> 0 us
  local copies, waits for them, and re-layouts: 273 us -> 3.02 us
  waiting for transfers between devices: 211 us -> 22.1 us
  blocking collectives: 0 us -> 98.4 us
  Pallas kernels: 0 us -> 43.2 us
  other arithmetic: 29.9 us -> 0.65 us
  starting transfers between devices: 27.8 us -> 8.46 us
  between operations: 15 us -> 0.65 us
    dot_general x32 -> x0, matrix products: 346 us -> none  [contract(): return jnp.einsum(form, values, matrix, precision=lax.Precision.HIGHEST)]
    psum x1 -> x0, waiting for transfers between devices: 148 us -> none  [per_device(): summed = lax.psum(contrib, ('inl', 'xl'))]
    all_to_all x0 -> x3, blocking collectives: none -> 98.4 us  [exchange(): return lax.all_to_all(value, axes, 0, 0, tiled=True)]
    unnamed x32 -> x3, local copies, waits for them, and re-layouts: 72.9 us -> 3.02 us
    all_to_all x6 -> x0, local copies, waits for them, and re-layouts: 68.8 us -> none  [the longest x1 23 us: to_lines(): lax.all_to_all(packed, ('inl', 'xl'), split_axis=3, concat_axis=4, tiled=...]
    another operation x5 -> x0, local copies, waits for them, and re-layouts: 49.1 us -> none  [the longest x2 16.2 us: one_step(): spec = to_spectrum(jnp.stack([yr, yi], axis=1).astype(jnp.bfloat16))]
    pallas_call x0 -> x6, Pallas kernels: none -> 43.2 us  [the longest x1 12.6 us: inline_step(): pl.pallas_call(inline_kernel, grid=(2,), in_specs=[pl.BlockSpec((DEVICES,...]
    all_to_all x4 -> x1, waiting for transfers between devices: 62.7 us -> 22.1 us  [exchange(): return lax.all_to_all(value, axes, 0, 0, tiled=True)]
  transfers between devices with their start and end apart: 5 -> 1, of which waited for: 4 -> 1; matrix products, arithmetic and copies ran while one was open for 3% -> 0% of each run, Pallas kernels for 0% -> 4%
where the time goes in v1:
time: 177 us; the launch traced here: 176 us
  blocking collectives  98.4 us (56%)
  Pallas kernels  43.2 us (24%)
  waiting for transfers between devices  22.1 us (12%)
  starting transfers between devices  8.46 us (5%)
  local copies, waits for them, and re-layouts  3.02 us (2%)
    all_to_all x3, blocking collectives, exchange(): return lax.all_to_all(value, axes, 0, 0, tiled=True)  98.4 us
    all_to_all x1, waiting for transfers between devices, exchange(): return lax.all_to_all(value, axes, 0, 0, tiled=True)  22.1 us
    pallas_call x1, Pallas kernels, inline_step(): pl.pallas_call(inline_kernel, grid=(2,), in_specs=[pl.BlockSpec((DEVICES,...  12.6 us
    pallas_call x1, Pallas kernels, cross_inverse(): pl.pallas_call(cross_inverse_kernel, grid=(2,), in_specs=[pl.BlockSpec((D...  9.08 us
    all_to_all x1, starting transfers between devices, exchange(): return lax.all_to_all(value, axes, 0, 0, tiled=True)  8.46 us
    pallas_call x1, Pallas kernels, phases(): pl.pallas_call(phase_kernel, grid=(2,), in_specs=[scalar, scalar, scalar,...  7.68 us
    pallas_call x1, Pallas kernels, cross_forward(): pl.pallas_call(cross_forward_kernel, grid=(2,), in_specs=[pl.BlockSpec((G...  7.16 us
    pallas_call x1, Pallas kernels, unpack(): pl.pallas_call(unpack_kernel, grid=(4,), in_specs=[pl.BlockSpec((GROUP, 3...  3.54 us
  transfers between devices with their start and end apart: 1, of which 1 were waited for; matrix products, arithmetic and copies ran while one was open for 0% of the time, Pallas kernels for 4%

profile of v1, /device:TPU:1, one launch (start us, length us, event | category | flops | bytes accessed | tf_op | source)
XLA Modules:
  0.0 176.4 jit_solution(10338536464068446101)
XLA Ops:
  0.6 3.1 %pack_fields.1 = bf16[16,288,256]{2,1,0:T(8,128)(2,1)} custom-call(bf16[2,2,16,32,256]{4,3,2,1,0:T(8,128)(2,1)} %bitcast.10, bf16[2,2,16,32,256]{4,3,2,1,0:T(8,128)(2,1)} %bitcast.11, s32[16,2,16,256]{3,2,1,0:T(8,128)} %bitcast.12), custom_call_target="tpu_custom_call" | custom-call | tf_op jit(solution)/shard_map/pack_fields/pallas_call | solution.py:404
  3.7 36.7 %all_to_all.20.lines.weight_one.weight_two = bf16[16,288,256]{2,1,0:T(8,128)(2,1)} all-to-all(bf16[16,288,256]{2,1,0:T(8,128)(2,1)} %pack_fields.1), channel_id=1, replica_groups=mesh['inl'=8,'xl'=16] {'xl'}, dimensions={0} | all-to-all | bytes 4718592 | tf_op jit(solution)/shard_map/all_to_all | solution.py:546
  40.3 7.2 %crossline_forward.1 = bf16[128,64,128]{2,1,0:T(8,128)(2,1)} custom-call(bf16[16,288,256]{2,1,0:T(8,128)(2,1)} %all_to_all.20.lines.weight_one.weight_two, f32[2,32,128]{2,1,0:T(8,128)} %constant.27.clone.twist, bf16[256,768]{1,0:T(8,128)(2,1)} %constant.28.clone.matrix), custom_call_target="tpu_custom_call" | custom-call | tf_op jit(solution)/shard_map/crossline_forward/pallas_call | solution.py:440
  47.5 8.5 %all-to-all-start.1 = ((bf16[128,64,128]{2,1,0:T(8,128)(2,1)}), bf16[128,64,128]{2,1,0:T(8,128)(2,1)S(1)}, u32[]{:S(2)}, u32[]{:S(2)}) async-start(bf16[128,64,128]{2,1,0:T(8,128)(2,1)} %crossline_forward.1), calls=%async_computation.1 | async-start | bytes 4194304 | tf_op jit(solution)/shard_map/all_to_all | solution.py:546
  56.0 0.7 pad_add_fusion.place
  56.6 7.7 %phase_table.1 = (f32[2,2,2,1024,128]{4,3,2,1,0:T(8,128)}, f32[128,128]{1,0:T(8,128)}) custom-call(s32[2]{0:T(128)} %pad_add_fusion.place, f32[2]{0:T(128)} %omega.1, f32[2]{0:T(128)} %slowness.1, s32[128,128]{1,0:T(8,128)} %wedge_map.1), custom_call_target="tpu_custom_call" | custom-call | tf_op jit(solution)/shard_map/phase_table/pallas_call | solution.py:421
  64.3 22.1 %all-to-all-done.1.lines = bf16[128,64,128]{2,1,0:T(8,128)(2,1)S(1)} async-done(((bf16[128,64,128]{2,1,0:T(8,128)(2,1)}), bf16[128,64,128]{2,1,0:T(8,128)(2,1)S(1)}, u32[]{:S(2)}, u32[]{:S(2)}) %all-to-all-start.1) | async-done | bytes 2097184 | tf_op jit(solution)/shard_map/all_to_all | solution.py:546
  86.4 0.0 copy-start
  86.4 1.4 copy-done
  87.8 12.6 %inline_step.1 = bf16[128,72,128]{2,1,0:T(8,128)(2,1)} custom-call(bf16[128,64,128]{2,1,0:T(8,128)(2,1)} %copy-done, f32[2,2,2,1024,128]{4,3,2,1,0:T(8,128)} %get-tuple-element.6.phase, f32[2,128,128]{2,1,0:T(8,128)} %constant.29.clone.twist, f32[2,128,128]{2,1,0:T(8,128)} %constant.30.clone.twist_inv, bf16[768,256]{1,0:T(8,128)(2,1)} %constant.31.clone.matrix, ...), custom_call_target="tpu_custom_call" | custom-call | tf_op jit(solution)/shard_map/inline_step/pallas_call | solution.py:458
  100.4 38.8 %all_to_all.21.lines.sums = bf16[128,72,128]{2,1,0:T(8,128)(2,1)} all-to-all(bf16[128,72,128]{2,1,0:T(8,128)(2,1)} %inline_step.1), channel_id=1, replica_groups=mesh['inl'=8,'xl'=16] {'inl','xl'}, dimensions={0} | all-to-all | bytes 4718592 | tf_op jit(solution)/shard_map/all_to_all | solution.py:546
  139.2 9.1 %crossline_inverse.1 = bf16[16,144,256]{2,1,0:T(8,128)(2,1)} custom-call(bf16[128,72,128]{2,1,0:T(8,128)(2,1)} %all_to_all.21.lines.sums, bf16[128,72,128]{2,1,0:T(8,128)(2,1)} %all_to_all.21.lines.sums, f32[128,128]{1,0:T(8,128)} %get-tuple-element.7.wedges, bf16[16,288,256]{2,1,0:T(8,128)(2,1)} %all_to_all.20.lines.weight_one.weight_two, ...), custom_call_target="tpu_custom_call" | custom-call | tf_op jit(solution)/shard_map/crossline_inverse/pallas_call | solution.py:491
  148.3 22.9 %all_to_all.22.block.coded = bf16[16,144,256]{2,1,0:T(8,128)(2,1)} all-to-all(bf16[16,144,256]{2,1,0:T(8,128)(2,1)} %crossline_inverse.1), channel_id=1, replica_groups=mesh['inl'=8,'xl'=16] {'xl'}, dimensions={0} | all-to-all | bytes 2359296 | tf_op jit(solution)/shard_map/all_to_all | solution.py:546
  171.2 3.5 %unpack_fields.1 = (bf16[2,2,16,32,256]{4,3,2,1,0:T(8,128)(2,1)}, f32[8,32,128]{2,1,0:T(8,128)}) custom-call(bf16[16,144,256]{2,1,0:T(8,128)(2,1)} %all_to_all.22.block.coded, bf16[16,144,256]{2,1,0:T(8,128)(2,1)} %all_to_all.22.block.coded), custom_call_target="tpu_custom_call" | custom-call | tf_op jit(solution)/shard_map/unpack_fields/pallas_call | solution.py:525
  174.8 1.6 copy.18
Async XLA Ops:
  47.5 38.9 %all-to-all-start.1 = ((bf16[128,64,128]{2,1,0:T(8,128)(2,1)}), bf16[128,64,128]{2,1,0:T(8,128)(2,1)S(1)}, u32[]{:S(2)}, u32[]{:S(2)}) async-start(bf16[128,64,128]{2,1,0:T(8,128)(2,1)} %crossline_forward.1), calls=%async_computation.1 | async-start | bytes 4194304 | tf_op jit(solution)/shard_map/all_to_all | solution.py:546
  86.4 1.4 copy-start

commit v2 on v0

v2 whole, which is shorter than its diff:
```python
import functools
import math

import jax
import jax.numpy as jnp
import ml_dtypes
import numpy as np
from jax import lax
from jax.experimental import pallas as pl
from jax.experimental.pallas import tpu as pltpu
from jax.sharding import Mesh
from jax.sharding import PartitionSpec as P

SIZE = 4096
DEVICES = 128
GROUP = 16
BF16 = jnp.bfloat16
F32 = jnp.float32
NAMES = ("x_hi", "z", "x_lo", "y", "core")
LINE = ("y", "x_lo", "core")
EVERY = ("x_lo", "x_hi", "z", "y", "core")
HALF = math.sqrt(0.5)


def line_rank(block):
    high, rest = divmod(block, 8)
    return rest // 2 * 4 + high * 2 + rest % 2


def every_rank(block):
    group, line = divmod(block, GROUP)
    return line // 2 % 2 * 64 + group * 8 + line // 4 * 2 + line % 2


def roots(rows, cols, length, sign):
    turn = np.outer(np.arange(rows), np.arange(cols)) % length
    return np.exp(sign * 2j * np.pi * turn / length)


def as_block(matrix):
    return np.block([[matrix.real, matrix.imag], [-matrix.imag, matrix.real]])


def two_parts(matrix):
    high = matrix.astype(np.float32).astype(ml_dtypes.bfloat16)
    low = (matrix - high.astype(np.float64)).astype(np.float32).astype(ml_dtypes.bfloat16)
    return high, low


def pair_table(values):
    return np.stack([values.real, values.imag]).astype(np.float32)


@functools.lru_cache(None)
def tables():
    out = {}
    high, low = two_parts(as_block(roots(128, 128, 128, -1)).T)
    out["cross_fwd"] = np.concatenate([high, high, low], axis=1)
    high, low = two_parts(as_block(roots(128, 128, 128, 1)) / SIZE)
    out["cross_inv"] = np.concatenate([high, low], axis=0)
    out["cross_tw_fwd"] = pair_table(roots(32, 128, SIZE, -1))
    out["cross_tw_inv"] = pair_table(roots(32, 128, SIZE, 1))
    for name, sign, scale in (("fwd", -1, 1.0), ("inv", 1, 1.0 / SIZE)):
        lanes = np.kron(np.eye(4), roots(32, 32, 32, sign))
        high, low = two_parts(as_block(lanes) * scale)
        out["inline_" + name] = np.concatenate([high, high, low], axis=0)
        out["inline_tw_" + name] = pair_table(np.tile(roots(128, 32, SIZE, sign), (1, 4)))
    return out


def add(x, y):
    return (x[0] + y[0], x[1] + y[1])


def sub(x, y):
    return (x[0] - y[0], x[1] - y[1])


def times(x, y):
    return (x[0] * y[0] - x[1] * y[1], x[0] * y[1] + x[1] * y[0])


def turn(x, numerator, length, sign):
    eighth = 8 * (numerator % length) * sign % (8 * length)
    if eighth % length:
        angle = sign * 2.0 * math.pi * (numerator % length) / length
        c, s = math.cos(angle), math.sin(angle)
        return (x[0] * c - x[1] * s, x[0] * s + x[1] * c)
    eighth = eighth // length
    r, i = x
    if eighth == 0:
        return x
    if eighth == 1:
        return ((r - i) * HALF, (r + i) * HALF)
    if eighth == 2:
        return (-i, r)
    if eighth == 3:
        return ((r + i) * -HALF, (r - i) * HALF)
    if eighth == 4:
        return (-r, -i)
    if eighth == 5:
        return ((i - r) * HALF, (r + i) * -HALF)
    if eighth == 6:
        return (i, -r)
    return ((r + i) * HALF, (i - r) * HALF)


def dft(x, sign):
    length = len(x)
    if length == 2:
        return [add(x[0], x[1]), sub(x[0], x[1])]
    if length == 4:
        t0, t1 = add(x[0], x[2]), sub(x[0], x[2])
        t2, t3 = add(x[1], x[3]), sub(x[1], x[3])
        r, i = t3
        if sign < 0:
            return [add(t0, t2), (t1[0] + i, t1[1] - r), sub(t0, t2), (t1[0] - i, t1[1] + r)]
        return [add(t0, t2), (t1[0] - i, t1[1] + r), sub(t0, t2), (t1[0] + i, t1[1] - r)]
    first = {8: 2, 16: 4, 32: 8}[length]
    second = length // first
    inner = [dft(x[low::second], sign) for low in range(second)]
    out = [None] * length
    for q in range(first):
        row = [turn(inner[low][q], low * q, length, sign) for low in range(second)]
        for p, value in enumerate(dft(row, sign)):
            out[q + first * p] = value
    return out


def split(value):
    high = value.astype(BF16)
    low = (value - high.astype(F32)).astype(BF16)
    return jnp.concatenate([high, low, high], axis=1)


def dot(x, y, dims=((1,), (0,))):
    return lax.dot_general(x, y, (dims, ((), ())), preferred_element_type=F32)


def pack_kernel(receiver, source, weight, out, raw, sems):
    copies = [pltpu.make_async_copy(weight, raw, sems.at[8])]
    for which, field in enumerate((receiver, source)):
        for part in range(2):
            for freq in range(2):
                rows = pl.ds(freq * 144 + which * 64 + part * 32, 32)
                sem = sems.at[which * 4 + part * 2 + freq]
                copies.append(
                    pltpu.make_async_copy(field.at[part, freq], out.at[:, rows, :], sem)
                )
    for copy in copies:
        copy.start()
    copies[0].wait()
    for freq in range(2):
        value = raw[:, freq]
        high = value >> 7
        code = 1.0 + (value & 127).astype(F32) * (1.0 / 128.0)
        for power in (1, 2, 4, 8, 16, 32):
            code = code * jnp.where((high & power) != 0, 2.0**power, 1.0)
        out[:, freq * 144 + 128 : freq * 144 + 144, :] = code.astype(BF16)
    for copy in copies[1:]:
        copy.wait()


def phase_kernel(omega, slowness, wedge_map, phase, wedges):
    x_hi, z, x_lo, y, core = (lax.axis_index(name) for name in NAMES)
    device = ((x_lo * 2 + x_hi) * 4 + z) * 8 + y * 2 + core
    step = 2.0 * math.pi / SIZE

    def signed(index):
        index = jnp.where(index >= SIZE // 2, index - SIZE, index)
        return step * index.astype(F32)

    def body(part, carry):
        row = part * 64 + lax.broadcasted_iota(jnp.int32, (64, 128), 0)
        lane = lax.broadcasted_iota(jnp.int32, (64, 128), 1)
        kx = signed((row >> 6) + 16 * ((row >> 3) & 7) + 128 * (lane & 31))
        ky = signed(device * 32 + (row & 7) + 8 * (lane >> 5))
        kx_sq = kx * kx
        ky_sq = ky * ky
        rows = pl.ds(pl.multiple_of(part * 64, 64), 64)
        for freq in range(2):
            for ref in range(2):
                number = omega[freq] * slowness[ref]
                quad = number * number - kx_sq - ky_sq
                root = jnp.sqrt(jnp.abs(quad))
                decay = jnp.exp(-root)
                inside = jnp.maximum(quad, 0.0)
                even = jnp.full_like(quad, 1.0 / math.factorial(22))
                odd = jnp.full_like(quad, 1.0 / math.factorial(23))
                for n in range(10, -1, -1):
                    even = 1.0 / math.factorial(2 * n) - inside * even
                    odd = 1.0 / math.factorial(2 * n + 1) - inside * odd
                phase[freq, ref, 0, rows, :] = jnp.where(quad >= 0, even, decay)
                phase[freq, ref, 1, rows, :] = jnp.where(quad >= 0, odd * root, 0.0)
        return carry

    lax.fori_loop(0, 16, body, 0)
    rows = wedge_map[pl.ds(y, 32, stride=4), :].astype(F32)
    wedges[...] = jnp.concatenate([rows] * 4, axis=0).T


def cross_forward_kernel(lines, twist, table, out, matrix, work, turned, ready, sem, sems):
    fetch = pltpu.make_async_copy(table, matrix, sem)
    fetch.start()

    def send(index):
        rows = pl.ds(pl.multiple_of(index * 16, 16), 16)
        return pltpu.make_async_copy(ready.at[index], out.at[:, rows, :], sems.at[index])

    def field(index, carry):
        start = index // 2 * 144 + index % 2 * 64
        for part in range(2):
            for low in range(4):
                values = []
                for high in range(8):
                    a = 4 * high + low
                    lanes = pl.ds((a % 2) * 128, 128)
                    pair = []
                    for side in range(2):
                        row = pl.multiple_of(start + side * 32 + part * 16, 16)
                        value = lines[line_rank(a // 2), pl.ds(row, 16), lanes]
                        pair.append(value.astype(F32))
                    values.append(tuple(pair))
                for q, value in enumerate(dft(values, -1)):
                    r, i = turn(value, low * q, 32, -1)
                    work[q, low, 0, part * 16 : part * 16 + 16, :] = r
                    work[q, low, 1, part * 16 : part * 16 + 16, :] = i

        @pl.when(index == 0)
        def _():
            fetch.wait()

        for pair in range(4):
            real, imag = [], []
            for q in (2 * pair, 2 * pair + 1):
                values = dft([(work[q, low, 0], work[q, low, 1]) for low in range(4)], -1)
                for p, value in enumerate(values):
                    k = q + 8 * p
                    r, i = times(value, (twist[0, k : k + 1, :], twist[1, k : k + 1, :]))
                    real.append(r)
                    imag.append(i)
            both = [jnp.concatenate(real, axis=0), jnp.concatenate(imag, axis=0)]
            value = dot(matrix[...], split(jnp.concatenate(both, axis=1)), ((1,), (1,)))
            for side in range(2):
                for half in range(2):
                    turned[pl.ds(side * 8 + pair * 2 + half, 128, stride=16), :] = value[
                        side * 128 : side * 128 + 128, half * 128 : half * 128 + 128
                    ]
        ready[index] = turned[...].reshape(128, 16, 128).astype(BF16)
        send(index).start()
        return carry

    lax.fori_loop(0, 4, field, 0)
    for index in range(4):
        send(index).wait()


def inline_kernel(
    lines,
    phase,
    twist,
    twist_inv,
    table,
    table_inv,
    out,
    held,
    matrix,
    matrix_inv,
    shifts,
    work,
    spec,
    term,
    sums,
    sems,
):
    fetch = pltpu.make_async_copy(table, matrix, sems.at[2])
    fetch_inv = pltpu.make_async_copy(table_inv, matrix_inv, sems.at[3])

    def fetch_phase(freq):
        return pltpu.make_async_copy(phase.at[freq], shifts.at[freq], sems.at[freq])

    def fetch_lines(index):
        rows = pl.ds(pl.multiple_of(index * 16, 16), 16)
        return pltpu.make_async_copy(lines.at[:, rows, :], held.at[index], sems.at[4 + index])

    order = [fetch_lines(0), fetch, fetch_lines(1), fetch_phase(0), fetch_inv]
    for copy in order + [fetch_lines(2), fetch_lines(3), fetch_phase(1)]:
        copy.start()
    term[...] = jnp.zeros_like(term)

    def one_freq(freq, carry):
        def forward(which, carry):
            index = freq * 2 + which
            fetch_lines(index).wait()
            for low in range(8):
                values = []
                for high in range(16):
                    value = held[index, every_rank(8 * high + low)].astype(F32)
                    values.append((value[0:8], value[8:16]))
                for q, value in enumerate(dft(values, -1)):
                    r, i = turn(value, low * q, 128, -1)
                    work[q * 8 + low, 0] = r
                    work[q * 8 + low, 1] = i

            @pl.when(index == 0)
            def _():
                fetch.wait()

            for part in range(4):
                real, imag = [], []
                for q in range(4 * part, 4 * part + 4):
                    values = [(work[q * 8 + low, 0], work[q * 8 + low, 1]) for low in range(8)]
                    for p, value in enumerate(dft(values, -1)):
                        k = q + 16 * p
                        r, i = times(value, (twist[0, k : k + 1, :], twist[1, k : k + 1, :]))
                        real.append(r)
                        imag.append(i)
                both = [jnp.concatenate(real, axis=0), jnp.concatenate(imag, axis=0)]
                block = slice(part * 256, part * 256 + 256)
                spec[which, block, :] = dot(split(jnp.concatenate(both, axis=1)), matrix[...])
            return carry

        lax.fori_loop(0, 2, forward, 0)
        for part in range(4):
            block = slice(part * 256, part * 256 + 256)
            both = spec[0, block, :] * spec[1, block, :]
            term[block, :] += both[:, 0:128] + both[:, 128:256]

        fetch_phase(freq).wait()

        @pl.when(freq == 0)
        def _():
            fetch_inv.wait()

        def inverse(ref, carry):
            for part in range(4):
                block = slice(part * 256, part * 256 + 256)
                value = (spec[0, block, 0:128], spec[0, block, 128:256])
                shift = (shifts[freq, ref, 0, block, :], shifts[freq, ref, 1, block, :])
                turned = jnp.concatenate(times(value, shift), axis=1)
                turned = dot(split(turned), matrix_inv[...])
                for j in range(4):
                    q = 4 * part + j
                    values = []
                    for p in range(8):
                        k = q + 16 * p
                        row = 64 * j + 8 * p
                        value = (turned[row : row + 8, 0:128], turned[row : row + 8, 128:256])
                        values.append(
                            times(value, (twist_inv[0, k : k + 1, :], twist_inv[1, k : k + 1, :]))
                        )
                    for low, value in enumerate(dft(values, 1)):
                        r, i = turn(value, low * q, 128, 1)
                        work[low * 16 + q, 0] = r
                        work[low * 16 + q, 1] = i
            rows = pl.ds(pl.multiple_of(freq * 32 + ref * 16, 16), 16)
            for low in range(8):
                values = [(work[low * 16 + q, 0], work[low * 16 + q, 1]) for q in range(16)]
                for high, value in enumerate(dft(values, 1)):
                    value = jnp.concatenate(value, axis=0).astype(BF16)
                    out[every_rank(8 * high + low), rows, :] = value
            return carry

        lax.fori_loop(0, 2, inverse, 0)
        return carry

    lax.fori_loop(0, 2, one_freq, 0)
    total = term[...].reshape(128, 8, 128).sum(axis=1)
    for q in range(16):
        sums[pl.ds(q, 8, stride=16), :] = total[8 * q : 8 * q + 8, :]
    total = sums[...]
    total = total + pltpu.roll(total, 64, 1)
    total = total + pltpu.roll(total, 32, 1)
    high = total.astype(BF16).astype(F32)
    rest = total - high
    middle = rest.astype(BF16).astype(F32)
    low = rest - middle
    place = lax.broadcasted_iota(jnp.int32, (128, 128), 1) >> 5
    value = jnp.where(place == 0, high, jnp.where(place == 1, middle, low))
    value = jnp.where(place == 3, 0.0, value).reshape(16, 8, 128).astype(BF16)
    for block in range(DEVICES):
        out[every_rank(block), 64:72, :] = value[block % GROUP]


def cross_inverse_kernel(
    lines, wedges, packed, twist, table, out, matrix, flat, work, kept, share, sem
):
    fetch = pltpu.make_async_copy(table, matrix, sem)
    fetch.start()
    for half in range(2):
        value = packed[:, half * 144 + 128 : half * 144 + 144, :].astype(F32)
        high = jnp.zeros_like(value)
        for power in (32, 16, 8, 4, 2, 1):
            over = value >= 2.0**power
            value = jnp.where(over, value * 2.0**-power, value)
            high = jnp.where(over, high + float(power), high)
        share[:, half * 16 : half * 16 + 16, :] = (high + (value - 1.0)) * (1.0 / 32.0)

    def gather(d, totals):
        value = lines[d, 64:72, :].astype(F32)
        where = wedges[pl.ds(d, 1), :]
        return tuple(
            total + jnp.where(where == float(w), value, 0.0) for w, total in enumerate(totals)
        )

    zero = jnp.zeros((8, 128), F32)
    totals = lax.fori_loop(0, 128, gather, (zero,) * 8, unroll=8)
    highs, lows = [], []
    for total in totals:
        total = total + pltpu.roll(total, 64, 1)
        total = total + pltpu.roll(total, 32, 1)
        total = total * (1.0 / (SIZE * SIZE * math.sqrt(SIZE)))
        highs.append(total.astype(BF16).astype(F32))
        lows.append(total - highs[-1])
    place = lax.broadcasted_iota(jnp.int32, (8, 128), 1) >> 5
    for half in range(2):
        rows = []
        for first in (half * 2, half * 2 + 4):
            even = jnp.where(place == 0, highs[first], lows[first])
            odd = jnp.where(place == 2, highs[first + 1], lows[first + 1])
            rows.append(jnp.where(place < 2, even, odd))
        value = jnp.concatenate(rows, axis=0).astype(BF16)
        for group in range(16):
            out[group, 128:144, half * 128 : half * 128 + 128] = value

    fetch.wait()

    def one_freq(freq, carry):
        for ref in range(2):
            rows = pl.ds(pl.multiple_of(freq * 32 + ref * 16, 16), 16)
            flat[...] = lines[:, rows, :].astype(F32).reshape(2048, 128)
            for g in range(8):
                pair = [flat[pl.ds(side * 8 + g, 128, stride=16), :] for side in range(2)]
                value = jnp.concatenate([x.T for x in pair], axis=1).astype(BF16)
                value = dot(jnp.concatenate([value, value], axis=1), matrix[...])
                values = []
                for p in range(4):
                    k = g + 8 * p
                    block = value[32 * p : 32 * p + 32, :]
                    block = (block[:, 0:128], block[:, 128:256])
                    values.append(times(block, (twist[0, k : k + 1, :], twist[1, k : k + 1, :])))
                for low, value in enumerate(dft(values, 1)):
                    r, i = turn(value, low * g, 32, 1)
                    work[low, g, 0] = r
                    work[low, g, 1] = i

            def rows16(part, carry):
                start = pl.multiple_of(part * 16, 16)
                rows = pl.ds(start, 16)
                for low in range(4):
                    values = [(work[low, g, 0, rows, :], work[low, g, 1, rows, :]) for g in range(8)]
                    for high, value in enumerate(dft(values, 1)):
                        a = 4 * high + low
                        lanes = slice((a % 2) * 128, (a % 2) * 128 + 128)
                        for side in range(2):
                            rounded = value[side].astype(BF16)
                            if ref == 0:
                                kept[a, side, rows, :] = rounded
                            else:
                                s = share[line_rank(a // 2), rows, lanes]
                                first = kept[a, side, rows, :].astype(F32)
                                mixed = first * s + rounded.astype(F32) * (1.0 - s)
                                row = pl.multiple_of(freq * 64 + side * 32 + part * 16, 16)
                                out[line_rank(a // 2), pl.ds(row, 16), lanes] = mixed.astype(BF16)
                return carry

            lax.fori_loop(0, 2, rows16, 0)
        return carry

    lax.fori_loop(0, 2, one_freq, 0)


def unpack_kernel(home, out, angles, turned, sems):
    copies = []
    for part in range(4):
        block = home.at[:, pl.ds(part * 32, 32), :]
        copies.append(pltpu.make_async_copy(block, out.at[part % 2, part // 2], sems.at[part]))
    for copy in copies:
        copy.start()
    value = home[:, 128:144, :].astype(F32)
    for half in range(2):
        for top in range(2):
            part = value[:, top * 8 : top * 8 + 8, half * 128 : half * 128 + 128]
            flipped = part.reshape(128, 128).T
            w = top * 4 + half * 2
            turned[pl.ds(w, 32, stride=8), :] = flipped[0:32] + flipped[32:64]
            turned[pl.ds(w + 1, 32, stride=8), :] = flipped[64:96] + flipped[96:128]
    for k in range(32):
        angles[:, k * 128 : k * 128 + 128] = turned[k * 8 : k * 8 + 8, :]
    for copy in copies:
        copy.wait()


FAR = pl.BlockSpec(memory_space=pltpu.HBM)
LOCAL = pl.BlockSpec(memory_space=pltpu.VMEM)
SCALAR = pl.BlockSpec(memory_space=pltpu.SMEM)


def near(value):
    return pltpu.with_memory_space_constraint(value, pltpu.VMEM)


def far(value):
    return pltpu.with_memory_space_constraint(value, pltpu.HBM)


def call(kernel, name, outs, out_specs, in_specs, scratch, mebibytes, args):
    return pl.pallas_call(
        kernel,
        in_specs=in_specs,
        out_specs=out_specs,
        out_shape=outs,
        scratch_shapes=scratch,
        compiler_params=pltpu.CompilerParams(vmem_limit_bytes=mebibytes * 2**20),
        name=name,
    )(*args)


def pack(receiver, source, weight):
    args = (
        far(receiver.reshape(2, 2, GROUP, 32, 256)),
        far(source.reshape(2, 2, GROUP, 32, 256)),
        far(weight.reshape(GROUP, 2, 16, 256)),
    )
    scratch = [pltpu.VMEM((GROUP, 2, 16, 256), jnp.int32), pltpu.SemaphoreType.DMA((9,))]
    outs = pltpu.VMEM((GROUP, 288, 256), BF16)
    return call(pack_kernel, "pack_fields", outs, LOCAL, [FAR] * 3, scratch, 12, args)


def phases(omega, slowness, wedge_map):
    outs = [
        jax.ShapeDtypeStruct((2, 2, 2, 1024, 128), F32),
        jax.ShapeDtypeStruct((128, 128), F32),
    ]
    args = (omega, slowness, wedge_map)
    specs = [SCALAR] * 2 + [LOCAL]
    return call(phase_kernel, "phase_table", outs, [LOCAL] * 2, specs, [], 12, args)


def cross_forward(packed):
    t = tables()
    args = [near(packed), near(jnp.asarray(t["cross_tw_fwd"])), jnp.asarray(t["cross_fwd"])]
    outs = pltpu.HBM((DEVICES, 64, 128), BF16)
    scratch = [
        pltpu.VMEM((256, 768), BF16),
        pltpu.VMEM((8, 4, 2, 32, 128), F32),
        pltpu.VMEM((2048, 128), F32),
        pltpu.VMEM((4, DEVICES, 16, 128), BF16),
        pltpu.SemaphoreType.DMA,
        pltpu.SemaphoreType.DMA((4,)),
    ]
    return call(
        cross_forward_kernel, "crossline_forward", outs, FAR, [LOCAL] * 2 + [FAR], scratch, 16, args
    )


def inline_step(lines, phase):
    t = tables()
    args = [far(lines), far(phase)]
    args += [near(jnp.asarray(t[n])) for n in ("inline_tw_fwd", "inline_tw_inv")]
    args += [jnp.asarray(t[n]) for n in ("inline_fwd", "inline_inv")]
    outs = pltpu.VMEM((DEVICES, 72, 128), BF16)
    scratch = [
        pltpu.VMEM((4, DEVICES, 16, 128), BF16),
        pltpu.VMEM((768, 256), BF16),
        pltpu.VMEM((768, 256), BF16),
        pltpu.VMEM((2, 2, 2, 1024, 128), F32),
        pltpu.VMEM((128, 2, 8, 128), F32),
        pltpu.VMEM((2, 1024, 256), F32),
        pltpu.VMEM((1024, 128), F32),
        pltpu.VMEM((128, 128), F32),
        pltpu.SemaphoreType.DMA((8,)),
    ]
    specs = [FAR, FAR, LOCAL, LOCAL, FAR, FAR]
    return call(inline_kernel, "inline_step", outs, LOCAL, specs, scratch, 20, args)


def cross_inverse(partial, wedges, packed):
    t = tables()
    args = [near(partial), near(wedges), near(packed), near(jnp.asarray(t["cross_tw_inv"]))]
    args.append(jnp.asarray(t["cross_inv"]))
    outs = pltpu.VMEM((GROUP, 144, 256), BF16)
    scratch = [
        pltpu.VMEM((512, 256), BF16),
        pltpu.VMEM((2048, 128), F32),
        pltpu.VMEM((4, 8, 2, 32, 128), F32),
        pltpu.VMEM((32, 2, 32, 128), BF16),
        pltpu.VMEM((GROUP, 32, 256), F32),
        pltpu.SemaphoreType.DMA,
    ]
    return call(
        cross_inverse_kernel, "crossline_inverse", outs, LOCAL, [LOCAL] * 4 + [FAR], scratch, 16, args
    )


def unpack(home):
    outs = [
        jax.ShapeDtypeStruct((2, 2, GROUP, 32, 256), BF16),
        jax.ShapeDtypeStruct((8, SIZE), F32),
    ]
    scratch = [pltpu.VMEM((256, 128), F32), pltpu.SemaphoreType.DMA((4,))]
    specs = [FAR, LOCAL]
    return call(unpack_kernel, "unpack_fields", outs, specs, [LOCAL], scratch, 12, [near(home)])


def exchange(value, axes):
    return lax.all_to_all(value, axes, 0, 0, tiled=True)


def per_device(receiver, source, weight, omega, slowness, wedge_map):
    packed = exchange(pack(receiver, source, weight), LINE)
    phase, wedges = phases(omega, slowness, wedge_map)
    lines = exchange(cross_forward(packed), EVERY)
    partial = exchange(inline_step(lines, phase), EVERY)
    home = exchange(cross_inverse(partial, wedges, packed), LINE)
    mixed, angles = unpack(home)
    return (mixed.reshape(2, 2, 512, 256), angles)


def solution(mesh):
    fine = Mesh(mesh.devices.reshape(2, 4, 2, 4, 2), NAMES)
    rows, columns = ("x_hi", "z"), ("x_lo", "y", "core")
    return jax.shard_map(
        per_device,
        mesh=fine,
        in_specs=(
            P(None, None, rows, columns),
            P(None, None, rows, columns),
            P(rows, columns),
            P(),
            P(),
            P(),
        ),
        out_specs=(P(None, None, rows, columns), P()),
        check_vma=False,
    )
```

time: 908 us -> 159 us (0.18)
  matrix products: 346 us -> 0 us
  local copies, waits for them, and re-layouts: 273 us -> 2.03 us
  waiting for transfers between devices: 211 us -> 22.9 us
  blocking collectives: 0 us -> 94.6 us
  Pallas kernels: 0 us -> 29.9 us
  other arithmetic: 29.9 us -> 0 us
  starting transfers between devices: 27.8 us -> 8.81 us
  between operations: 15 us -> 0.81 us
    dot_general x32 -> x0, matrix products: 346 us -> none  [contract(): return jnp.einsum(form, values, matrix, precision=lax.Precision.HIGHEST)]
    psum x1 -> x0, waiting for transfers between devices: 148 us -> none  [per_device(): summed = lax.psum(contrib, ('inl', 'xl'))]
    all_to_all x0 -> x3, blocking collectives: none -> 94.6 us  [exchange(): return lax.all_to_all(value, axes, 0, 0, tiled=True)]
    unnamed x32 -> x24, local copies, waits for them, and re-layouts: 72.9 us -> 2.03 us
    all_to_all x6 -> x0, local copies, waits for them, and re-layouts: 68.8 us -> none  [the longest x1 23 us: to_lines(): lax.all_to_all(packed, ('inl', 'xl'), split_axis=3, concat_axis=4, tiled=...]
    another operation x5 -> x0, local copies, waits for them, and re-layouts: 49.1 us -> none  [the longest x2 16.2 us: one_step(): spec = to_spectrum(jnp.stack([yr, yi], axis=1).astype(jnp.bfloat16))]
    all_to_all x4 -> x1, waiting for transfers between devices: 62.7 us -> 22.9 us  [exchange(): return lax.all_to_all(value, axes, 0, 0, tiled=True)]
    pallas_call x0 -> x6, Pallas kernels: none -> 29.9 us  [call(): pl.pallas_call(kernel, in_specs=in_specs, out_specs=out_specs, out_shape=...]
  transfers between devices with their start and end apart: 5 -> 1, of which waited for: 4 -> 1; matrix products, arithmetic and copies ran while one was open for 3% -> 0% of each run, Pallas kernels for 0% -> 3%
where the time goes in v2:
time: 159 us
  blocking collectives  94.6 us (59%)
  Pallas kernels  29.9 us (19%)
  waiting for transfers between devices  22.9 us (14%)
  starting transfers between devices  8.81 us (6%)
  local copies, waits for them, and re-layouts  2.03 us (1%)
    all_to_all x3, blocking collectives, exchange(): return lax.all_to_all(value, axes, 0, 0, tiled=True)  94.6 us
    pallas_call x6, Pallas kernels, call(): pl.pallas_call(kernel, in_specs=in_specs, out_specs=out_specs, out_shape=...  29.9 us
    all_to_all x1, waiting for transfers between devices, exchange(): return lax.all_to_all(value, axes, 0, 0, tiled=True)  22.9 us
    all_to_all x1, starting transfers between devices, exchange(): return lax.all_to_all(value, axes, 0, 0, tiled=True)  8.81 us
  transfers between devices with their start and end apart: 1, of which 1 were waited for; matrix products, arithmetic and copies ran while one was open for 0% of the time, Pallas kernels for 3%

profile of v2, /device:TPU:1, one launch (start us, length us, event | category | flops | bytes accessed | tf_op | source)
XLA Modules:
  0.0 159.0 jit_solution(214090462820857578)
XLA Ops:
  0.6 1.7 %pack_fields.1 = bf16[16,288,256]{2,1,0:T(8,128)(2,1)S(1)} custom-call(bf16[2,2,16,32,256]{4,3,2,1,0:T(8,128)(2,1)} %bitcast.4, bf16[2,2,16,32,256]{4,3,2,1,0:T(8,128)(2,1)} %bitcast.5, s32[16,2,16,256]{3,2,1,0:T(8,128)} %bitcast.6), custom_call_target="tpu_custom_call" | custom-call | tf_op jit(solution)/shard_map/pack_fields/pallas_call | solution.py:508
  2.4 0.0 copy-start.3
  2.4 0.0 copy-start.9
  2.4 36.5 %all_to_all.20.lines.packed = bf16[16,288,256]{2,1,0:T(8,128)(2,1)S(1)} all-to-all(bf16[16,288,256]{2,1,0:T(8,128)(2,1)S(1)} %pack_fields.1), channel_id=1, replica_groups=mesh['x_hi'=2,'z'=4,'x_lo'=2,'y'=4,'core'=2] {'y','x_lo','core'}, dimensions={0} | all-to-all | bytes 4718592 | tf_op jit(solution)/shard_map/all_to_all | solution.py:607
  38.9 0.0 copy-done.3
  38.9 0.0 copy-done.9
  38.9 5.5 %crossline_forward.1 = bf16[128,64,128]{2,1,0:T(8,128)(2,1)} custom-call(bf16[16,288,256]{2,1,0:T(8,128)(2,1)S(1)} %all_to_all.20.lines.packed, f32[2,32,128]{2,1,0:T(8,128)S(1)} %copy-done.9, bf16[256,768]{1,0:T(8,128)(2,1)S(1)} %copy-done.3), custom_call_target="tpu_custom_call" | custom-call | tf_op jit(solution)/shard_map/crossline_forward/pallas_call | solution.py:508
  44.4 0.0 copy-start.7
  44.4 0.0 copy-start.10
  44.5 0.0 copy-start.11
  44.5 0.0 copy-start.1
  44.5 0.0 copy-start.2
  44.5 0.0 copy-start.5
  44.5 0.0 copy-start.6
  44.5 8.8 %all-to-all-start.1 = ((bf16[128,64,128]{2,1,0:T(8,128)(2,1)}), bf16[128,64,128]{2,1,0:T(8,128)(2,1)}, u32[]{:S(2)}, u32[]{:S(2)}) async-start(bf16[128,64,128]{2,1,0:T(8,128)(2,1)} %crossline_forward.1), calls=%async_computation.1 | async-start | bytes 4194304 | tf_op jit(solution)/shard_map/all_to_all | solution.py:607
  53.3 0.0 copy-done.7
  53.3 0.0 copy-done.10
  53.4 0.0 copy-done.11
  53.4 5.5 %phase_table.1 = (f32[2,2,2,1024,128]{4,3,2,1,0:T(8,128)S(1)}, f32[128,128]{1,0:T(8,128)S(1)}) custom-call(f32[2]{0:T(128)S(1)} %copy-done.10, f32[2]{0:T(128)S(1)} %copy-done.11, s32[128,128]{1,0:T(8,128)S(1)} %copy-done.7), custom_call_target="tpu_custom_call" | custom-call | tf_op jit(solution)/shard_map/phase_table/pallas_call | solution.py:508
  58.9 0.0 copy-start
  58.9 1.9 %copy-done = f32[2,2,2,1024,128]{4,3,2,1,0:T(8,128)} copy-done((f32[2,2,2,1024,128]{4,3,2,1,0:T(8,128)}, f32[2,2,2,1024,128]{4,3,2,1,0:T(8,128)S(1)}, u32[]{:S(2)}) %copy-start) | copy-done | bytes 4194328
  60.8 22.9 %all-to-all-done.1.lines = bf16[128,64,128]{2,1,0:T(8,128)(2,1)} async-done(((bf16[128,64,128]{2,1,0:T(8,128)(2,1)}), bf16[128,64,128]{2,1,0:T(8,128)(2,1)}, u32[]{:S(2)}, u32[]{:S(2)}) %all-to-all-start.1) | async-done | bytes 2097184 | tf_op jit(solution)/shard_map/all_to_all | solution.py:607
  83.7 0.0 copy-done.1
  83.7 0.0 copy-done.2
  83.7 0.0 copy-done.5
  83.7 0.0 copy-done.6
  83.7 9.8 %inline_step.1 = bf16[128,72,128]{2,1,0:T(8,128)(2,1)S(1)} custom-call(bf16[128,64,128]{2,1,0:T(8,128)(2,1)} %all-to-all-done.1.lines, f32[2,2,2,1024,128]{4,3,2,1,0:T(8,128)} %copy-done, f32[2,128,128]{2,1,0:T(8,128)S(1)} %copy-done.6, f32[2,128,128]{2,1,0:T(8,128)S(1)} %copy-done.5, bf16[768,256]{1,0:T(8,128)(2,1)S(1)} %copy-done.2, ...), custom_call_target="tpu_custom_call" | custom-call | tf_op jit(solution)/shard_map/inline_step/pallas_call | solution.py:508
  93.5 0.0 copy-start.4
  93.5 0.0 copy-start.8
  93.6 37.5 %all_to_all.21.lines = bf16[128,72,128]{2,1,0:T(8,128)(2,1)S(1)} all-to-all(bf16[128,72,128]{2,1,0:T(8,128)(2,1)S(1)} %inline_step.1), channel_id=1, replica_groups=mesh['x_hi'=2,'z'=4,'x_lo'=2,'y'=4,'core'=2] {'x_lo','x_hi','z','y','core'}, dimensions={0} | all-to-all | bytes 4718592 | tf_op jit(solution)/shard_map/all_to_all | solution.py:607
  131.1 0.0 copy-done.4
  131.1 0.0 copy-done.8
  131.1 5.7 %crossline_inverse.1 = bf16[16,144,256]{2,1,0:T(8,128)(2,1)S(1)} custom-call(bf16[128,72,128]{2,1,0:T(8,128)(2,1)S(1)} %all_to_all.21.lines, f32[128,128]{1,0:T(8,128)S(1)} %get-tuple-element.7.wedges, bf16[16,288,256]{2,1,0:T(8,128)(2,1)S(1)} %all_to_all.20.lines.packed, f32[2,32,128]{2,1,0:T(8,128)S(1)} %copy-done.8, bf16[512,256]{1,0:T(8,128)(2,1)S(1)} %copy-done.4), custom_call_target="tpu_custom_call" | custom-call | tf_op jit(solution)/shard_map/crossline_inverse/pallas_call | solution.py:508
  136.7 20.6 %all_to_all.22.home = bf16[16,144,256]{2,1,0:T(8,128)(2,1)S(1)} all-to-all(bf16[16,144,256]{2,1,0:T(8,128)(2,1)S(1)} %crossline_inverse.1), channel_id=1, replica_groups=mesh['x_hi'=2,'z'=4,'x_lo'=2,'y'=4,'core'=2] {'y','x_lo','core'}, dimensions={0} | all-to-all | bytes 2359296 | tf_op jit(solution)/shard_map/all_to_all | solution.py:607
  157.3 1.7 %unpack_fields.1 = (bf16[2,2,16,32,256]{4,3,2,1,0:T(8,128)(2,1)}, f32[8,4096]{1,0:T(8,128)}) custom-call(bf16[16,144,256]{2,1,0:T(8,128)(2,1)S(1)} %all_to_all.22.home), custom_call_target="tpu_custom_call" | custom-call | tf_op jit(solution)/shard_map/unpack_fields/pallas_call | solution.py:508
Async XLA Ops:
  2.4 36.5 %copy-start.3 = (bf16[256,768]{1,0:T(8,128)(2,1)S(1)}, bf16[256,768]{1,0:T(8,128)(2,1)}, u32[]{:S(2)}) copy-start(bf16[256,768]{1,0:T(8,128)(2,1)} %constant.17.clone.table) | copy-start | bytes 1179652
  2.4 36.5 %copy-start.9 = (f32[2,32,128]{2,1,0:T(8,128)S(1)}, f32[2,32,128]{2,1,0:T(8,128)}, u32[]{:S(2)}) copy-start(f32[2,32,128]{2,1,0:T(8,128)} %constant.16.clone.twist) | copy-start | bytes 98308
  44.4 8.9 %copy-start.7 = (s32[128,128]{1,0:T(8,128)S(1)}, s32[128,128]{1,0:T(8,128)}, u32[]{:S(2)}) copy-start(s32[128,128]{1,0:T(8,128)} %wedge_map.1) | copy-start | bytes 196612
  44.4 8.9 %copy-start.10 = (f32[2]{0:T(128)S(1)}, f32[2]{0:T(128)}, u32[]{:S(2)}) copy-start(f32[2]{0:T(128)} %omega.1) | copy-start | bytes 28
  44.5 8.9 %copy-start.11 = (f32[2]{0:T(128)S(1)}, f32[2]{0:T(128)}, u32[]{:S(2)}) copy-start(f32[2]{0:T(128)} %slowness.1) | copy-start | bytes 28
  44.5 39.2 %copy-start.1 = (bf16[768,256]{1,0:T(8,128)(2,1)S(1)}, bf16[768,256]{1,0:T(8,128)(2,1)}, u32[]{:S(2)}) copy-start(bf16[768,256]{1,0:T(8,128)(2,1)} %constant.21.clone.table_inv) | copy-start | bytes 1179652
  44.5 39.2 %copy-start.2 = (bf16[768,256]{1,0:T(8,128)(2,1)S(1)}, bf16[768,256]{1,0:T(8,128)(2,1)}, u32[]{:S(2)}) copy-start(bf16[768,256]{1,0:T(8,128)(2,1)} %constant.20.clone.table) | copy-start | bytes 1179652
  44.5 39.2 %copy-start.5 = (f32[2,128,128]{2,1,0:T(8,128)S(1)}, f32[2,128,128]{2,1,0:T(8,128)}, u32[]{:S(2)}) copy-start(f32[2,128,128]{2,1,0:T(8,128)} %constant.19.clone.twist_inv) | copy-start | bytes 393220
  44.5 39.2 %copy-start.6 = (f32[2,128,128]{2,1,0:T(8,128)S(1)}, f32[2,128,128]{2,1,0:T(8,128)}, u32[]{:S(2)}) copy-start(f32[2,128,128]{2,1,0:T(8,128)} %constant.18.clone.twist) | copy-start | bytes 393220
  44.5 39.2 %all-to-all-start.1 = ((bf16[128,64,128]{2,1,0:T(8,128)(2,1)}), bf16[128,64,128]{2,1,0:T(8,128)(2,1)}, u32[]{:S(2)}, u32[]{:S(2)}) async-start(bf16[128,64,128]{2,1,0:T(8,128)(2,1)} %crossline_forward.1), calls=%async_computation.1 | async-start | bytes 4194304 | tf_op jit(solution)/shard_map/all_to_all | solution.py:607
  58.9 2.0 %copy-start = (f32[2,2,2,1024,128]{4,3,2,1,0:T(8,128)}, f32[2,2,2,1024,128]{4,3,2,1,0:T(8,128)S(1)}, u32[]{:S(2)}) copy-start(f32[2,2,2,1024,128]{4,3,2,1,0:T(8,128)S(1)} %get-tuple-element.6.phase) | copy-start | bytes 12582916
  93.5 37.5 %copy-start.4 = (bf16[512,256]{1,0:T(8,128)(2,1)S(1)}, bf16[512,256]{1,0:T(8,128)(2,1)}, u32[]{:S(2)}) copy-start(bf16[512,256]{1,0:T(8,128)(2,1)} %constant.23.clone.table) | copy-start | bytes 786436
  93.5 37.5 %copy-start.8 = (f32[2,32,128]{2,1,0:T(8,128)S(1)}, f32[2,32,128]{2,1,0:T(8,128)}, u32[]{:S(2)}) copy-start(f32[2,32,128]{2,1,0:T(8,128)} %constant.22.clone.twist) | copy-start | bytes 98308

commit v3 on v2

--- a/solution.py
+++ b/solution.py
@@ -47,6 +47,19 @@
     return high, low
 
 
+def gains(length):
+    turns = np.exp(2j * np.pi * np.arange(length) / length)
+    factors = np.exp2(np.arange(4096) / 4096)
+    best = []
+    for row in range(length):
+        entries = turns[row * np.arange(length) % length]
+        entries = np.concatenate([entries.real, entries.imag])
+        scaled = factors[:, None] * entries
+        rounded = scaled.astype(np.float32).astype(ml_dtypes.bfloat16).astype(np.float64)
+        best.append(factors[(np.square(rounded - scaled).sum(axis=1) / factors**2).argmin()])
+    return np.array(best)
+
+
 def pair_table(values):
     return np.stack([values.real, values.imag]).astype(np.float32)
 
@@ -60,11 +73,14 @@
     out["cross_inv"] = np.concatenate([high, low], axis=0)
     out["cross_tw_fwd"] = pair_table(roots(32, 128, SIZE, -1))
     out["cross_tw_inv"] = pair_table(roots(32, 128, SIZE, 1))
+    gain = np.tile(gains(32), 4)
+    out["phase_scale"] = (1.0 / gain).astype(np.float32)[None, :]
     for name, sign, scale in (("fwd", -1, 1.0), ("inv", 1, 1.0 / SIZE)):
         lanes = np.kron(np.eye(4), roots(32, 32, 32, sign))
-        high, low = two_parts(as_block(lanes) * scale)
-        out["inline_" + name] = np.concatenate([high, high, low], axis=0)
-        out["inline_tw_" + name] = pair_table(np.tile(roots(128, 32, SIZE, sign), (1, 4)))
+        high, _ = two_parts(np.tile(gain, 2)[:, None] * as_block(lanes) * scale)
+        out["inline_" + name] = high
+    out["inline_tw_fwd"] = pair_table(np.tile(roots(128, 32, SIZE, -1), (1, 4)) / gain)
+    out["inline_tw_inv"] = pair_table(np.tile(roots(128, 32, SIZE, 1), (1, 4)))
     return out
 
 
@@ -129,12 +145,16 @@
 
 def split(value):
     high = value.astype(BF16)
-    low = (value - high.astype(F32)).astype(BF16)
-    return jnp.concatenate([high, low, high], axis=1)
+    return high, (value - high.astype(F32)).astype(BF16)
 
 
 def dot(x, y, dims=((1,), (0,))):
     return lax.dot_general(x, y, (dims, ((), ())), preferred_element_type=F32)
+
+
+def dot2(value, matrix):
+    high, low = split(value)
+    return dot(high, matrix[...]) + dot(low, matrix[...])
 
 
 def pack_kernel(receiver, source, weight, out, raw, sems):
@@ -161,7 +181,7 @@
         copy.wait()
 
 
-def phase_kernel(omega, slowness, wedge_map, phase, wedges):
+def prepare_kernel(omega, slowness, scale, wedge_map, packed, phase, wedges, share):
     x_hi, z, x_lo, y, core = (lax.axis_index(name) for name in NAMES)
     device = ((x_lo * 2 + x_hi) * 4 + z) * 8 + y * 2 + core
     step = 2.0 * math.pi / SIZE
@@ -190,13 +210,26 @@
                 for n in range(10, -1, -1):
                     even = 1.0 / math.factorial(2 * n) - inside * even
                     odd = 1.0 / math.factorial(2 * n + 1) - inside * odd
-                phase[freq, ref, 0, rows, :] = jnp.where(quad >= 0, even, decay)
-                phase[freq, ref, 1, rows, :] = jnp.where(quad >= 0, odd * root, 0.0)
+                real = jnp.where(quad >= 0, even, decay)
+                imag = jnp.where(quad >= 0, odd * root, 0.0)
+                phase[freq, ref, 0, rows, :] = real * scale[...]
+                phase[freq, ref, 1, rows, :] = imag * scale[...]
         return carry
 
     lax.fori_loop(0, 16, body, 0)
     rows = wedge_map[pl.ds(y, 32, stride=4), :].astype(F32)
     wedges[...] = jnp.concatenate([rows] * 4, axis=0).T
+    for half in range(2):
+        for a in range(32):
+            lanes = slice((a % 2) * 128, (a % 2) * 128 + 128)
+            block = packed[line_rank(a // 2), half * 144 + 128 : half * 144 + 144, lanes]
+            value = block.astype(F32)
+            high = jnp.zeros_like(value)
+            for power in (32, 16, 8, 4, 2, 1):
+                over = value >= 2.0**power
+                value = jnp.where(over, value * 2.0**-power, value)
+                high = jnp.where(over, high + float(power), high)
+            share[a, half * 16 : half * 16 + 16, :] = (high + (value - 1.0)) * (1.0 / 32.0)
 
 
 def cross_forward_kernel(lines, twist, table, out, matrix, work, turned, ready, sem, sems):
@@ -240,17 +273,19 @@
                     real.append(r)
                     imag.append(i)
             both = [jnp.concatenate(real, axis=0), jnp.concatenate(imag, axis=0)]
-            value = dot(matrix[...], split(jnp.concatenate(both, axis=1)), ((1,), (1,)))
+            high, low = split(jnp.concatenate(both, axis=1))
+            parts = jnp.concatenate([high, low, high], axis=1)
+            value = dot(matrix[...], parts, ((1,), (1,)))
             for side in range(2):
                 for half in range(2):
-                    turned[pl.ds(side * 8 + pair * 2 + half, 128, stride=16), :] = value[
+                    turned[pl.ds(side * 8 + pair * 2 + half, 128, stride=24), :] = value[
                         side * 128 : side * 128 + 128, half * 128 : half * 128 + 128
                     ]
-        ready[index] = turned[...].reshape(128, 16, 128).astype(BF16)
+        ready[index] = turned[...].reshape(128, 24, 128)[:, :16].astype(BF16)
         send(index).start()
         return carry
 
-    lax.fori_loop(0, 4, field, 0)
+    lax.fori_loop(0, 4, field, 0, unroll=True)
     for index in range(4):
         send(index).wait()
 
@@ -317,10 +352,10 @@
                         imag.append(i)
                 both = [jnp.concatenate(real, axis=0), jnp.concatenate(imag, axis=0)]
                 block = slice(part * 256, part * 256 + 256)
-                spec[which, block, :] = dot(split(jnp.concatenate(both, axis=1)), matrix[...])
+                spec[which, block, :] = dot2(jnp.concatenate(both, axis=1), matrix)
             return carry
 
-        lax.fori_loop(0, 2, forward, 0)
+        lax.fori_loop(0, 2, forward, 0, unroll=True)
         for part in range(4):
             block = slice(part * 256, part * 256 + 256)
             both = spec[0, block, :] * spec[1, block, :]
@@ -338,7 +373,7 @@
                 value = (spec[0, block, 0:128], spec[0, block, 128:256])
                 shift = (shifts[freq, ref, 0, block, :], shifts[freq, ref, 1, block, :])
                 turned = jnp.concatenate(times(value, shift), axis=1)
-                turned = dot(split(turned), matrix_inv[...])
+                turned = dot2(turned, matrix_inv)
                 for j in range(4):
                     q = 4 * part + j
                     values = []
@@ -361,7 +396,7 @@
                     out[every_rank(8 * high + low), rows, :] = value
             return carry
 
-        lax.fori_loop(0, 2, inverse, 0)
+        lax.fori_loop(0, 2, inverse, 0, unroll=True)
         return carry
 
     lax.fori_loop(0, 2, one_freq, 0)
@@ -383,19 +418,12 @@
 
 
 def cross_inverse_kernel(
-    lines, wedges, packed, twist, table, out, matrix, flat, work, kept, share, sem
+    lines, wedges, shares, twist, table, out, matrix, flat, work, kept, share, sems
 ):
-    fetch = pltpu.make_async_copy(table, matrix, sem)
+    fetch = pltpu.make_async_copy(table, matrix, sems.at[0])
     fetch.start()
-    for half in range(2):
-        value = packed[:, half * 144 + 128 : half * 144 + 144, :].astype(F32)
-        high = jnp.zeros_like(value)
-        for power in (32, 16, 8, 4, 2, 1):
-            over = value >= 2.0**power
-            value = jnp.where(over, value * 2.0**-power, value)
-            high = jnp.where(over, high + float(power), high)
-        share[:, half * 16 : half * 16 + 16, :] = (high + (value - 1.0)) * (1.0 / 32.0)
-
+    fetch_share = pltpu.make_async_copy(shares, share, sems.at[1])
+    fetch_share.start()
     def gather(d, totals):
         value = lines[d, 64:72, :].astype(F32)
         where = wedges[pl.ds(d, 1), :]
@@ -424,13 +452,15 @@
             out[group, 128:144, half * 128 : half * 128 + 128] = value
 
     fetch.wait()
+    fetch_share.wait()
 
     def one_freq(freq, carry):
         for ref in range(2):
             rows = pl.ds(pl.multiple_of(freq * 32 + ref * 16, 16), 16)
-            flat[...] = lines[:, rows, :].astype(F32).reshape(2048, 128)
+            for d in range(128):
+                flat[24 * d : 24 * d + 16, :] = lines[d, rows, :].astype(F32)
             for g in range(8):
-                pair = [flat[pl.ds(side * 8 + g, 128, stride=16), :] for side in range(2)]
+                pair = [flat[pl.ds(side * 8 + g, 128, stride=24), :] for side in range(2)]
                 value = jnp.concatenate([x.T for x in pair], axis=1).astype(BF16)
                 value = dot(jnp.concatenate([value, value], axis=1), matrix[...])
                 values = []
@@ -457,14 +487,14 @@
                             if ref == 0:
                                 kept[a, side, rows, :] = rounded
                             else:
-                                s = share[line_rank(a // 2), rows, lanes]
+                                s = share[a, rows, :]
                                 first = kept[a, side, rows, :].astype(F32)
                                 mixed = first * s + rounded.astype(F32) * (1.0 - s)
                                 row = pl.multiple_of(freq * 64 + side * 32 + part * 16, 16)
                                 out[line_rank(a // 2), pl.ds(row, 16), lanes] = mixed.astype(BF16)
                 return carry
 
-            lax.fori_loop(0, 2, rows16, 0)
+            lax.fori_loop(0, 2, rows16, 0, unroll=True)
         return carry
 
     lax.fori_loop(0, 2, one_freq, 0)
@@ -527,14 +557,16 @@
     return call(pack_kernel, "pack_fields", outs, LOCAL, [FAR] * 3, scratch, 12, args)
 
 
-def phases(omega, slowness, wedge_map):
+def prepare(omega, slowness, wedge_map, packed):
     outs = [
-        jax.ShapeDtypeStruct((2, 2, 2, 1024, 128), F32),
-        jax.ShapeDtypeStruct((128, 128), F32),
+        pltpu.HBM((2, 2, 2, 1024, 128), F32),
+        pltpu.VMEM((128, 128), F32),
+        pltpu.HBM((32, 32, 128), F32),
     ]
-    args = (omega, slowness, wedge_map)
-    specs = [SCALAR] * 2 + [LOCAL]
-    return call(phase_kernel, "phase_table", outs, [LOCAL] * 2, specs, [], 12, args)
+    scale = jnp.asarray(tables()["phase_scale"])
+    args = (omega, slowness, scale, wedge_map, near(packed))
+    specs = [SCALAR] * 2 + [LOCAL] * 3
+    return call(prepare_kernel, "prepare", outs, [LOCAL] * 3, specs, [], 16, args)
 
 
 def cross_forward(packed):
@@ -544,7 +576,7 @@
     scratch = [
         pltpu.VMEM((256, 768), BF16),
         pltpu.VMEM((8, 4, 2, 32, 128), F32),
-        pltpu.VMEM((2048, 128), F32),
+        pltpu.VMEM((3072, 128), F32),
         pltpu.VMEM((4, DEVICES, 16, 128), BF16),
         pltpu.SemaphoreType.DMA,
         pltpu.SemaphoreType.DMA((4,)),
@@ -562,8 +594,8 @@
     outs = pltpu.VMEM((DEVICES, 72, 128), BF16)
     scratch = [
         pltpu.VMEM((4, DEVICES, 16, 128), BF16),
-        pltpu.VMEM((768, 256), BF16),
-        pltpu.VMEM((768, 256), BF16),
+        pltpu.VMEM((256, 256), BF16),
+        pltpu.VMEM((256, 256), BF16),
         pltpu.VMEM((2, 2, 2, 1024, 128), F32),
         pltpu.VMEM((128, 2, 8, 128), F32),
         pltpu.VMEM((2, 1024, 256), F32),
@@ -575,21 +607,21 @@
     return call(inline_kernel, "inline_step", outs, LOCAL, specs, scratch, 20, args)
 
 
-def cross_inverse(partial, wedges, packed):
+def cross_inverse(partial, wedges, share):
     t = tables()
-    args = [near(partial), near(wedges), near(packed), near(jnp.asarray(t["cross_tw_inv"]))]
+    args = [near(partial), near(wedges), far(share), near(jnp.asarray(t["cross_tw_inv"]))]
     args.append(jnp.asarray(t["cross_inv"]))
     outs = pltpu.VMEM((GROUP, 144, 256), BF16)
     scratch = [
         pltpu.VMEM((512, 256), BF16),
-        pltpu.VMEM((2048, 128), F32),
+        pltpu.VMEM((3072, 128), F32),
         pltpu.VMEM((4, 8, 2, 32, 128), F32),
         pltpu.VMEM((32, 2, 32, 128), BF16),
-        pltpu.VMEM((GROUP, 32, 256), F32),
-        pltpu.SemaphoreType.DMA,
+        pltpu.VMEM((32, 32, 128), F32),
+        pltpu.SemaphoreType.DMA((2,)),
     ]
     return call(
-        cross_inverse_kernel, "crossline_inverse", outs, LOCAL, [LOCAL] * 4 + [FAR], scratch, 16, args
+        cross_inverse_kernel, "crossline_inverse", outs, LOCAL, [LOCAL, LOCAL, FAR, LOCAL, FAR], scratch, 16, args
     )
 
 
@@ -609,10 +641,10 @@
 
 def per_device(receiver, source, weight, omega, slowness, wedge_map):
     packed = exchange(pack(receiver, source, weight), LINE)
-    phase, wedges = phases(omega, slowness, wedge_map)
+    phase, wedges, share = prepare(omega, slowness, wedge_map, packed)
     lines = exchange(cross_forward(packed), EVERY)
     partial = exchange(inline_step(lines, phase), EVERY)
-    home = exchange(cross_inverse(partial, wedges, packed), LINE)
+    home = exchange(cross_inverse(partial, wedges, share), LINE)
     mixed, angles = unpack(home)
     return (mixed.reshape(2, 2, 512, 256), angles)
 

time: 159 us -> 155 us (0.975)
  local copies, waits for them, and re-layouts: 2.03 us -> 0.08 us
  Pallas kernels: 29.9 us -> 28.3 us
    unnamed x24, local copies, waits for them, and re-layouts: 2.03 us -> 0.08 us
    pallas_call x6, Pallas kernels: 29.9 us -> 28.3 us  [call(): pl.pallas_call(kernel, in_specs=in_specs, out_specs=out_specs, out_shape=...]
  transfers between devices with their start and end apart: 1 -> 1, of which waited for: 1 -> 1; matrix products, arithmetic and copies ran while one was open for 0% -> 0% of each run, Pallas kernels for 3% -> 5%
where the time goes in v3:
time: 155 us
  blocking collectives  94.6 us (61%)
  Pallas kernels  28.3 us (18%)
  waiting for transfers between devices  22.6 us (15%)
  starting transfers between devices  8.81 us (6%)
    all_to_all x3, blocking collectives, exchange(): return lax.all_to_all(value, axes, 0, 0, tiled=True)  94.6 us
    pallas_call x6, Pallas kernels, call(): pl.pallas_call(kernel, in_specs=in_specs, out_specs=out_specs, out_shape=...  28.3 us
    all_to_all x1, waiting for transfers between devices, exchange(): return lax.all_to_all(value, axes, 0, 0, tiled=True)  22.6 us
    all_to_all x1, starting transfers between devices, exchange(): return lax.all_to_all(value, axes, 0, 0, tiled=True)  8.81 us
  transfers between devices with their start and end apart: 1, of which 1 were waited for; matrix products, arithmetic and copies ran while one was open for 0% of the time, Pallas kernels for 5%

profile of v3, /device:TPU:1, one launch (start us, length us, event | category | flops | bytes accessed | tf_op | source)
XLA Modules:
  0.0 155.1 jit_solution(376338397074858502)
XLA Ops:
  0.6 1.7 %pack_fields.1 = bf16[16,288,256]{2,1,0:T(8,128)(2,1)S(1)} custom-call(bf16[2,2,16,32,256]{4,3,2,1,0:T(8,128)(2,1)} %bitcast.4, bf16[2,2,16,32,256]{4,3,2,1,0:T(8,128)(2,1)} %bitcast.5, s32[16,2,16,256]{3,2,1,0:T(8,128)} %bitcast.6), custom_call_target="tpu_custom_call" | custom-call | tf_op jit(solution)/shard_map/pack_fields/pallas_call | solution.py:538
  2.4 0.0 copy-start
  2.4 0.0 copy-start.8
  2.4 36.5 %all_to_all.20.lines.packed = bf16[16,288,256]{2,1,0:T(8,128)(2,1)S(1)} all-to-all(bf16[16,288,256]{2,1,0:T(8,128)(2,1)S(1)} %pack_fields.1), channel_id=1, replica_groups=mesh['x_hi'=2,'z'=4,'x_lo'=2,'y'=4,'core'=2] {'y','x_lo','core'}, dimensions={0} | all-to-all | bytes 4718592 | tf_op jit(solution)/shard_map/all_to_all | solution.py:639
  38.9 0.0 copy-done
  38.9 0.0 copy-done.8
  38.9 4.6 %crossline_forward.1 = bf16[128,64,128]{2,1,0:T(8,128)(2,1)} custom-call(bf16[16,288,256]{2,1,0:T(8,128)(2,1)S(1)} %all_to_all.20.lines.packed, f32[2,32,128]{2,1,0:T(8,128)S(1)} %copy-done.8, bf16[256,768]{1,0:T(8,128)(2,1)S(1)} %copy-done), custom_call_target="tpu_custom_call" | custom-call | tf_op jit(solution)/shard_map/crossline_forward/pallas_call | solution.py:538
  43.5 0.0 copy-start.6
  43.5 0.0 copy-start.9
  43.5 0.0 copy-start.10
  43.5 0.0 copy-start.11
  43.5 0.0 copy-start.2
  43.5 0.0 copy-start.3
  43.6 0.0 copy-start.4
  43.6 0.0 copy-start.5
  43.6 8.8 %all-to-all-start.1 = ((bf16[128,64,128]{2,1,0:T(8,128)(2,1)}), bf16[128,64,128]{2,1,0:T(8,128)(2,1)}, u32[]{:S(2)}, u32[]{:S(2)}) async-start(bf16[128,64,128]{2,1,0:T(8,128)(2,1)} %crossline_forward.1), calls=%async_computation.1 | async-start | bytes 4194304 | tf_op jit(solution)/shard_map/all_to_all | solution.py:639
  52.4 0.0 copy-done.6
  52.4 0.0 copy-done.9
  52.4 0.0 copy-done.10
  52.4 0.0 copy-done.11
  52.4 7.7 %prepare.1 = (f32[2,2,2,1024,128]{4,3,2,1,0:T(8,128)}, f32[128,128]{1,0:T(8,128)S(1)}, f32[32,32,128]{2,1,0:T(8,128)}) custom-call(f32[2]{0:T(128)S(1)} %copy-done.9, f32[2]{0:T(128)S(1)} %copy-done.10, f32[1,128]{1,0:T(1,128)S(1)} %copy-done.11, s32[128,128]{1,0:T(8,128)S(1)} %copy-done.6, bf16[16,288,256]{2,1,0:T(8,128)(2,1)S(1)} %all_to_all.20.lines.packed), custom_call_target="tpu_custom_call" | custom-call | tf_op jit(solution)/shard_map/prepare/pallas_call | solution.py:538
  60.2 22.6 %all-to-all-done.1.lines = bf16[128,64,128]{2,1,0:T(8,128)(2,1)} async-done(((bf16[128,64,128]{2,1,0:T(8,128)(2,1)}), bf16[128,64,128]{2,1,0:T(8,128)(2,1)}, u32[]{:S(2)}, u32[]{:S(2)}) %all-to-all-start.1) | async-done | bytes 2097184 | tf_op jit(solution)/shard_map/all_to_all | solution.py:639
  82.7 0.0 copy-done.2
  82.7 0.0 copy-done.3
  82.8 0.0 copy-done.4
  82.8 0.0 copy-done.5
  82.8 8.2 %inline_step.1 = bf16[128,72,128]{2,1,0:T(8,128)(2,1)S(1)} custom-call(bf16[128,64,128]{2,1,0:T(8,128)(2,1)} %all-to-all-done.1.lines, f32[2,2,2,1024,128]{4,3,2,1,0:T(8,128)} %get-tuple-element.7.phase, f32[2,128,128]{2,1,0:T(8,128)S(1)} %copy-done.5, f32[2,128,128]{2,1,0:T(8,128)S(1)} %copy-done.4, bf16[256,256]{1,0:T(8,128)(2,1)S(1)} %copy-done.3, ...), custom_call_target="tpu_custom_call" | custom-call | tf_op jit(solution)/shard_map/inline_step/pallas_call | solution.py:538
  91.0 0.0 copy-start.1
  91.0 0.0 copy-start.7
  91.0 37.5 %all_to_all.21.lines = bf16[128,72,128]{2,1,0:T(8,128)(2,1)S(1)} all-to-all(bf16[128,72,128]{2,1,0:T(8,128)(2,1)S(1)} %inline_step.1), channel_id=1, replica_groups=mesh['x_hi'=2,'z'=4,'x_lo'=2,'y'=4,'core'=2] {'x_lo','x_hi','z','y','core'}, dimensions={0} | all-to-all | bytes 4718592 | tf_op jit(solution)/shard_map/all_to_all | solution.py:639
  128.5 0.0 copy-done.1
  128.5 0.0 copy-done.7
  128.5 4.3 %crossline_inverse.1 = bf16[16,144,256]{2,1,0:T(8,128)(2,1)S(1)} custom-call(bf16[128,72,128]{2,1,0:T(8,128)(2,1)S(1)} %all_to_all.21.lines, f32[128,128]{1,0:T(8,128)S(1)} %get-tuple-element.8.wedges, f32[32,32,128]{2,1,0:T(8,128)} %get-tuple-element.9.shares, f32[2,32,128]{2,1,0:T(8,128)S(1)} %copy-done.7, bf16[512,256]{1,0:T(8,128)(2,1)S(1)} %copy-done.1), custom_call_target="tpu_custom_call" | custom-call | tf_op jit(solution)/shard_map/crossline_inverse/pallas_call | solution.py:538
  132.9 20.6 %all_to_all.22.home = bf16[16,144,256]{2,1,0:T(8,128)(2,1)S(1)} all-to-all(bf16[16,144,256]{2,1,0:T(8,128)(2,1)S(1)} %crossline_inverse.1), channel_id=1, replica_groups=mesh['x_hi'=2,'z'=4,'x_lo'=2,'y'=4,'core'=2] {'y','x_lo','core'}, dimensions={0} | all-to-all | bytes 2359296 | tf_op jit(solution)/shard_map/all_to_all | solution.py:639
  153.5 1.7 %unpack_fields.1 = (bf16[2,2,16,32,256]{4,3,2,1,0:T(8,128)(2,1)}, f32[8,4096]{1,0:T(8,128)}) custom-call(bf16[16,144,256]{2,1,0:T(8,128)(2,1)S(1)} %all_to_all.22.home), custom_call_target="tpu_custom_call" | custom-call | tf_op jit(solution)/shard_map/unpack_fields/pallas_call | solution.py:538
Async XLA Ops:
  2.4 36.5 %copy-start = (bf16[256,768]{1,0:T(8,128)(2,1)S(1)}, bf16[256,768]{1,0:T(8,128)(2,1)}, u32[]{:S(2)}) copy-start(bf16[256,768]{1,0:T(8,128)(2,1)} %constant.20.clone.table) | copy-start | bytes 1179652
  2.4 36.5 %copy-start.8 = (f32[2,32,128]{2,1,0:T(8,128)S(1)}, f32[2,32,128]{2,1,0:T(8,128)}, u32[]{:S(2)}) copy-start(f32[2,32,128]{2,1,0:T(8,128)} %constant.19.clone.twist) | copy-start | bytes 98308
  43.5 8.9 %copy-start.6 = (s32[128,128]{1,0:T(8,128)S(1)}, s32[128,128]{1,0:T(8,128)}, u32[]{:S(2)}) copy-start(s32[128,128]{1,0:T(8,128)} %wedge_map.1) | copy-start | bytes 196612
  43.5 8.9 %copy-start.9 = (f32[2]{0:T(128)S(1)}, f32[2]{0:T(128)}, u32[]{:S(2)}) copy-start(f32[2]{0:T(128)} %omega.1) | copy-start | bytes 28
  43.5 8.9 %copy-start.10 = (f32[2]{0:T(128)S(1)}, f32[2]{0:T(128)}, u32[]{:S(2)}) copy-start(f32[2]{0:T(128)} %slowness.1) | copy-start | bytes 28
  43.5 8.9 %copy-start.11 = (f32[1,128]{1,0:T(1,128)S(1)}, f32[1,128]{1,0:T(1,128)}, u32[]{:S(2)}) copy-start(f32[1,128]{1,0:T(1,128)} %constant.18.clone.scale) | copy-start | bytes 1540
  43.5 39.2 %copy-start.2 = (bf16[256,256]{1,0:T(8,128)(2,1)S(1)}, bf16[256,256]{1,0:T(8,128)(2,1)}, u32[]{:S(2)}) copy-start(bf16[256,256]{1,0:T(8,128)(2,1)} %constant.24.clone.table_inv) | copy-start | bytes 393220
  43.5 39.2 %copy-start.3 = (bf16[256,256]{1,0:T(8,128)(2,1)S(1)}, bf16[256,256]{1,0:T(8,128)(2,1)}, u32[]{:S(2)}) copy-start(bf16[256,256]{1,0:T(8,128)(2,1)} %constant.23.clone.table) | copy-start | bytes 393220
  43.6 39.2 %copy-start.4 = (f32[2,128,128]{2,1,0:T(8,128)S(1)}, f32[2,128,128]{2,1,0:T(8,128)}, u32[]{:S(2)}) copy-start(f32[2,128,128]{2,1,0:T(8,128)} %constant.22.clone.twist_inv) | copy-start | bytes 393220
  43.6 39.2 %copy-start.5 = (f32[2,128,128]{2,1,0:T(8,128)S(1)}, f32[2,128,128]{2,1,0:T(8,128)}, u32[]{:S(2)}) copy-start(f32[2,128,128]{2,1,0:T(8,128)} %constant.21.clone.twist) | copy-start | bytes 393220
  43.6 39.2 %all-to-all-start.1 = ((bf16[128,64,128]{2,1,0:T(8,128)(2,1)}), bf16[128,64,128]{2,1,0:T(8,128)(2,1)}, u32[]{:S(2)}, u32[]{:S(2)}) async-start(bf16[128,64,128]{2,1,0:T(8,128)(2,1)} %crossline_forward.1), calls=%async_computation.1 | async-start | bytes 4194304 | tf_op jit(solution)/shard_map/all_to_all | solution.py:639
  91.0 37.6 %copy-start.1 = (bf16[512,256]{1,0:T(8,128)(2,1)S(1)}, bf16[512,256]{1,0:T(8,128)(2,1)}, u32[]{:S(2)}) copy-start(bf16[512,256]{1,0:T(8,128)(2,1)} %constant.26.clone.table) | copy-start | bytes 786436
  91.0 37.6 %copy-start.7 = (f32[2,32,128]{2,1,0:T(8,128)S(1)}, f32[2,32,128]{2,1,0:T(8,128)}, u32[]{:S(2)}) copy-start(f32[2,32,128]{2,1,0:T(8,128)} %constant.25.clone.twist) | copy-start | bytes 98308

commit v4 on v3

--- a/solution.py
+++ b/solution.py
@@ -14,22 +14,27 @@
 SIZE = 4096
 DEVICES = 128
 GROUP = 16
+ROWS = ("x_hi", "z_hi", "z_lo")
+COLUMNS = ("x_lo", "y_hi", "y_lo", "core")
+NAMES = ROWS + COLUMNS
+LINE = ("core", "y_lo", "y_hi", "x_lo")
+EVERY = ("z_lo", "z_hi", "y_lo", "y_hi", "x_lo", "x_hi", "core")
 BF16 = jnp.bfloat16
 F32 = jnp.float32
-NAMES = ("x_hi", "z", "x_lo", "y", "core")
-LINE = ("y", "x_lo", "core")
-EVERY = ("x_lo", "x_hi", "z", "y", "core")
 HALF = math.sqrt(0.5)
 
 
+def reorder(value, old, new):
+    bits = {name: value >> place & 1 for place, name in enumerate(reversed(old))}
+    return sum(bits[name] << place for place, name in enumerate(reversed(new)))
+
+
 def line_rank(block):
-    high, rest = divmod(block, 8)
-    return rest // 2 * 4 + high * 2 + rest % 2
+    return reorder(block, COLUMNS, LINE)
 
 
 def every_rank(block):
-    group, line = divmod(block, GROUP)
-    return line // 2 % 2 * 64 + group * 8 + line // 4 * 2 + line % 2
+    return reorder(block, ROWS + LINE, EVERY)
 
 
 def roots(rows, cols, length, sign):
@@ -182,8 +187,10 @@
 
 
 def prepare_kernel(omega, slowness, scale, wedge_map, packed, phase, wedges, share):
-    x_hi, z, x_lo, y, core = (lax.axis_index(name) for name in NAMES)
-    device = ((x_lo * 2 + x_hi) * 4 + z) * 8 + y * 2 + core
+    place = {name: lax.axis_index(name) for name in NAMES}
+    device = 0
+    for name in EVERY:
+        device = device * 2 + place[name]
     step = 2.0 * math.pi / SIZE
 
     def signed(index):
@@ -217,7 +224,7 @@
         return carry
 
     lax.fori_loop(0, 16, body, 0)
-    rows = wedge_map[pl.ds(y, 32, stride=4), :].astype(F32)
+    rows = wedge_map[pl.ds(place["core"] * 2 + place["y_lo"], 32, stride=4), :].astype(F32)
     wedges[...] = jnp.concatenate([rows] * 4, axis=0).T
     for half in range(2):
         for a in range(32):
@@ -407,12 +414,8 @@
     total = total + pltpu.roll(total, 64, 1)
     total = total + pltpu.roll(total, 32, 1)
     high = total.astype(BF16).astype(F32)
-    rest = total - high
-    middle = rest.astype(BF16).astype(F32)
-    low = rest - middle
     place = lax.broadcasted_iota(jnp.int32, (128, 128), 1) >> 5
-    value = jnp.where(place == 0, high, jnp.where(place == 1, middle, low))
-    value = jnp.where(place == 3, 0.0, value).reshape(16, 8, 128).astype(BF16)
+    value = jnp.where(place % 2 == 0, high, total - high).reshape(16, 8, 128).astype(BF16)
     for block in range(DEVICES):
         out[every_rank(block), 64:72, :] = value[block % GROUP]
 
@@ -424,38 +427,35 @@
     fetch.start()
     fetch_share = pltpu.make_async_copy(shares, share, sems.at[1])
     fetch_share.start()
+    place = lax.broadcasted_iota(jnp.int32, (8, 128), 1) >> 5
+    odd = (place >> 1).astype(F32)
+
     def gather(d, totals):
         value = lines[d, 64:72, :].astype(F32)
-        where = wedges[pl.ds(d, 1), :]
+        where = wedges[pl.ds(d, 1), :] - odd
         return tuple(
-            total + jnp.where(where == float(w), value, 0.0) for w, total in enumerate(totals)
+            total + jnp.where(where == 2.0 * j, value, 0.0) for j, total in enumerate(totals)
         )
 
     zero = jnp.zeros((8, 128), F32)
-    totals = lax.fori_loop(0, 128, gather, (zero,) * 8, unroll=8)
-    highs, lows = [], []
-    for total in totals:
-        total = total + pltpu.roll(total, 64, 1)
-        total = total + pltpu.roll(total, 32, 1)
-        total = total * (1.0 / (SIZE * SIZE * math.sqrt(SIZE)))
-        highs.append(total.astype(BF16).astype(F32))
-        lows.append(total - highs[-1])
-    place = lax.broadcasted_iota(jnp.int32, (8, 128), 1) >> 5
+    totals = lax.fori_loop(0, 128, gather, (zero,) * 4, unroll=16)
+    totals = [total + pltpu.roll(total, 96, 1) for total in totals]
     for half in range(2):
-        rows = []
-        for first in (half * 2, half * 2 + 4):
-            even = jnp.where(place == 0, highs[first], lows[first])
-            odd = jnp.where(place == 2, highs[first + 1], lows[first + 1])
-            rows.append(jnp.where(place < 2, even, odd))
-        value = jnp.concatenate(rows, axis=0).astype(BF16)
+        value = jnp.where(place % 2 == 0, totals[2 * half], pltpu.roll(totals[2 * half + 1], 32, 1))
+        value = (value * (1.0 / (SIZE * SIZE * math.sqrt(SIZE)))).astype(BF16)
         for group in range(16):
-            out[group, 128:144, half * 128 : half * 128 + 128] = value
+            out[group, 128:136, half * 128 : half * 128 + 128] = value
 
     fetch.wait()
-    fetch_share.wait()
 
     def one_freq(freq, carry):
         for ref in range(2):
+            if ref == 1:
+
+                @pl.when(freq == 0)
+                def _():
+                    fetch_share.wait()
+
             rows = pl.ds(pl.multiple_of(freq * 32 + ref * 16, 16), 16)
             for d in range(128):
                 flat[24 * d : 24 * d + 16, :] = lines[d, rows, :].astype(F32)
@@ -507,14 +507,12 @@
         copies.append(pltpu.make_async_copy(block, out.at[part % 2, part // 2], sems.at[part]))
     for copy in copies:
         copy.start()
-    value = home[:, 128:144, :].astype(F32)
+    value = home[:, 128:136, :].astype(F32)
     for half in range(2):
-        for top in range(2):
-            part = value[:, top * 8 : top * 8 + 8, half * 128 : half * 128 + 128]
-            flipped = part.reshape(128, 128).T
-            w = top * 4 + half * 2
-            turned[pl.ds(w, 32, stride=8), :] = flipped[0:32] + flipped[32:64]
-            turned[pl.ds(w + 1, 32, stride=8), :] = flipped[64:96] + flipped[96:128]
+        flipped = value[:, :, half * 128 : half * 128 + 128].reshape(128, 128).T
+        for group, wedge in enumerate((0, 2, 1, 3)):
+            rows = pl.ds(half * 4 + wedge, 32, stride=8)
+            turned[rows, :] = flipped[group * 32 : group * 32 + 32]
     for k in range(32):
         angles[:, k * 128 : k * 128 + 128] = turned[k * 8 : k * 8 + 8, :]
     for copy in copies:
@@ -611,7 +609,7 @@
     t = tables()
     args = [near(partial), near(wedges), far(share), near(jnp.asarray(t["cross_tw_inv"]))]
     args.append(jnp.asarray(t["cross_inv"]))
-    outs = pltpu.VMEM((GROUP, 144, 256), BF16)
+    outs = pltpu.VMEM((GROUP, 136, 256), BF16)
     scratch = [
         pltpu.VMEM((512, 256), BF16),
         pltpu.VMEM((3072, 128), F32),
@@ -650,19 +648,18 @@
 
 
 def solution(mesh):
-    fine = Mesh(mesh.devices.reshape(2, 4, 2, 4, 2), NAMES)
-    rows, columns = ("x_hi", "z"), ("x_lo", "y", "core")
+    fine = Mesh(mesh.devices.reshape((2,) * 7), NAMES)
     return jax.shard_map(
         per_device,
         mesh=fine,
         in_specs=(
-            P(None, None, rows, columns),
-            P(None, None, rows, columns),
-            P(rows, columns),
+            P(None, None, ROWS, COLUMNS),
+            P(None, None, ROWS, COLUMNS),
+            P(ROWS, COLUMNS),
             P(),
             P(),
             P(),
         ),
-        out_specs=(P(None, None, rows, columns), P()),
+        out_specs=(P(None, None, ROWS, COLUMNS), P()),
         check_vma=False,
     )

time: 155 us -> 154 us (level)
  no operation moved by 1% of the time
where the time goes in v4:
time: 154 us
  blocking collectives  93.6 us (61%)
  Pallas kernels  27.8 us (18%)
  waiting for transfers between devices  22 us (14%)
  starting transfers between devices  9.31 us (6%)
    all_to_all x3, blocking collectives, exchange(): return lax.all_to_all(value, axes, 0, 0, tiled=True)  93.6 us
    pallas_call x6, Pallas kernels, call(): pl.pallas_call(kernel, in_specs=in_specs, out_specs=out_specs, out_shape=...  27.8 us
    all_to_all x1, waiting for transfers between devices, exchange(): return lax.all_to_all(value, axes, 0, 0, tiled=True)  22 us
    all_to_all x1, starting transfers between devices, exchange(): return lax.all_to_all(value, axes, 0, 0, tiled=True)  9.31 us
  transfers between devices with their start and end apart: 1, of which 1 were waited for; matrix products, arithmetic and copies ran while one was open for 0% of the time, Pallas kernels for 5%

profile of v4, /device:TPU:1, one launch (start us, length us, event | category | flops | bytes accessed | tf_op | source)
XLA Modules:
  0.0 153.6 jit_solution(751035722489262180)
XLA Ops:
  0.6 1.7 %pack_fields.1 = bf16[16,288,256]{2,1,0:T(8,128)(2,1)S(1)} custom-call(bf16[2,2,16,32,256]{4,3,2,1,0:T(8,128)(2,1)} %bitcast.4, bf16[2,2,16,32,256]{4,3,2,1,0:T(8,128)(2,1)} %bitcast.5, s32[16,2,16,256]{3,2,1,0:T(8,128)} %bitcast.6), custom_call_target="tpu_custom_call" | custom-call | tf_op jit(solution)/shard_map/pack_fields/pallas_call | solution.py:536
  2.4 0.0 copy-start
  2.4 0.0 copy-start.8
  2.4 36.2 %all_to_all.20.lines.packed = bf16[16,288,256]{2,1,0:T(8,128)(2,1)S(1)} all-to-all(bf16[16,288,256]{2,1,0:T(8,128)(2,1)S(1)} %pack_fields.1), channel_id=1, replica_groups=mesh['x_hi'=2,'z_hi'=2,'z_lo'=2,'x_lo'=2,'y_hi'=2,'y_lo'=2,'core'=2] {'c..., dimensions={0} | all-to-all | bytes 4718592 | tf_op jit(solution)/shard_map/all_to_all | solution.py:637
  38.6 0.0 copy-done
  38.6 0.0 copy-done.8
  38.6 4.6 %crossline_forward.1 = bf16[128,64,128]{2,1,0:T(8,128)(2,1)} custom-call(bf16[16,288,256]{2,1,0:T(8,128)(2,1)S(1)} %all_to_all.20.lines.packed, f32[2,32,128]{2,1,0:T(8,128)S(1)} %copy-done.8, bf16[256,768]{1,0:T(8,128)(2,1)S(1)} %copy-done), custom_call_target="tpu_custom_call" | custom-call | tf_op jit(solution)/shard_map/crossline_forward/pallas_call | solution.py:536
  43.2 0.0 copy-start.6
  43.2 0.0 copy-start.9
  43.3 0.0 copy-start.10
  43.3 0.0 copy-start.11
  43.3 0.0 copy-start.2
  43.3 0.0 copy-start.3
  43.3 0.0 copy-start.4
  43.3 0.0 copy-start.5
  43.3 9.3 %all-to-all-start.1 = ((bf16[128,64,128]{2,1,0:T(8,128)(2,1)}), bf16[128,64,128]{2,1,0:T(8,128)(2,1)}, u32[]{:S(2)}, u32[]{:S(2)}) async-start(bf16[128,64,128]{2,1,0:T(8,128)(2,1)} %crossline_forward.1), calls=%async_computation.1 | async-start | bytes 4194304 | tf_op jit(solution)/shard_map/all_to_all | solution.py:637
  52.6 0.0 copy-done.6
  52.7 0.0 copy-done.9
  52.7 0.0 copy-done.10
  52.7 0.0 copy-done.11
  52.7 7.7 %prepare.1 = (f32[2,2,2,1024,128]{4,3,2,1,0:T(8,128)}, f32[128,128]{1,0:T(8,128)S(1)}, f32[32,32,128]{2,1,0:T(8,128)}) custom-call(f32[2]{0:T(128)S(1)} %copy-done.9, f32[2]{0:T(128)S(1)} %copy-done.10, f32[1,128]{1,0:T(1,128)S(1)} %copy-done.11, s32[128,128]{1,0:T(8,128)S(1)} %copy-done.6, bf16[16,288,256]{2,1,0:T(8,128)(2,1)S(1)} %all_to_all.20.lines.packed), custom_call_target="tpu_custom_call" | custom-call | tf_op jit(solution)/shard_map/prepare/pallas_call | solution.py:536
  60.4 22.0 %all-to-all-done.1.lines = bf16[128,64,128]{2,1,0:T(8,128)(2,1)} async-done(((bf16[128,64,128]{2,1,0:T(8,128)(2,1)}), bf16[128,64,128]{2,1,0:T(8,128)(2,1)}, u32[]{:S(2)}, u32[]{:S(2)}) %all-to-all-start.1) | async-done | bytes 2097184 | tf_op jit(solution)/shard_map/all_to_all | solution.py:637
  82.4 0.0 copy-done.2
  82.4 0.0 copy-done.3
  82.4 0.0 copy-done.4
  82.4 0.0 copy-done.5
  82.4 8.2 %inline_step.1 = bf16[128,72,128]{2,1,0:T(8,128)(2,1)S(1)} custom-call(bf16[128,64,128]{2,1,0:T(8,128)(2,1)} %all-to-all-done.1.lines, f32[2,2,2,1024,128]{4,3,2,1,0:T(8,128)} %get-tuple-element.7.phase, f32[2,128,128]{2,1,0:T(8,128)S(1)} %copy-done.5, f32[2,128,128]{2,1,0:T(8,128)S(1)} %copy-done.4, bf16[256,256]{1,0:T(8,128)(2,1)S(1)} %copy-done.3, ...), custom_call_target="tpu_custom_call" | custom-call | tf_op jit(solution)/shard_map/inline_step/pallas_call | solution.py:536
  90.6 0.0 copy-start.1
  90.6 0.0 copy-start.7
  90.7 37.8 %all_to_all.21.lines = bf16[128,72,128]{2,1,0:T(8,128)(2,1)S(1)} all-to-all(bf16[128,72,128]{2,1,0:T(8,128)(2,1)S(1)} %inline_step.1), channel_id=1, replica_groups=mesh['x_hi'=2,'z_hi'=2,'z_lo'=2,'x_lo'=2,'y_hi'=2,'y_lo'=2,'core'=2] {'z..., dimensions={0} | all-to-all | bytes 4718592 | tf_op jit(solution)/shard_map/all_to_all | solution.py:637
  128.4 0.0 copy-done.1
  128.4 0.0 copy-done.7
  128.4 3.9 %crossline_inverse.1 = bf16[16,136,256]{2,1,0:T(8,128)(2,1)S(1)} custom-call(bf16[128,72,128]{2,1,0:T(8,128)(2,1)S(1)} %all_to_all.21.lines, f32[128,128]{1,0:T(8,128)S(1)} %get-tuple-element.8.wedges, f32[32,32,128]{2,1,0:T(8,128)} %get-tuple-element.9.shares, f32[2,32,128]{2,1,0:T(8,128)S(1)} %copy-done.7, bf16[512,256]{1,0:T(8,128)(2,1)S(1)} %copy-done.1), custom_call_target="tpu_custom_call" | custom-call | tf_op jit(solution)/shard_map/crossline_inverse/pallas_call | solution.py:536
  132.4 19.5 %all_to_all.22.home = bf16[16,136,256]{2,1,0:T(8,128)(2,1)S(1)} all-to-all(bf16[16,136,256]{2,1,0:T(8,128)(2,1)S(1)} %crossline_inverse.1), channel_id=1, replica_groups=mesh['x_hi'=2,'z_hi'=2,'z_lo'=2,'x_lo'=2,'y_hi'=2,'y_lo'=2,'core'=2] {'c..., dimensions={0} | all-to-all | bytes 2228224 | tf_op jit(solution)/shard_map/all_to_all | solution.py:637
  151.9 1.7 %unpack_fields.1 = (bf16[2,2,16,32,256]{4,3,2,1,0:T(8,128)(2,1)}, f32[8,4096]{1,0:T(8,128)}) custom-call(bf16[16,136,256]{2,1,0:T(8,128)(2,1)S(1)} %all_to_all.22.home), custom_call_target="tpu_custom_call" | custom-call | tf_op jit(solution)/shard_map/unpack_fields/pallas_call | solution.py:536
Async XLA Ops:
  2.4 36.3 %copy-start = (bf16[256,768]{1,0:T(8,128)(2,1)S(1)}, bf16[256,768]{1,0:T(8,128)(2,1)}, u32[]{:S(2)}) copy-start(bf16[256,768]{1,0:T(8,128)(2,1)} %constant.20.clone.table) | copy-start | bytes 1179652
  2.4 36.3 %copy-start.8 = (f32[2,32,128]{2,1,0:T(8,128)S(1)}, f32[2,32,128]{2,1,0:T(8,128)}, u32[]{:S(2)}) copy-start(f32[2,32,128]{2,1,0:T(8,128)} %constant.19.clone.twist) | copy-start | bytes 98308
  43.2 9.4 %copy-start.6 = (s32[128,128]{1,0:T(8,128)S(1)}, s32[128,128]{1,0:T(8,128)}, u32[]{:S(2)}) copy-start(s32[128,128]{1,0:T(8,128)} %wedge_map.1) | copy-start | bytes 196612
  43.2 9.4 %copy-start.9 = (f32[2]{0:T(128)S(1)}, f32[2]{0:T(128)}, u32[]{:S(2)}) copy-start(f32[2]{0:T(128)} %omega.1) | copy-start | bytes 28
  43.3 9.4 %copy-start.10 = (f32[2]{0:T(128)S(1)}, f32[2]{0:T(128)}, u32[]{:S(2)}) copy-start(f32[2]{0:T(128)} %slowness.1) | copy-start | bytes 28
  43.3 9.4 %copy-start.11 = (f32[1,128]{1,0:T(1,128)S(1)}, f32[1,128]{1,0:T(1,128)}, u32[]{:S(2)}) copy-start(f32[1,128]{1,0:T(1,128)} %constant.18.clone.scale) | copy-start | bytes 1540
  43.3 39.1 %copy-start.2 = (bf16[256,256]{1,0:T(8,128)(2,1)S(1)}, bf16[256,256]{1,0:T(8,128)(2,1)}, u32[]{:S(2)}) copy-start(bf16[256,256]{1,0:T(8,128)(2,1)} %constant.24.clone.table_inv) | copy-start | bytes 393220
  43.3 39.1 %copy-start.3 = (bf16[256,256]{1,0:T(8,128)(2,1)S(1)}, bf16[256,256]{1,0:T(8,128)(2,1)}, u32[]{:S(2)}) copy-start(bf16[256,256]{1,0:T(8,128)(2,1)} %constant.23.clone.table) | copy-start | bytes 393220
  43.3 39.1 %copy-start.4 = (f32[2,128,128]{2,1,0:T(8,128)S(1)}, f32[2,128,128]{2,1,0:T(8,128)}, u32[]{:S(2)}) copy-start(f32[2,128,128]{2,1,0:T(8,128)} %constant.22.clone.twist_inv) | copy-start | bytes 393220
  43.3 39.1 %copy-start.5 = (f32[2,128,128]{2,1,0:T(8,128)S(1)}, f32[2,128,128]{2,1,0:T(8,128)}, u32[]{:S(2)}) copy-start(f32[2,128,128]{2,1,0:T(8,128)} %constant.21.clone.twist) | copy-start | bytes 393220
  43.3 39.1 %all-to-all-start.1 = ((bf16[128,64,128]{2,1,0:T(8,128)(2,1)}), bf16[128,64,128]{2,1,0:T(8,128)(2,1)}, u32[]{:S(2)}, u32[]{:S(2)}) async-start(bf16[128,64,128]{2,1,0:T(8,128)(2,1)} %crossline_forward.1), calls=%async_computation.1 | async-start | bytes 4194304 | tf_op jit(solution)/shard_map/all_to_all | solution.py:637
  90.6 37.8 %copy-start.1 = (bf16[512,256]{1,0:T(8,128)(2,1)S(1)}, bf16[512,256]{1,0:T(8,128)(2,1)}, u32[]{:S(2)}) copy-start(bf16[512,256]{1,0:T(8,128)(2,1)} %constant.26.clone.table) | copy-start | bytes 786436
  90.6 37.8 %copy-start.7 = (f32[2,32,128]{2,1,0:T(8,128)S(1)}, f32[2,32,128]{2,1,0:T(8,128)}, u32[]{:S(2)}) copy-start(f32[2,32,128]{2,1,0:T(8,128)} %constant.25.clone.twist) | copy-start | bytes 98308

commit v5 on v4

--- a/solution.py
+++ b/solution.py
@@ -500,7 +500,7 @@
     lax.fori_loop(0, 2, one_freq, 0)
 
 
-def unpack_kernel(home, out, angles, turned, sems):
+def unpack_kernel(home, out, angles, turned, wide, sems):
     copies = []
     for part in range(4):
         block = home.at[:, pl.ds(part * 32, 32), :]
@@ -514,7 +514,9 @@
             rows = pl.ds(half * 4 + wedge, 32, stride=8)
             turned[rows, :] = flipped[group * 32 : group * 32 + 32]
     for k in range(32):
-        angles[:, k * 128 : k * 128 + 128] = turned[k * 8 : k * 8 + 8, :]
+        wide[:, k * 128 : k * 128 + 128] = turned[k * 8 : k * 8 + 8, :]
+    copies.append(pltpu.make_async_copy(wide, angles, sems.at[4]))
+    copies[4].start()
     for copy in copies:
         copy.wait()
 
@@ -625,11 +627,15 @@
 
 def unpack(home):
     outs = [
-        jax.ShapeDtypeStruct((2, 2, GROUP, 32, 256), BF16),
-        jax.ShapeDtypeStruct((8, SIZE), F32),
+        pltpu.HBM((2, 2, GROUP, 32, 256), BF16),
+        pltpu.HBM((8, SIZE), F32),
     ]
-    scratch = [pltpu.VMEM((256, 128), F32), pltpu.SemaphoreType.DMA((4,))]
-    specs = [FAR, LOCAL]
+    scratch = [
+        pltpu.VMEM((256, 128), F32),
+        pltpu.VMEM((8, SIZE), F32),
+        pltpu.SemaphoreType.DMA((5,)),
+    ]
+    specs = [FAR, FAR]
     return call(unpack_kernel, "unpack_fields", outs, specs, [LOCAL], scratch, 12, [near(home)])
 
 

time: 154 us -> 153 us (level)
  no operation moved by 1% of the time
where the time goes in v5:
time: 153 us
  blocking collectives  93.6 us (61%)
  Pallas kernels  27.2 us (18%)
  waiting for transfers between devices  22 us (14%)
  starting transfers between devices  9.31 us (6%)
    all_to_all x3, blocking collectives, exchange(): return lax.all_to_all(value, axes, 0, 0, tiled=True)  93.6 us
    pallas_call x6, Pallas kernels, call(): pl.pallas_call(kernel, in_specs=in_specs, out_specs=out_specs, out_shape=...  27.2 us
    all_to_all x1, waiting for transfers between devices, exchange(): return lax.all_to_all(value, axes, 0, 0, tiled=True)  22 us
    all_to_all x1, starting transfers between devices, exchange(): return lax.all_to_all(value, axes, 0, 0, tiled=True)  9.31 us
  transfers between devices with their start and end apart: 1, of which 1 were waited for; matrix products, arithmetic and copies ran while one was open for 0% of the time, Pallas kernels for 5%

profile of v5, /device:TPU:1, one launch (start us, length us, event | category | flops | bytes accessed | tf_op | source)
XLA Modules:
  0.0 153.0 jit_solution(15465380018671051727)
XLA Ops:
  0.6 1.7 %pack_fields.1 = bf16[16,288,256]{2,1,0:T(8,128)(2,1)S(1)} custom-call(bf16[2,2,16,32,256]{4,3,2,1,0:T(8,128)(2,1)} %bitcast.4, bf16[2,2,16,32,256]{4,3,2,1,0:T(8,128)(2,1)} %bitcast.5, s32[16,2,16,256]{3,2,1,0:T(8,128)} %bitcast.6), custom_call_target="tpu_custom_call" | custom-call | tf_op jit(solution)/shard_map/pack_fields/pallas_call | solution.py:538
  2.4 0.0 copy-start
  2.4 0.0 copy-start.8
  2.4 36.2 %all_to_all.20.lines.packed = bf16[16,288,256]{2,1,0:T(8,128)(2,1)S(1)} all-to-all(bf16[16,288,256]{2,1,0:T(8,128)(2,1)S(1)} %pack_fields.1), channel_id=1, replica_groups=mesh['x_hi'=2,'z_hi'=2,'z_lo'=2,'x_lo'=2,'y_hi'=2,'y_lo'=2,'core'=2] {'c..., dimensions={0} | all-to-all | bytes 4718592 | tf_op jit(solution)/shard_map/all_to_all | solution.py:643
  38.6 0.0 copy-done
  38.6 0.0 copy-done.8
  38.6 4.6 %crossline_forward.1 = bf16[128,64,128]{2,1,0:T(8,128)(2,1)} custom-call(bf16[16,288,256]{2,1,0:T(8,128)(2,1)S(1)} %all_to_all.20.lines.packed, f32[2,32,128]{2,1,0:T(8,128)S(1)} %copy-done.8, bf16[256,768]{1,0:T(8,128)(2,1)S(1)} %copy-done), custom_call_target="tpu_custom_call" | custom-call | tf_op jit(solution)/shard_map/crossline_forward/pallas_call | solution.py:538
  43.2 0.0 copy-start.6
  43.2 0.0 copy-start.9
  43.3 0.0 copy-start.10
  43.3 0.0 copy-start.11
  43.3 0.0 copy-start.2
  43.3 0.0 copy-start.3
  43.3 0.0 copy-start.4
  43.3 0.0 copy-start.5
  43.3 9.3 %all-to-all-start.1 = ((bf16[128,64,128]{2,1,0:T(8,128)(2,1)}), bf16[128,64,128]{2,1,0:T(8,128)(2,1)}, u32[]{:S(2)}, u32[]{:S(2)}) async-start(bf16[128,64,128]{2,1,0:T(8,128)(2,1)} %crossline_forward.1), calls=%async_computation.1 | async-start | bytes 4194304 | tf_op jit(solution)/shard_map/all_to_all | solution.py:643
  52.6 0.0 copy-done.6
  52.7 0.0 copy-done.9
  52.7 0.0 copy-done.10
  52.7 0.0 copy-done.11
  52.7 7.7 %prepare.1 = (f32[2,2,2,1024,128]{4,3,2,1,0:T(8,128)}, f32[128,128]{1,0:T(8,128)S(1)}, f32[32,32,128]{2,1,0:T(8,128)}) custom-call(f32[2]{0:T(128)S(1)} %copy-done.9, f32[2]{0:T(128)S(1)} %copy-done.10, f32[1,128]{1,0:T(1,128)S(1)} %copy-done.11, s32[128,128]{1,0:T(8,128)S(1)} %copy-done.6, bf16[16,288,256]{2,1,0:T(8,128)(2,1)S(1)} %all_to_all.20.lines.packed), custom_call_target="tpu_custom_call" | custom-call | tf_op jit(solution)/shard_map/prepare/pallas_call | solution.py:538
  60.4 22.0 %all-to-all-done.1.lines = bf16[128,64,128]{2,1,0:T(8,128)(2,1)} async-done(((bf16[128,64,128]{2,1,0:T(8,128)(2,1)}), bf16[128,64,128]{2,1,0:T(8,128)(2,1)}, u32[]{:S(2)}, u32[]{:S(2)}) %all-to-all-start.1) | async-done | bytes 2097184 | tf_op jit(solution)/shard_map/all_to_all | solution.py:643
  82.4 0.0 copy-done.2
  82.4 0.0 copy-done.3
  82.4 0.0 copy-done.4
  82.4 0.0 copy-done.5
  82.4 8.2 %inline_step.1 = bf16[128,72,128]{2,1,0:T(8,128)(2,1)S(1)} custom-call(bf16[128,64,128]{2,1,0:T(8,128)(2,1)} %all-to-all-done.1.lines, f32[2,2,2,1024,128]{4,3,2,1,0:T(8,128)} %get-tuple-element.7.phase, f32[2,128,128]{2,1,0:T(8,128)S(1)} %copy-done.5, f32[2,128,128]{2,1,0:T(8,128)S(1)} %copy-done.4, bf16[256,256]{1,0:T(8,128)(2,1)S(1)} %copy-done.3, ...), custom_call_target="tpu_custom_call" | custom-call | tf_op jit(solution)/shard_map/inline_step/pallas_call | solution.py:538
  90.6 0.0 copy-start.1
  90.6 0.0 copy-start.7
  90.7 37.8 %all_to_all.21.lines = bf16[128,72,128]{2,1,0:T(8,128)(2,1)S(1)} all-to-all(bf16[128,72,128]{2,1,0:T(8,128)(2,1)S(1)} %inline_step.1), channel_id=1, replica_groups=mesh['x_hi'=2,'z_hi'=2,'z_lo'=2,'x_lo'=2,'y_hi'=2,'y_lo'=2,'core'=2] {'z..., dimensions={0} | all-to-all | bytes 4718592 | tf_op jit(solution)/shard_map/all_to_all | solution.py:643
  128.4 0.0 copy-done.1
  128.4 0.0 copy-done.7
  128.4 3.9 %crossline_inverse.1 = bf16[16,136,256]{2,1,0:T(8,128)(2,1)S(1)} custom-call(bf16[128,72,128]{2,1,0:T(8,128)(2,1)S(1)} %all_to_all.21.lines, f32[128,128]{1,0:T(8,128)S(1)} %get-tuple-element.8.wedges, f32[32,32,128]{2,1,0:T(8,128)} %get-tuple-element.9.shares, f32[2,32,128]{2,1,0:T(8,128)S(1)} %copy-done.7, bf16[512,256]{1,0:T(8,128)(2,1)S(1)} %copy-done.1), custom_call_target="tpu_custom_call" | custom-call | tf_op jit(solution)/shard_map/crossline_inverse/pallas_call | solution.py:538
  132.4 19.5 %all_to_all.22.home = bf16[16,136,256]{2,1,0:T(8,128)(2,1)S(1)} all-to-all(bf16[16,136,256]{2,1,0:T(8,128)(2,1)S(1)} %crossline_inverse.1), channel_id=1, replica_groups=mesh['x_hi'=2,'z_hi'=2,'z_lo'=2,'x_lo'=2,'y_hi'=2,'y_lo'=2,'core'=2] {'c..., dimensions={0} | all-to-all | bytes 2228224 | tf_op jit(solution)/shard_map/all_to_all | solution.py:643
  151.9 1.0 unpack_fields.1
Async XLA Ops:
  2.4 36.3 %copy-start = (bf16[256,768]{1,0:T(8,128)(2,1)S(1)}, bf16[256,768]{1,0:T(8,128)(2,1)}, u32[]{:S(2)}) copy-start(bf16[256,768]{1,0:T(8,128)(2,1)} %constant.20.clone.table) | copy-start | bytes 1179652
  2.4 36.3 %copy-start.8 = (f32[2,32,128]{2,1,0:T(8,128)S(1)}, f32[2,32,128]{2,1,0:T(8,128)}, u32[]{:S(2)}) copy-start(f32[2,32,128]{2,1,0:T(8,128)} %constant.19.clone.twist) | copy-start | bytes 98308
  43.2 9.4 %copy-start.6 = (s32[128,128]{1,0:T(8,128)S(1)}, s32[128,128]{1,0:T(8,128)}, u32[]{:S(2)}) copy-start(s32[128,128]{1,0:T(8,128)} %wedge_map.1) | copy-start | bytes 196612
  43.2 9.4 %copy-start.9 = (f32[2]{0:T(128)S(1)}, f32[2]{0:T(128)}, u32[]{:S(2)}) copy-start(f32[2]{0:T(128)} %omega.1) | copy-start | bytes 28
  43.3 9.4 %copy-start.10 = (f32[2]{0:T(128)S(1)}, f32[2]{0:T(128)}, u32[]{:S(2)}) copy-start(f32[2]{0:T(128)} %slowness.1) | copy-start | bytes 28
  43.3 9.4 %copy-start.11 = (f32[1,128]{1,0:T(1,128)S(1)}, f32[1,128]{1,0:T(1,128)}, u32[]{:S(2)}) copy-start(f32[1,128]{1,0:T(1,128)} %constant.18.clone.scale) | copy-start | bytes 1540
  43.3 39.1 %copy-start.2 = (bf16[256,256]{1,0:T(8,128)(2,1)S(1)}, bf16[256,256]{1,0:T(8,128)(2,1)}, u32[]{:S(2)}) copy-start(bf16[256,256]{1,0:T(8,128)(2,1)} %constant.24.clone.table_inv) | copy-start | bytes 393220
  43.3 39.1 %copy-start.3 = (bf16[256,256]{1,0:T(8,128)(2,1)S(1)}, bf16[256,256]{1,0:T(8,128)(2,1)}, u32[]{:S(2)}) copy-start(bf16[256,256]{1,0:T(8,128)(2,1)} %constant.23.clone.table) | copy-start | bytes 393220
  43.3 39.1 %copy-start.4 = (f32[2,128,128]{2,1,0:T(8,128)S(1)}, f32[2,128,128]{2,1,0:T(8,128)}, u32[]{:S(2)}) copy-start(f32[2,128,128]{2,1,0:T(8,128)} %constant.22.clone.twist_inv) | copy-start | bytes 393220
  43.3 39.1 %copy-start.5 = (f32[2,128,128]{2,1,0:T(8,128)S(1)}, f32[2,128,128]{2,1,0:T(8,128)}, u32[]{:S(2)}) copy-start(f32[2,128,128]{2,1,0:T(8,128)} %constant.21.clone.twist) | copy-start | bytes 393220
  43.3 39.1 %all-to-all-start.1 = ((bf16[128,64,128]{2,1,0:T(8,128)(2,1)}), bf16[128,64,128]{2,1,0:T(8,128)(2,1)}, u32[]{:S(2)}, u32[]{:S(2)}) async-start(bf16[128,64,128]{2,1,0:T(8,128)(2,1)} %crossline_forward.1), calls=%async_computation.1 | async-start | bytes 4194304 | tf_op jit(solution)/shard_map/all_to_all | solution.py:643
  90.6 37.8 %copy-start.1 = (bf16[512,256]{1,0:T(8,128)(2,1)S(1)}, bf16[512,256]{1,0:T(8,128)(2,1)}, u32[]{:S(2)}) copy-start(bf16[512,256]{1,0:T(8,128)(2,1)} %constant.26.clone.table) | copy-start | bytes 786436
  90.6 37.8 %copy-start.7 = (f32[2,32,128]{2,1,0:T(8,128)S(1)}, f32[2,32,128]{2,1,0:T(8,128)}, u32[]{:S(2)}) copy-start(f32[2,32,128]{2,1,0:T(8,128)} %constant.25.clone.twist) | copy-start | bytes 98308

commit v6 on v5

--- a/solution.py
+++ b/solution.py
@@ -19,6 +19,7 @@
 NAMES = ROWS + COLUMNS
 LINE = ("core", "y_lo", "y_hi", "x_lo")
 EVERY = ("z_lo", "z_hi", "y_lo", "y_hi", "x_lo", "x_hi", "core")
+MESSAGE = 66
 BF16 = jnp.bfloat16
 F32 = jnp.float32
 HALF = math.sqrt(0.5)
@@ -186,7 +187,9 @@
         copy.wait()
 
 
-def prepare_kernel(omega, slowness, scale, wedge_map, packed, phase, wedges, share):
+def prepare_kernel(
+    omega, slowness, scale, wedge_map, packed, phase, wedges, share, tiles
+):
     place = {name: lax.axis_index(name) for name in NAMES}
     device = 0
     for name in EVERY:
@@ -224,8 +227,11 @@
         return carry
 
     lax.fori_loop(0, 16, body, 0)
-    rows = wedge_map[pl.ds(place["core"] * 2 + place["y_lo"], 32, stride=4), :].astype(F32)
-    wedges[...] = jnp.concatenate([rows] * 4, axis=0).T
+    tiles[0:128, :] = wedge_map[...].astype(F32)
+    rows = [tiles[pl.ds(high, 32, stride=4), :] for high in range(4)]
+    rows = jnp.concatenate(rows, axis=0).T
+    wedges[pl.ds(0, 128, stride=2), :] = rows
+    wedges[pl.ds(1, 128, stride=2), :] = rows
     for half in range(2):
         for a in range(32):
             lanes = slice((a % 2) * 128, (a % 2) * 128 + 128)
@@ -288,7 +294,7 @@
                     turned[pl.ds(side * 8 + pair * 2 + half, 128, stride=24), :] = value[
                         side * 128 : side * 128 + 128, half * 128 : half * 128 + 128
                     ]
-        ready[index] = turned[...].reshape(128, 24, 128)[:, :16].astype(BF16)
+        ready[index] = turned[0:3072, :].reshape(128, 24, 128)[:, :16].astype(BF16)
         send(index).start()
         return carry
 
@@ -322,7 +328,7 @@
         return pltpu.make_async_copy(phase.at[freq], shifts.at[freq], sems.at[freq])
 
     def fetch_lines(index):
-        rows = pl.ds(pl.multiple_of(index * 16, 16), 16)
+        rows = pl.ds(index * 16, 16)
         return pltpu.make_async_copy(lines.at[:, rows, :], held.at[index], sems.at[4 + index])
 
     order = [fetch_lines(0), fetch, fetch_lines(1), fetch_phase(0), fetch_inv]
@@ -330,8 +336,8 @@
         copy.start()
     term[...] = jnp.zeros_like(term)
 
-    def one_freq(freq, carry):
-        def forward(which, carry):
+    def one_freq(freq):
+        def forward(which):
             index = freq * 2 + which
             fetch_lines(index).wait()
             for low in range(8):
@@ -344,10 +350,8 @@
                     work[q * 8 + low, 0] = r
                     work[q * 8 + low, 1] = i
 
-            @pl.when(index == 0)
-            def _():
+            if index == 0:
                 fetch.wait()
-
             for part in range(4):
                 real, imag = [], []
                 for q in range(4 * part, 4 * part + 4):
@@ -360,9 +364,9 @@
                 both = [jnp.concatenate(real, axis=0), jnp.concatenate(imag, axis=0)]
                 block = slice(part * 256, part * 256 + 256)
                 spec[which, block, :] = dot2(jnp.concatenate(both, axis=1), matrix)
-            return carry
-
-        lax.fori_loop(0, 2, forward, 0, unroll=True)
+
+        for which in range(2):
+            forward(which)
         for part in range(4):
             block = slice(part * 256, part * 256 + 256)
             both = spec[0, block, :] * spec[1, block, :]
@@ -370,11 +374,10 @@
 
         fetch_phase(freq).wait()
 
-        @pl.when(freq == 0)
-        def _():
+        if freq == 0:
             fetch_inv.wait()
 
-        def inverse(ref, carry):
+        def inverse(ref):
             for part in range(4):
                 block = slice(part * 256, part * 256 + 256)
                 value = (spec[0, block, 0:128], spec[0, block, 128:256])
@@ -395,29 +398,35 @@
                         r, i = turn(value, low * q, 128, 1)
                         work[low * 16 + q, 0] = r
                         work[low * 16 + q, 1] = i
-            rows = pl.ds(pl.multiple_of(freq * 32 + ref * 16, 16), 16)
             for low in range(8):
                 values = [(work[low * 16 + q, 0], work[low * 16 + q, 1]) for q in range(16)]
                 for high, value in enumerate(dft(values, 1)):
                     value = jnp.concatenate(value, axis=0).astype(BF16)
-                    out[every_rank(8 * high + low), rows, :] = value
-            return carry
-
-        lax.fori_loop(0, 2, inverse, 0, unroll=True)
-        return carry
-
-    lax.fori_loop(0, 2, one_freq, 0)
+                    start = every_rank(8 * high + low) * MESSAGE + freq * 32 + ref * 16
+                    out[start : start + 16, :] = value
+
+        for ref in range(2):
+            inverse(ref)
+
+    for freq in range(2):
+        one_freq(freq)
     total = term[...].reshape(128, 8, 128).sum(axis=1)
     for q in range(16):
         sums[pl.ds(q, 8, stride=16), :] = total[8 * q : 8 * q + 8, :]
-    total = sums[...]
+    total = sums[0:128, :]
     total = total + pltpu.roll(total, 64, 1)
     total = total + pltpu.roll(total, 32, 1)
-    high = total.astype(BF16).astype(F32)
-    place = lax.broadcasted_iota(jnp.int32, (128, 128), 1) >> 5
-    value = jnp.where(place % 2 == 0, high, total - high).reshape(16, 8, 128).astype(BF16)
+    place = lax.broadcasted_iota(jnp.int32, (32, 128), 1) >> 5
+    value = total[0:32, :]
+    for u in range(1, 4):
+        value = jnp.where(place == u, total[32 * u : 32 * u + 32, :], value)
+    for v in range(2):
+        sums[pl.ds(v, 16, stride=2), :] = value[16 * v : 16 * v + 16, :]
+    value = sums[0:32, :].astype(BF16)
     for block in range(DEVICES):
-        out[every_rank(block), 64:72, :] = value[block % GROUP]
+        start = every_rank(block) * MESSAGE + 64
+        line = block % GROUP
+        out[start : start + 2, :] = value[2 * line : 2 * line + 2, :]
 
 
 def cross_inverse_kernel(
@@ -427,38 +436,35 @@
     fetch.start()
     fetch_share = pltpu.make_async_copy(shares, share, sems.at[1])
     fetch_share.start()
-    place = lax.broadcasted_iota(jnp.int32, (8, 128), 1) >> 5
-    odd = (place >> 1).astype(F32)
-
-    def gather(d, totals):
-        value = lines[d, 64:72, :].astype(F32)
-        where = wedges[pl.ds(d, 1), :] - odd
+    for d in range(DEVICES):
+        flat[2 * d : 2 * d + 2, :] = lines[d * MESSAGE + 64 : d * MESSAGE + 66, :].astype(F32)
+
+    def gather(step, totals):
+        rows = pl.ds(pl.multiple_of(step * 8, 8), 8)
+        value, where = flat[rows, :], wedges[rows, :]
         return tuple(
-            total + jnp.where(where == 2.0 * j, value, 0.0) for j, total in enumerate(totals)
+            total + jnp.where(where == float(w), value, 0.0) for w, total in enumerate(totals)
         )
 
     zero = jnp.zeros((8, 128), F32)
-    totals = lax.fori_loop(0, 128, gather, (zero,) * 4, unroll=16)
-    totals = [total + pltpu.roll(total, 96, 1) for total in totals]
+    totals = lax.fori_loop(0, 32, gather, (zero,) * 8, unroll=8)
+    totals = [t[0:2] + t[2:4] + (t[4:6] + t[6:8]) for t in totals]
     for half in range(2):
-        value = jnp.where(place % 2 == 0, totals[2 * half], pltpu.roll(totals[2 * half + 1], 32, 1))
+        value = jnp.concatenate(totals[4 * half : 4 * half + 4], axis=0)
         value = (value * (1.0 / (SIZE * SIZE * math.sqrt(SIZE)))).astype(BF16)
         for group in range(16):
             out[group, 128:136, half * 128 : half * 128 + 128] = value
 
     fetch.wait()
 
-    def one_freq(freq, carry):
+    def one_freq(freq):
         for ref in range(2):
-            if ref == 1:
-
-                @pl.when(freq == 0)
-                def _():
-                    fetch_share.wait()
-
-            rows = pl.ds(pl.multiple_of(freq * 32 + ref * 16, 16), 16)
+            if freq == 0 and ref == 1:
+                fetch_share.wait()
+
             for d in range(128):
-                flat[24 * d : 24 * d + 16, :] = lines[d, rows, :].astype(F32)
+                rows = pl.ds(d * MESSAGE + freq * 32 + ref * 16, 16)
+                flat[24 * d : 24 * d + 16, :] = lines[rows, :].astype(F32)
             for g in range(8):
                 pair = [flat[pl.ds(side * 8 + g, 128, stride=24), :] for side in range(2)]
                 value = jnp.concatenate([x.T for x in pair], axis=1).astype(BF16)
@@ -495,24 +501,30 @@
                 return carry
 
             lax.fori_loop(0, 2, rows16, 0, unroll=True)
-        return carry
-
-    lax.fori_loop(0, 2, one_freq, 0)
-
-
-def unpack_kernel(home, out, angles, turned, wide, sems):
+
+    for freq in range(2):
+        one_freq(freq)
+
+
+def unpack_kernel(home, out, angles, coded, turned, wide, sems):
     copies = []
     for part in range(4):
         block = home.at[:, pl.ds(part * 32, 32), :]
         copies.append(pltpu.make_async_copy(block, out.at[part % 2, part // 2], sems.at[part]))
     for copy in copies:
         copy.start()
-    value = home[:, 128:136, :].astype(F32)
+    place = lax.broadcasted_iota(jnp.int32, (32, 128), 1) >> 5
     for half in range(2):
-        flipped = value[:, :, half * 128 : half * 128 + 128].reshape(128, 128).T
-        for group, wedge in enumerate((0, 2, 1, 3)):
-            rows = pl.ds(half * 4 + wedge, 32, stride=8)
-            turned[rows, :] = flipped[group * 32 : group * 32 + 32]
+        rows = home[:, 128:136, half * 128 : half * 128 + 128].astype(F32)
+        coded[0:128, :] = rows.reshape(128, 128)
+        rows = [coded[pl.ds(r, 16, stride=8), :] for r in range(8)]
+        flipped = jnp.concatenate(rows, axis=0).T
+        for w in range(4):
+            value = pltpu.roll(flipped[0:32], (4 - w) * 32 % 128, 1)
+            for u in range(1, 4):
+                part = pltpu.roll(flipped[32 * u : 32 * u + 32], (4 + u - w) * 32 % 128, 1)
+                value = jnp.where(place == u, part, value)
+            turned[pl.ds(half * 4 + w, 32, stride=8), :] = value
     for k in range(32):
         wide[:, k * 128 : k * 128 + 128] = turned[k * 8 : k * 8 + 8, :]
     copies.append(pltpu.make_async_copy(wide, angles, sems.at[4]))
@@ -560,13 +572,14 @@
 def prepare(omega, slowness, wedge_map, packed):
     outs = [
         pltpu.HBM((2, 2, 2, 1024, 128), F32),
-        pltpu.VMEM((128, 128), F32),
+        pltpu.VMEM((264, 128), F32),
         pltpu.HBM((32, 32, 128), F32),
     ]
     scale = jnp.asarray(tables()["phase_scale"])
     args = (omega, slowness, scale, wedge_map, near(packed))
     specs = [SCALAR] * 2 + [LOCAL] * 3
-    return call(prepare_kernel, "prepare", outs, [LOCAL] * 3, specs, [], 16, args)
+    scratch = [pltpu.VMEM((136, 128), F32)]
+    return call(prepare_kernel, "prepare", outs, [LOCAL] * 3, specs, scratch, 16, args)
 
 
 def cross_forward(packed):
@@ -576,7 +589,7 @@
     scratch = [
         pltpu.VMEM((256, 768), BF16),
         pltpu.VMEM((8, 4, 2, 32, 128), F32),
-        pltpu.VMEM((3072, 128), F32),
+        pltpu.VMEM((3096, 128), F32),
         pltpu.VMEM((4, DEVICES, 16, 128), BF16),
         pltpu.SemaphoreType.DMA,
         pltpu.SemaphoreType.DMA((4,)),
@@ -591,7 +604,7 @@
     args = [far(lines), far(phase)]
     args += [near(jnp.asarray(t[n])) for n in ("inline_tw_fwd", "inline_tw_inv")]
     args += [jnp.asarray(t[n]) for n in ("inline_fwd", "inline_inv")]
-    outs = pltpu.VMEM((DEVICES, 72, 128), BF16)
+    outs = pltpu.VMEM((DEVICES * MESSAGE, 128), BF16)
     scratch = [
         pltpu.VMEM((4, DEVICES, 16, 128), BF16),
         pltpu.VMEM((256, 256), BF16),
@@ -600,7 +613,7 @@
         pltpu.VMEM((128, 2, 8, 128), F32),
         pltpu.VMEM((2, 1024, 256), F32),
         pltpu.VMEM((1024, 128), F32),
-        pltpu.VMEM((128, 128), F32),
+        pltpu.VMEM((144, 128), F32),
         pltpu.SemaphoreType.DMA((8,)),
     ]
     specs = [FAR, FAR, LOCAL, LOCAL, FAR, FAR]
@@ -614,7 +627,7 @@
     outs = pltpu.VMEM((GROUP, 136, 256), BF16)
     scratch = [
         pltpu.VMEM((512, 256), BF16),
-        pltpu.VMEM((3072, 128), F32),
+        pltpu.VMEM((3096, 128), F32),
         pltpu.VMEM((4, 8, 2, 32, 128), F32),
         pltpu.VMEM((32, 2, 32, 128), BF16),
         pltpu.VMEM((32, 32, 128), F32),
@@ -631,7 +644,8 @@
         pltpu.HBM((8, SIZE), F32),
     ]
     scratch = [
-        pltpu.VMEM((256, 128), F32),
+        pltpu.VMEM((136, 128), F32),
+        pltpu.VMEM((264, 128), F32),
         pltpu.VMEM((8, SIZE), F32),
         pltpu.SemaphoreType.DMA((5,)),
     ]
@@ -647,7 +661,8 @@
     packed = exchange(pack(receiver, source, weight), LINE)
     phase, wedges, share = prepare(omega, slowness, wedge_map, packed)
     lines = exchange(cross_forward(packed), EVERY)
-    partial = exchange(inline_step(lines, phase), EVERY)
+    partial = inline_step(lines, phase).reshape(DEVICES, MESSAGE // 2, 2, 128)
+    partial = exchange(partial, EVERY).reshape(DEVICES * MESSAGE, 128)
     home = exchange(cross_inverse(partial, wedges, share), LINE)
     mixed, angles = unpack(home)
     return (mixed.reshape(2, 2, 512, 256), angles)

time: 153 us -> 151 us (0.987)
  blocking collectives: 93.6 us -> 91.3 us
    all_to_all x3, blocking collectives: 93.6 us -> 91.3 us  [exchange(): return lax.all_to_all(value, axes, 0, 0, tiled=True)]
where the time goes in v6:
time: 151 us
  blocking collectives  91.3 us (60%)
  Pallas kernels  27.4 us (18%)
  waiting for transfers between devices  21.9 us (15%)
  starting transfers between devices  9.32 us (6%)
    all_to_all x3, blocking collectives, exchange(): return lax.all_to_all(value, axes, 0, 0, tiled=True)  91.3 us
    pallas_call x6, Pallas kernels, call(): pl.pallas_call(kernel, in_specs=in_specs, out_specs=out_specs, out_shape=...  27.4 us
    all_to_all x1, waiting for transfers between devices, exchange(): return lax.all_to_all(value, axes, 0, 0, tiled=True)  21.9 us
    all_to_all x1, starting transfers between devices, exchange(): return lax.all_to_all(value, axes, 0, 0, tiled=True)  9.32 us
  transfers between devices with their start and end apart: 1, of which 1 were waited for; matrix products, arithmetic and copies ran while one was open for 0% of the time, Pallas kernels for 5%

profile of v6, /device:TPU:1, one launch (start us, length us, event | category | flops | bytes accessed | tf_op | source)
XLA Modules:
  0.0 151.0 jit_solution(15955957642477706432)
XLA Ops:
  0.6 1.7 %pack_fields.1 = bf16[16,288,256]{2,1,0:T(8,128)(2,1)S(1)} custom-call(bf16[2,2,16,32,256]{4,3,2,1,0:T(8,128)(2,1)} %bitcast.8, bf16[2,2,16,32,256]{4,3,2,1,0:T(8,128)(2,1)} %bitcast.9, s32[16,2,16,256]{3,2,1,0:T(8,128)} %bitcast.10), custom_call_target="tpu_custom_call" | custom-call | tf_op jit(solution)/shard_map/pack_fields/pallas_call | solution.py:550
  2.4 0.0 copy-start
  2.4 0.0 copy-start.8
  2.4 36.2 %all_to_all.20.lines.packed = bf16[16,288,256]{2,1,0:T(8,128)(2,1)S(1)} all-to-all(bf16[16,288,256]{2,1,0:T(8,128)(2,1)S(1)} %pack_fields.1), channel_id=1, replica_groups=mesh['x_hi'=2,'z_hi'=2,'z_lo'=2,'x_lo'=2,'y_hi'=2,'y_lo'=2,'core'=2] {'c..., dimensions={0} | all-to-all | bytes 4718592 | tf_op jit(solution)/shard_map/all_to_all | solution.py:657
  38.6 0.0 copy-done
  38.6 0.0 copy-done.8
  38.6 4.6 %crossline_forward.1 = bf16[128,64,128]{2,1,0:T(8,128)(2,1)} custom-call(bf16[16,288,256]{2,1,0:T(8,128)(2,1)S(1)} %all_to_all.20.lines.packed, f32[2,32,128]{2,1,0:T(8,128)S(1)} %copy-done.8, bf16[256,768]{1,0:T(8,128)(2,1)S(1)} %copy-done), custom_call_target="tpu_custom_call" | custom-call | tf_op jit(solution)/shard_map/crossline_forward/pallas_call | solution.py:550
  43.2 0.0 copy-start.6
  43.2 0.0 copy-start.9
  43.3 0.0 copy-start.10
  43.3 0.0 copy-start.11
  43.3 9.3 %all-to-all-start.1 = ((bf16[128,64,128]{2,1,0:T(8,128)(2,1)}), bf16[128,64,128]{2,1,0:T(8,128)(2,1)}, u32[]{:S(2)}, u32[]{:S(2)}) async-start(bf16[128,64,128]{2,1,0:T(8,128)(2,1)} %crossline_forward.1), calls=%async_computation.1 | async-start | bytes 4194304 | tf_op jit(solution)/shard_map/all_to_all | solution.py:657
  52.6 0.0 copy-done.6
  52.6 0.0 copy-done.9
  52.6 0.0 copy-done.10
  52.6 0.0 copy-done.11
  52.6 0.0 copy-start.2
  52.7 0.0 copy-start.3
  52.7 0.0 copy-start.4
  52.7 0.0 copy-start.5
  52.7 7.7 %prepare.1 = (f32[2,2,2,1024,128]{4,3,2,1,0:T(8,128)}, f32[264,128]{1,0:T(8,128)S(1)}, f32[32,32,128]{2,1,0:T(8,128)}) custom-call(f32[2]{0:T(128)S(1)} %copy-done.9, f32[2]{0:T(128)S(1)} %copy-done.10, f32[1,128]{1,0:T(1,128)S(1)} %copy-done.11, s32[128,128]{1,0:T(8,128)S(1)} %copy-done.6, bf16[16,288,256]{2,1,0:T(8,128)(2,1)S(1)} %all_to_all.20.lines.packed), custom_call_target="tpu_custom_call" | custom-call | tf_op jit(solution)/shard_map/prepare/pallas_call | solution.py:550
  60.4 21.9 %all-to-all-done.1.lines = bf16[128,64,128]{2,1,0:T(8,128)(2,1)} async-done(((bf16[128,64,128]{2,1,0:T(8,128)(2,1)}), bf16[128,64,128]{2,1,0:T(8,128)(2,1)}, u32[]{:S(2)}, u32[]{:S(2)}) %all-to-all-start.1) | async-done | bytes 2097184 | tf_op jit(solution)/shard_map/all_to_all | solution.py:657
  82.4 0.0 copy-done.2
  82.4 0.0 copy-done.3
  82.4 0.0 copy-done.4
  82.4 0.0 copy-done.5
  82.4 8.5 %inline_step.1 = bf16[8448,128]{1,0:T(8,128)(2,1)S(1)} custom-call(bf16[128,64,128]{2,1,0:T(8,128)(2,1)} %all-to-all-done.1.lines, f32[2,2,2,1024,128]{4,3,2,1,0:T(8,128)} %get-tuple-element.7.phase, f32[2,128,128]{2,1,0:T(8,128)S(1)} %copy-done.5, f32[2,128,128]{2,1,0:T(8,128)S(1)} %copy-done.4, bf16[256,256]{1,0:T(8,128)(2,1)S(1)} %copy-done.3, ...), custom_call_target="tpu_custom_call" | custom-call | tf_op jit(solution)/shard_map/inline_step/pallas_call | solution.py:550
  90.9 0.0 copy-start.1
  90.9 0.0 copy-start.7
  90.9 35.6 %all_to_all.21 = bf16[128,33,2,128]{3,2,1,0:T(2,128)(2,1)S(1)} all-to-all(bf16[128,33,2,128]{3,2,1,0:T(2,128)(2,1)S(1)} %bitcast.7), channel_id=1, replica_groups=mesh['x_hi'=2,'z_hi'=2,'z_lo'=2,'x_lo'=2,'y_hi'=2,'y_lo'=2,'core'=2] {'z..., dimensions={0} | all-to-all | bytes 4325376 | tf_op jit(solution)/shard_map/all_to_all | solution.py:657
  126.5 0.0 copy-done.1
  126.5 0.0 copy-done.7
  126.5 3.8 %crossline_inverse.1 = bf16[16,136,256]{2,1,0:T(8,128)(2,1)S(1)} custom-call(bf16[8448,128]{1,0:T(8,128)(2,1)S(1)} %bitcast.6, f32[264,128]{1,0:T(8,128)S(1)} %get-tuple-element.8.wedges, f32[32,32,128]{2,1,0:T(8,128)} %get-tuple-element.9.shares, f32[2,32,128]{2,1,0:T(8,128)S(1)} %copy-done.7, bf16[512,256]{1,0:T(8,128)(2,1)S(1)} %copy-done.1), custom_call_target="tpu_custom_call" | custom-call | tf_op jit(solution)/shard_map/crossline_inverse/pallas_call | solution.py:550
  130.3 19.5 %all_to_all.22.home = bf16[16,136,256]{2,1,0:T(8,128)(2,1)S(1)} all-to-all(bf16[16,136,256]{2,1,0:T(8,128)(2,1)S(1)} %crossline_inverse.1), channel_id=1, replica_groups=mesh['x_hi'=2,'z_hi'=2,'z_lo'=2,'x_lo'=2,'y_hi'=2,'y_lo'=2,'core'=2] {'c..., dimensions={0} | all-to-all | bytes 2228224 | tf_op jit(solution)/shard_map/all_to_all | solution.py:657
  149.8 1.0 unpack_fields.1
Async XLA Ops:
  2.4 36.3 %copy-start = (bf16[256,768]{1,0:T(8,128)(2,1)S(1)}, bf16[256,768]{1,0:T(8,128)(2,1)}, u32[]{:S(2)}) copy-start(bf16[256,768]{1,0:T(8,128)(2,1)} %constant.20.clone.table) | copy-start | bytes 1179652
  2.4 36.3 %copy-start.8 = (f32[2,32,128]{2,1,0:T(8,128)S(1)}, f32[2,32,128]{2,1,0:T(8,128)}, u32[]{:S(2)}) copy-start(f32[2,32,128]{2,1,0:T(8,128)} %constant.19.clone.twist) | copy-start | bytes 98308
  43.2 9.4 %copy-start.6 = (s32[128,128]{1,0:T(8,128)S(1)}, s32[128,128]{1,0:T(8,128)}, u32[]{:S(2)}) copy-start(s32[128,128]{1,0:T(8,128)} %wedge_map.1) | copy-start | bytes 196612
  43.2 9.4 %copy-start.9 = (f32[2]{0:T(128)S(1)}, f32[2]{0:T(128)}, u32[]{:S(2)}) copy-start(f32[2]{0:T(128)} %omega.1) | copy-start | bytes 28
  43.3 9.4 %copy-start.10 = (f32[2]{0:T(128)S(1)}, f32[2]{0:T(128)}, u32[]{:S(2)}) copy-start(f32[2]{0:T(128)} %slowness.1) | copy-start | bytes 28
  43.3 9.4 %copy-start.11 = (f32[1,128]{1,0:T(1,128)S(1)}, f32[1,128]{1,0:T(1,128)}, u32[]{:S(2)}) copy-start(f32[1,128]{1,0:T(1,128)} %constant.18.clone.scale) | copy-start | bytes 1540
  43.3 39.1 %all-to-all-start.1 = ((bf16[128,64,128]{2,1,0:T(8,128)(2,1)}), bf16[128,64,128]{2,1,0:T(8,128)(2,1)}, u32[]{:S(2)}, u32[]{:S(2)}) async-start(bf16[128,64,128]{2,1,0:T(8,128)(2,1)} %crossline_forward.1), calls=%async_computation.1 | async-start | bytes 4194304 | tf_op jit(solution)/shard_map/all_to_all | solution.py:657
  52.6 29.7 %copy-start.2 = (bf16[256,256]{1,0:T(8,128)(2,1)S(1)}, bf16[256,256]{1,0:T(8,128)(2,1)}, u32[]{:S(2)}) copy-start(bf16[256,256]{1,0:T(8,128)(2,1)} %constant.24.clone.table_inv) | copy-start | bytes 393220
  52.7 29.7 %copy-start.3 = (bf16[256,256]{1,0:T(8,128)(2,1)S(1)}, bf16[256,256]{1,0:T(8,128)(2,1)}, u32[]{:S(2)}) copy-start(bf16[256,256]{1,0:T(8,128)(2,1)} %constant.23.clone.table) | copy-start | bytes 393220
  52.7 29.7 %copy-start.4 = (f32[2,128,128]{2,1,0:T(8,128)S(1)}, f32[2,128,128]{2,1,0:T(8,128)}, u32[]{:S(2)}) copy-start(f32[2,128,128]{2,1,0:T(8,128)} %constant.22.clone.twist_inv) | copy-start | bytes 393220
  52.7 29.7 %copy-start.5 = (f32[2,128,128]{2,1,0:T(8,128)S(1)}, f32[2,128,128]{2,1,0:T(8,128)}, u32[]{:S(2)}) copy-start(f32[2,128,128]{2,1,0:T(8,128)} %constant.21.clone.twist) | copy-start | bytes 393220
  90.9 35.6 %copy-start.1 = (bf16[512,256]{1,0:T(8,128)(2,1)S(1)}, bf16[512,256]{1,0:T(8,128)(2,1)}, u32[]{:S(2)}) copy-start(bf16[512,256]{1,0:T(8,128)(2,1)} %constant.26.clone.table) | copy-start | bytes 786436
  90.9 35.6 %copy-start.7 = (f32[2,32,128]{2,1,0:T(8,128)S(1)}, f32[2,32,128]{2,1,0:T(8,128)}, u32[]{:S(2)}) copy-start(f32[2,32,128]{2,1,0:T(8,128)} %constant.25.clone.twist) | copy-start | bytes 98308

commit v7 on v6

--- a/solution.py
+++ b/solution.py
@@ -73,11 +73,12 @@
 @functools.lru_cache(None)
 def tables():
     out = {}
-    high, low = two_parts(as_block(roots(128, 128, 128, -1)).T)
-    out["cross_fwd"] = np.concatenate([high, high, low], axis=1)
+    gain = gains(128)
+    high, _ = two_parts((np.tile(gain, 2)[:, None] * as_block(roots(128, 128, 128, -1))).T)
+    out["cross_fwd"] = high
     high, low = two_parts(as_block(roots(128, 128, 128, 1)) / SIZE)
     out["cross_inv"] = np.concatenate([high, low], axis=0)
-    out["cross_tw_fwd"] = pair_table(roots(32, 128, SIZE, -1))
+    out["cross_tw_fwd"] = pair_table(roots(32, 128, SIZE, -1) / gain)
     out["cross_tw_inv"] = pair_table(roots(32, 128, SIZE, 1))
     gain = np.tile(gains(32), 4)
     out["phase_scale"] = (1.0 / gain).astype(np.float32)[None, :]
@@ -287,8 +288,7 @@
                     imag.append(i)
             both = [jnp.concatenate(real, axis=0), jnp.concatenate(imag, axis=0)]
             high, low = split(jnp.concatenate(both, axis=1))
-            parts = jnp.concatenate([high, low, high], axis=1)
-            value = dot(matrix[...], parts, ((1,), (1,)))
+            value = dot(matrix[...], high, ((1,), (1,))) + dot(matrix[...], low, ((1,), (1,)))
             for side in range(2):
                 for half in range(2):
                     turned[pl.ds(side * 8 + pair * 2 + half, 128, stride=24), :] = value[
@@ -587,7 +587,7 @@
     args = [near(packed), near(jnp.asarray(t["cross_tw_fwd"])), jnp.asarray(t["cross_fwd"])]
     outs = pltpu.HBM((DEVICES, 64, 128), BF16)
     scratch = [
-        pltpu.VMEM((256, 768), BF16),
+        pltpu.VMEM((256, 256), BF16),
         pltpu.VMEM((8, 4, 2, 32, 128), F32),
         pltpu.VMEM((3096, 128), F32),
         pltpu.VMEM((4, DEVICES, 16, 128), BF16),

time: 151 us -> 151 us (level)
  no operation moved by 1% of the time
where the time goes in v7:
time: 151 us
  blocking collectives  91.3 us (60%)
  Pallas kernels  27 us (18%)
  waiting for transfers between devices  21.9 us (15%)
  starting transfers between devices  9.33 us (6%)
    all_to_all x3, blocking collectives, exchange(): return lax.all_to_all(value, axes, 0, 0, tiled=True)  91.3 us
    pallas_call x6, Pallas kernels, call(): pl.pallas_call(kernel, in_specs=in_specs, out_specs=out_specs, out_shape=...  27 us
    all_to_all x1, waiting for transfers between devices, exchange(): return lax.all_to_all(value, axes, 0, 0, tiled=True)  21.9 us
    all_to_all x1, starting transfers between devices, exchange(): return lax.all_to_all(value, axes, 0, 0, tiled=True)  9.33 us
  transfers between devices with their start and end apart: 1, of which 1 were waited for; matrix products, arithmetic and copies ran while one was open for 0% of the time, Pallas kernels for 5%

profile of v7, /device:TPU:1, one launch (start us, length us, event | category | flops | bytes accessed | tf_op | source)
XLA Modules:
  0.0 150.6 jit_solution(1240403861490631342)
XLA Ops:
  0.6 1.7 %pack_fields.1 = bf16[16,288,256]{2,1,0:T(8,128)(2,1)S(1)} custom-call(bf16[2,2,16,32,256]{4,3,2,1,0:T(8,128)(2,1)} %bitcast.8, bf16[2,2,16,32,256]{4,3,2,1,0:T(8,128)(2,1)} %bitcast.9, s32[16,2,16,256]{3,2,1,0:T(8,128)} %bitcast.10), custom_call_target="tpu_custom_call" | custom-call | tf_op jit(solution)/shard_map/pack_fields/pallas_call | solution.py:550
  2.4 0.0 copy-start.5
  2.4 0.0 copy-start.8
  2.4 36.2 %all_to_all.20.lines.packed = bf16[16,288,256]{2,1,0:T(8,128)(2,1)S(1)} all-to-all(bf16[16,288,256]{2,1,0:T(8,128)(2,1)S(1)} %pack_fields.1), channel_id=1, replica_groups=mesh['x_hi'=2,'z_hi'=2,'z_lo'=2,'x_lo'=2,'y_hi'=2,'y_lo'=2,'core'=2] {'c..., dimensions={0} | all-to-all | bytes 4718592 | tf_op jit(solution)/shard_map/all_to_all | solution.py:657
  38.6 0.0 copy-done.5
  38.6 0.0 copy-done.8
  38.6 4.2 %crossline_forward.1 = bf16[128,64,128]{2,1,0:T(8,128)(2,1)} custom-call(bf16[16,288,256]{2,1,0:T(8,128)(2,1)S(1)} %all_to_all.20.lines.packed, f32[2,32,128]{2,1,0:T(8,128)S(1)} %copy-done.8, bf16[256,256]{1,0:T(8,128)(2,1)S(1)} %copy-done.5), custom_call_target="tpu_custom_call" | custom-call | tf_op jit(solution)/shard_map/crossline_forward/pallas_call | solution.py:550
  42.8 0.0 copy-start.6
  42.8 0.0 copy-start.9
  42.9 0.0 copy-start.10
  42.9 0.0 copy-start.11
  42.9 9.3 %all-to-all-start.1 = ((bf16[128,64,128]{2,1,0:T(8,128)(2,1)}), bf16[128,64,128]{2,1,0:T(8,128)(2,1)}, u32[]{:S(2)}, u32[]{:S(2)}) async-start(bf16[128,64,128]{2,1,0:T(8,128)(2,1)} %crossline_forward.1), calls=%async_computation.1 | async-start | bytes 4194304 | tf_op jit(solution)/shard_map/all_to_all | solution.py:657
  52.2 0.0 copy-done.6
  52.2 0.0 copy-done.9
  52.2 0.0 copy-done.10
  52.2 0.0 copy-done.11
  52.3 0.0 copy-start.1
  52.3 0.0 copy-start.2
  52.3 0.0 copy-start.3
  52.3 0.0 copy-start.4
  52.3 7.7 %prepare.1 = (f32[2,2,2,1024,128]{4,3,2,1,0:T(8,128)}, f32[264,128]{1,0:T(8,128)S(1)}, f32[32,32,128]{2,1,0:T(8,128)}) custom-call(f32[2]{0:T(128)S(1)} %copy-done.9, f32[2]{0:T(128)S(1)} %copy-done.10, f32[1,128]{1,0:T(1,128)S(1)} %copy-done.11, s32[128,128]{1,0:T(8,128)S(1)} %copy-done.6, bf16[16,288,256]{2,1,0:T(8,128)(2,1)S(1)} %all_to_all.20.lines.packed), custom_call_target="tpu_custom_call" | custom-call | tf_op jit(solution)/shard_map/prepare/pallas_call | solution.py:550
  60.0 21.9 %all-to-all-done.1.lines = bf16[128,64,128]{2,1,0:T(8,128)(2,1)} async-done(((bf16[128,64,128]{2,1,0:T(8,128)(2,1)}), bf16[128,64,128]{2,1,0:T(8,128)(2,1)}, u32[]{:S(2)}, u32[]{:S(2)}) %all-to-all-start.1) | async-done | bytes 2097184 | tf_op jit(solution)/shard_map/all_to_all | solution.py:657
  82.0 0.0 copy-done.1
  82.0 0.0 copy-done.2
  82.0 0.0 copy-done.3
  82.0 0.0 copy-done.4
  82.0 8.5 %inline_step.1 = bf16[8448,128]{1,0:T(8,128)(2,1)S(1)} custom-call(bf16[128,64,128]{2,1,0:T(8,128)(2,1)} %all-to-all-done.1.lines, f32[2,2,2,1024,128]{4,3,2,1,0:T(8,128)} %get-tuple-element.7.phase, f32[2,128,128]{2,1,0:T(8,128)S(1)} %copy-done.4, f32[2,128,128]{2,1,0:T(8,128)S(1)} %copy-done.3, bf16[256,256]{1,0:T(8,128)(2,1)S(1)} %copy-done.2, ...), custom_call_target="tpu_custom_call" | custom-call | tf_op jit(solution)/shard_map/inline_step/pallas_call | solution.py:550
  90.5 0.0 copy-start
  90.5 0.0 copy-start.7
  90.5 35.6 %all_to_all.21 = bf16[128,33,2,128]{3,2,1,0:T(2,128)(2,1)S(1)} all-to-all(bf16[128,33,2,128]{3,2,1,0:T(2,128)(2,1)S(1)} %bitcast.7), channel_id=1, replica_groups=mesh['x_hi'=2,'z_hi'=2,'z_lo'=2,'x_lo'=2,'y_hi'=2,'y_lo'=2,'core'=2] {'z..., dimensions={0} | all-to-all | bytes 4325376 | tf_op jit(solution)/shard_map/all_to_all | solution.py:657
  126.1 0.0 copy-done
  126.1 0.0 copy-done.7
  126.1 3.8 %crossline_inverse.1 = bf16[16,136,256]{2,1,0:T(8,128)(2,1)S(1)} custom-call(bf16[8448,128]{1,0:T(8,128)(2,1)S(1)} %bitcast.6, f32[264,128]{1,0:T(8,128)S(1)} %get-tuple-element.8.wedges, f32[32,32,128]{2,1,0:T(8,128)} %get-tuple-element.9.shares, f32[2,32,128]{2,1,0:T(8,128)S(1)} %copy-done.7, bf16[512,256]{1,0:T(8,128)(2,1)S(1)} %copy-done), custom_call_target="tpu_custom_call" | custom-call | tf_op jit(solution)/shard_map/crossline_inverse/pallas_call | solution.py:550
  130.0 19.5 %all_to_all.22.home = bf16[16,136,256]{2,1,0:T(8,128)(2,1)S(1)} all-to-all(bf16[16,136,256]{2,1,0:T(8,128)(2,1)S(1)} %crossline_inverse.1), channel_id=1, replica_groups=mesh['x_hi'=2,'z_hi'=2,'z_lo'=2,'x_lo'=2,'y_hi'=2,'y_lo'=2,'core'=2] {'c..., dimensions={0} | all-to-all | bytes 2228224 | tf_op jit(solution)/shard_map/all_to_all | solution.py:657
  149.4 1.0 unpack_fields.1
Async XLA Ops:
  2.4 36.3 %copy-start.5 = (bf16[256,256]{1,0:T(8,128)(2,1)S(1)}, bf16[256,256]{1,0:T(8,128)(2,1)}, u32[]{:S(2)}) copy-start(bf16[256,256]{1,0:T(8,128)(2,1)} %constant.20.clone.table) | copy-start | bytes 393220
  2.4 36.3 %copy-start.8 = (f32[2,32,128]{2,1,0:T(8,128)S(1)}, f32[2,32,128]{2,1,0:T(8,128)}, u32[]{:S(2)}) copy-start(f32[2,32,128]{2,1,0:T(8,128)} %constant.19.clone.twist) | copy-start | bytes 98308
  42.8 9.4 %copy-start.6 = (s32[128,128]{1,0:T(8,128)S(1)}, s32[128,128]{1,0:T(8,128)}, u32[]{:S(2)}) copy-start(s32[128,128]{1,0:T(8,128)} %wedge_map.1) | copy-start | bytes 196612
  42.8 9.4 %copy-start.9 = (f32[2]{0:T(128)S(1)}, f32[2]{0:T(128)}, u32[]{:S(2)}) copy-start(f32[2]{0:T(128)} %omega.1) | copy-start | bytes 28
  42.9 9.4 %copy-start.10 = (f32[2]{0:T(128)S(1)}, f32[2]{0:T(128)}, u32[]{:S(2)}) copy-start(f32[2]{0:T(128)} %slowness.1) | copy-start | bytes 28
  42.9 9.4 %copy-start.11 = (f32[1,128]{1,0:T(1,128)S(1)}, f32[1,128]{1,0:T(1,128)}, u32[]{:S(2)}) copy-start(f32[1,128]{1,0:T(1,128)} %constant.18.clone.scale) | copy-start | bytes 1540
  42.9 39.1 %all-to-all-start.1 = ((bf16[128,64,128]{2,1,0:T(8,128)(2,1)}), bf16[128,64,128]{2,1,0:T(8,128)(2,1)}, u32[]{:S(2)}, u32[]{:S(2)}) async-start(bf16[128,64,128]{2,1,0:T(8,128)(2,1)} %crossline_forward.1), calls=%async_computation.1 | async-start | bytes 4194304 | tf_op jit(solution)/shard_map/all_to_all | solution.py:657
  52.3 29.7 %copy-start.1 = (bf16[256,256]{1,0:T(8,128)(2,1)S(1)}, bf16[256,256]{1,0:T(8,128)(2,1)}, u32[]{:S(2)}) copy-start(bf16[256,256]{1,0:T(8,128)(2,1)} %constant.24.clone.table_inv) | copy-start | bytes 393220
  52.3 29.7 %copy-start.2 = (bf16[256,256]{1,0:T(8,128)(2,1)S(1)}, bf16[256,256]{1,0:T(8,128)(2,1)}, u32[]{:S(2)}) copy-start(bf16[256,256]{1,0:T(8,128)(2,1)} %constant.23.clone.table) | copy-start | bytes 393220
  52.3 29.7 %copy-start.3 = (f32[2,128,128]{2,1,0:T(8,128)S(1)}, f32[2,128,128]{2,1,0:T(8,128)}, u32[]{:S(2)}) copy-start(f32[2,128,128]{2,1,0:T(8,128)} %constant.22.clone.twist_inv) | copy-start | bytes 393220
  52.3 29.7 %copy-start.4 = (f32[2,128,128]{2,1,0:T(8,128)S(1)}, f32[2,128,128]{2,1,0:T(8,128)}, u32[]{:S(2)}) copy-start(f32[2,128,128]{2,1,0:T(8,128)} %constant.21.clone.twist) | copy-start | bytes 393220
  90.5 35.6 %copy-start = (bf16[512,256]{1,0:T(8,128)(2,1)S(1)}, bf16[512,256]{1,0:T(8,128)(2,1)}, u32[]{:S(2)}) copy-start(bf16[512,256]{1,0:T(8,128)(2,1)} %constant.26.clone.table) | copy-start | bytes 786436
  90.5 35.6 %copy-start.7 = (f32[2,32,128]{2,1,0:T(8,128)S(1)}, f32[2,32,128]{2,1,0:T(8,128)}, u32[]{:S(2)}) copy-start(f32[2,32,128]{2,1,0:T(8,128)} %constant.25.clone.twist) | copy-start | bytes 98308

commit v8 on v6

--- a/solution.py
+++ b/solution.py
@@ -249,9 +249,10 @@
     fetch = pltpu.make_async_copy(table, matrix, sem)
     fetch.start()
 
-    def send(index):
+    def send(index, half):
         rows = pl.ds(pl.multiple_of(index * 16, 16), 16)
-        return pltpu.make_async_copy(ready.at[index], out.at[:, rows, :], sems.at[index])
+        part = pl.ds(64 * half, 64)
+        return pltpu.make_async_copy(ready.at[index, part], out.at[part, rows, :], sems.at[index, half])
 
     def field(index, carry):
         start = index // 2 * 144 + index % 2 * 64
@@ -294,13 +295,16 @@
                     turned[pl.ds(side * 8 + pair * 2 + half, 128, stride=24), :] = value[
                         side * 128 : side * 128 + 128, half * 128 : half * 128 + 128
                     ]
-        ready[index] = turned[0:3072, :].reshape(128, 24, 128)[:, :16].astype(BF16)
-        send(index).start()
+        for half in range(2):
+            block = turned[1536 * half : 1536 * half + 1536, :].reshape(64, 24, 128)[:, :16]
+            ready[index, 64 * half : 64 * half + 64] = block.astype(BF16)
+            send(index, half).start()
         return carry
 
     lax.fori_loop(0, 4, field, 0, unroll=True)
     for index in range(4):
-        send(index).wait()
+        send(index, 0).wait()
+        send(index, 1).wait()
 
 
 def inline_kernel(
@@ -592,7 +596,7 @@
         pltpu.VMEM((3096, 128), F32),
         pltpu.VMEM((4, DEVICES, 16, 128), BF16),
         pltpu.SemaphoreType.DMA,
-        pltpu.SemaphoreType.DMA((4,)),
+        pltpu.SemaphoreType.DMA((4, 2)),
     ]
     return call(
         cross_forward_kernel, "crossline_forward", outs, FAR, [LOCAL] * 2 + [FAR], scratch, 16, args

time: 151 us -> 151 us (level)
  no operation moved by 1% of the time
where the time goes in v8:
time: 151 us
  blocking collectives  91.3 us (60%)
  Pallas kernels  27.4 us (18%)
  waiting for transfers between devices  21.9 us (15%)
  starting transfers between devices  9.32 us (6%)
    all_to_all x3, blocking collectives, exchange(): return lax.all_to_all(value, axes, 0, 0, tiled=True)  91.3 us
    pallas_call x6, Pallas kernels, call(): pl.pallas_call(kernel, in_specs=in_specs, out_specs=out_specs, out_shape=...  27.4 us
    all_to_all x1, waiting for transfers between devices, exchange(): return lax.all_to_all(value, axes, 0, 0, tiled=True)  21.9 us
    all_to_all x1, starting transfers between devices, exchange(): return lax.all_to_all(value, axes, 0, 0, tiled=True)  9.32 us
  transfers between devices with their start and end apart: 1, of which 1 were waited for; matrix products, arithmetic and copies ran while one was open for 0% of the time, Pallas kernels for 5%

profile of v8, /device:TPU:1, one launch (start us, length us, event | category | flops | bytes accessed | tf_op | source)
XLA Modules:
  0.0 151.0 jit_solution(10785740044141507374)
XLA Ops:
  0.6 1.7 %pack_fields.1 = bf16[16,288,256]{2,1,0:T(8,128)(2,1)S(1)} custom-call(bf16[2,2,16,32,256]{4,3,2,1,0:T(8,128)(2,1)} %bitcast.8, bf16[2,2,16,32,256]{4,3,2,1,0:T(8,128)(2,1)} %bitcast.9, s32[16,2,16,256]{3,2,1,0:T(8,128)} %bitcast.10), custom_call_target="tpu_custom_call" | custom-call | tf_op jit(solution)/shard_map/pack_fields/pallas_call | solution.py:554
  2.4 0.0 copy-start
  2.4 0.0 copy-start.8
  2.4 36.2 %all_to_all.20.lines.packed = bf16[16,288,256]{2,1,0:T(8,128)(2,1)S(1)} all-to-all(bf16[16,288,256]{2,1,0:T(8,128)(2,1)S(1)} %pack_fields.1), channel_id=1, replica_groups=mesh['x_hi'=2,'z_hi'=2,'z_lo'=2,'x_lo'=2,'y_hi'=2,'y_lo'=2,'core'=2] {'c..., dimensions={0} | all-to-all | bytes 4718592 | tf_op jit(solution)/shard_map/all_to_all | solution.py:661
  38.6 0.0 copy-done
  38.6 0.0 copy-done.8
  38.6 4.6 %crossline_forward.1 = bf16[128,64,128]{2,1,0:T(8,128)(2,1)} custom-call(bf16[16,288,256]{2,1,0:T(8,128)(2,1)S(1)} %all_to_all.20.lines.packed, f32[2,32,128]{2,1,0:T(8,128)S(1)} %copy-done.8, bf16[256,768]{1,0:T(8,128)(2,1)S(1)} %copy-done), custom_call_target="tpu_custom_call" | custom-call | tf_op jit(solution)/shard_map/crossline_forward/pallas_call | solution.py:554
  43.2 0.0 copy-start.6
  43.2 0.0 copy-start.9
  43.2 0.0 copy-start.10
  43.3 0.0 copy-start.11
  43.3 9.3 %all-to-all-start.1 = ((bf16[128,64,128]{2,1,0:T(8,128)(2,1)}), bf16[128,64,128]{2,1,0:T(8,128)(2,1)}, u32[]{:S(2)}, u32[]{:S(2)}) async-start(bf16[128,64,128]{2,1,0:T(8,128)(2,1)} %crossline_forward.1), calls=%async_computation.1 | async-start | bytes 4194304 | tf_op jit(solution)/shard_map/all_to_all | solution.py:661
  52.6 0.0 copy-done.6
  52.6 0.0 copy-done.9
  52.6 0.0 copy-done.10
  52.6 0.0 copy-done.11
  52.6 0.0 copy-start.2
  52.6 0.0 copy-start.3
  52.7 0.0 copy-start.4
  52.7 0.0 copy-start.5
  52.7 7.7 %prepare.1 = (f32[2,2,2,1024,128]{4,3,2,1,0:T(8,128)}, f32[264,128]{1,0:T(8,128)S(1)}, f32[32,32,128]{2,1,0:T(8,128)}) custom-call(f32[2]{0:T(128)S(1)} %copy-done.9, f32[2]{0:T(128)S(1)} %copy-done.10, f32[1,128]{1,0:T(1,128)S(1)} %copy-done.11, s32[128,128]{1,0:T(8,128)S(1)} %copy-done.6, bf16[16,288,256]{2,1,0:T(8,128)(2,1)S(1)} %all_to_all.20.lines.packed), custom_call_target="tpu_custom_call" | custom-call | tf_op jit(solution)/shard_map/prepare/pallas_call | solution.py:554
  60.4 21.9 %all-to-all-done.1.lines = bf16[128,64,128]{2,1,0:T(8,128)(2,1)} async-done(((bf16[128,64,128]{2,1,0:T(8,128)(2,1)}), bf16[128,64,128]{2,1,0:T(8,128)(2,1)}, u32[]{:S(2)}, u32[]{:S(2)}) %all-to-all-start.1) | async-done | bytes 2097184 | tf_op jit(solution)/shard_map/all_to_all | solution.py:661
  82.3 0.0 copy-done.2
  82.3 0.0 copy-done.3
  82.4 0.0 copy-done.4
  82.4 0.0 copy-done.5
  82.4 8.5 %inline_step.1 = bf16[8448,128]{1,0:T(8,128)(2,1)S(1)} custom-call(bf16[128,64,128]{2,1,0:T(8,128)(2,1)} %all-to-all-done.1.lines, f32[2,2,2,1024,128]{4,3,2,1,0:T(8,128)} %get-tuple-element.7.phase, f32[2,128,128]{2,1,0:T(8,128)S(1)} %copy-done.5, f32[2,128,128]{2,1,0:T(8,128)S(1)} %copy-done.4, bf16[256,256]{1,0:T(8,128)(2,1)S(1)} %copy-done.3, ...), custom_call_target="tpu_custom_call" | custom-call | tf_op jit(solution)/shard_map/inline_step/pallas_call | solution.py:554
  90.9 0.0 copy-start.1
  90.9 0.0 copy-start.7
  90.9 35.6 %all_to_all.21 = bf16[128,33,2,128]{3,2,1,0:T(2,128)(2,1)S(1)} all-to-all(bf16[128,33,2,128]{3,2,1,0:T(2,128)(2,1)S(1)} %bitcast.7), channel_id=1, replica_groups=mesh['x_hi'=2,'z_hi'=2,'z_lo'=2,'x_lo'=2,'y_hi'=2,'y_lo'=2,'core'=2] {'z..., dimensions={0} | all-to-all | bytes 4325376 | tf_op jit(solution)/shard_map/all_to_all | solution.py:661
  126.5 0.0 copy-done.1
  126.5 0.0 copy-done.7
  126.5 3.8 %crossline_inverse.1 = bf16[16,136,256]{2,1,0:T(8,128)(2,1)S(1)} custom-call(bf16[8448,128]{1,0:T(8,128)(2,1)S(1)} %bitcast.6, f32[264,128]{1,0:T(8,128)S(1)} %get-tuple-element.8.wedges, f32[32,32,128]{2,1,0:T(8,128)} %get-tuple-element.9.shares, f32[2,32,128]{2,1,0:T(8,128)S(1)} %copy-done.7, bf16[512,256]{1,0:T(8,128)(2,1)S(1)} %copy-done.1), custom_call_target="tpu_custom_call" | custom-call | tf_op jit(solution)/shard_map/crossline_inverse/pallas_call | solution.py:554
  130.3 19.5 %all_to_all.22.home = bf16[16,136,256]{2,1,0:T(8,128)(2,1)S(1)} all-to-all(bf16[16,136,256]{2,1,0:T(8,128)(2,1)S(1)} %crossline_inverse.1), channel_id=1, replica_groups=mesh['x_hi'=2,'z_hi'=2,'z_lo'=2,'x_lo'=2,'y_hi'=2,'y_lo'=2,'core'=2] {'c..., dimensions={0} | all-to-all | bytes 2228224 | tf_op jit(solution)/shard_map/all_to_all | solution.py:661
  149.8 1.0 unpack_fields.1
Async XLA Ops:
  2.4 36.3 %copy-start = (bf16[256,768]{1,0:T(8,128)(2,1)S(1)}, bf16[256,768]{1,0:T(8,128)(2,1)}, u32[]{:S(2)}) copy-start(bf16[256,768]{1,0:T(8,128)(2,1)} %constant.20.clone.table) | copy-start | bytes 1179652
  2.4 36.3 %copy-start.8 = (f32[2,32,128]{2,1,0:T(8,128)S(1)}, f32[2,32,128]{2,1,0:T(8,128)}, u32[]{:S(2)}) copy-start(f32[2,32,128]{2,1,0:T(8,128)} %constant.19.clone.twist) | copy-start | bytes 98308
  43.2 9.4 %copy-start.6 = (s32[128,128]{1,0:T(8,128)S(1)}, s32[128,128]{1,0:T(8,128)}, u32[]{:S(2)}) copy-start(s32[128,128]{1,0:T(8,128)} %wedge_map.1) | copy-start | bytes 196612
  43.2 9.4 %copy-start.9 = (f32[2]{0:T(128)S(1)}, f32[2]{0:T(128)}, u32[]{:S(2)}) copy-start(f32[2]{0:T(128)} %omega.1) | copy-start | bytes 28
  43.2 9.4 %copy-start.10 = (f32[2]{0:T(128)S(1)}, f32[2]{0:T(128)}, u32[]{:S(2)}) copy-start(f32[2]{0:T(128)} %slowness.1) | copy-start | bytes 28
  43.3 9.4 %copy-start.11 = (f32[1,128]{1,0:T(1,128)S(1)}, f32[1,128]{1,0:T(1,128)}, u32[]{:S(2)}) copy-start(f32[1,128]{1,0:T(1,128)} %constant.18.clone.scale) | copy-start | bytes 1540
  43.3 39.1 %all-to-all-start.1 = ((bf16[128,64,128]{2,1,0:T(8,128)(2,1)}), bf16[128,64,128]{2,1,0:T(8,128)(2,1)}, u32[]{:S(2)}, u32[]{:S(2)}) async-start(bf16[128,64,128]{2,1,0:T(8,128)(2,1)} %crossline_forward.1), calls=%async_computation.1 | async-start | bytes 4194304 | tf_op jit(solution)/shard_map/all_to_all | solution.py:661
  52.6 29.7 %copy-start.2 = (bf16[256,256]{1,0:T(8,128)(2,1)S(1)}, bf16[256,256]{1,0:T(8,128)(2,1)}, u32[]{:S(2)}) copy-start(bf16[256,256]{1,0:T(8,128)(2,1)} %constant.24.clone.table_inv) | copy-start | bytes 393220
  52.6 29.7 %copy-start.3 = (bf16[256,256]{1,0:T(8,128)(2,1)S(1)}, bf16[256,256]{1,0:T(8,128)(2,1)}, u32[]{:S(2)}) copy-start(bf16[256,256]{1,0:T(8,128)(2,1)} %constant.23.clone.table) | copy-start | bytes 393220
  52.7 29.7 %copy-start.4 = (f32[2,128,128]{2,1,0:T(8,128)S(1)}, f32[2,128,128]{2,1,0:T(8,128)}, u32[]{:S(2)}) copy-start(f32[2,128,128]{2,1,0:T(8,128)} %constant.22.clone.twist_inv) | copy-start | bytes 393220
  52.7 29.7 %copy-start.5 = (f32[2,128,128]{2,1,0:T(8,128)S(1)}, f32[2,128,128]{2,1,0:T(8,128)}, u32[]{:S(2)}) copy-start(f32[2,128,128]{2,1,0:T(8,128)} %constant.21.clone.twist) | copy-start | bytes 393220
  90.9 35.6 %copy-start.1 = (bf16[512,256]{1,0:T(8,128)(2,1)S(1)}, bf16[512,256]{1,0:T(8,128)(2,1)}, u32[]{:S(2)}) copy-start(bf16[512,256]{1,0:T(8,128)(2,1)} %constant.26.clone.table) | copy-start | bytes 786436
  90.9 35.6 %copy-start.7 = (f32[2,32,128]{2,1,0:T(8,128)S(1)}, f32[2,32,128]{2,1,0:T(8,128)}, u32[]{:S(2)}) copy-start(f32[2,32,128]{2,1,0:T(8,128)} %constant.25.clone.twist) | copy-start | bytes 98308
